TPU v7x, 32 devices: a whole 2x2x4 slice. The times are simulated.
32 devices in a mesh: ctx: 4 (over y, x), exp: 8 (over z, core).
Axes of the slice: x: 2, y: 2, z: 4, core: 2. Of those that a mesh axis runs over, the one named last changes fastest.
Arguments:
- tokens: bfloat16 [8, 1024, 2048], P('exp', 'ctx'), may hold values from -6 to 6
- cotangent: bfloat16 [8, 1024, 2048], P('exp', 'ctx'), may hold values from -6 to 6
- lengths: int32 [8], P('exp'), may hold values from 897 to 1024
- span_order: int32 [8], replicated, may hold values from 0 to 7, each once
- routes: int32 [8, 1024, 8], P('exp', 'ctx'), may hold values from 0 to 15, all different within a row; in each aligned block of 256 rows (0 to 255, 256 to 511, ..., all dimensions but the last counted through in order) at most 192 rows name the same one
- w_query: bfloat16 [2048, 2048], P('exp'), may hold values from -0.125 to 0.125
- w_key: bfloat16 [2048, 2048], P('exp'), may hold values from -0.125 to 0.125
- w_value: bfloat16 [2048, 2048], P('exp'), may hold values from -0.125 to 0.125
- w_output: bfloat16 [2048, 2048], P('exp'), may hold values from -1.5 to 1.5
- w_router: bfloat16 [2048, 16], P('exp'), may hold values from -0.0625 to 0.0625
- gain_attn: bfloat16 [2048], P('exp'), may hold values from 0.099609375 to 1.8984375
- gain_query: bfloat16 [2048], P('exp'), may hold values from 0.099609375 to 1.8984375
- gain_key: bfloat16 [2048], P('exp'), may hold values from 0.099609375 to 1.8984375
- gain_mlp: bfloat16 [2048], P('exp'), may hold values from 0.099609375 to 1.8984375
- w_gate: bfloat16 [16, 2048, 1024], P('exp'), may hold values from -0.125 to 0.125
- w_up: bfloat16 [16, 2048, 1024], P('exp'), may hold values from -0.125 to 0.125
- w_down: bfloat16 [16, 1024, 2048], P('exp'), may hold values from -3 to 3
Outputs:
- mixed: bfloat16 [8, 1024, 2048], P('exp', 'ctx')
- d_tokens: bfloat16 [8, 1024, 2048], P('exp', 'ctx')
- g_w_query: float32 [2048, 2048], P('exp')
- g_w_key: float32 [2048, 2048], P('exp')
- g_w_value: float32 [2048, 2048], P('exp')
- g_w_output: float32 [2048, 2048], P('exp')
- g_w_router: float32 [2048, 16], P('exp')
- g_gain_attn: float32 [2048], P('exp')
- g_gain_query: float32 [2048], P('exp')
- g_gain_key: float32 [2048], P('exp')
- g_gain_mlp: float32 [2048], P('exp')
- g_w_gate: float32 [16, 2048, 1024], P('exp', 'ctx')
- g_w_up: float32 [16, 2048, 1024], P('exp', 'ctx')
- g_w_down: float32 [16, 1024, 2048], P('exp', 'ctx')
Inputs may be any that keep to these rules, and one draw needn't show every extreme that they name: `routes`: each row names 8 different experts; in the rows of one device no expert is named by more than 192 rows, a bound that some block reaches. `span_order`: each span number appears once. `lengths`: the slots whose position is at or beyond a sequence's length are padding.
All inputs are finite; a program needn't handle non-finite values.
Results may differ from a plain program's by a relative error of at most 0.025.
Values may be sent and summed in bfloat16 or wider, within the bound.
A program may use at most 448 MiB of HBM per device.

v0:
```python
import math

import jax
import jax.numpy as jnp
from jax import lax
from jax.sharding import PartitionSpec as P

HEADS = 16
HEAD_DIM = 128


EPSILON = 1e-05
ROPE_BASE = 10000.0
MASKED_SCORE = -1e30
FULL_PRECISION = lax.Precision.HIGHEST
CONTRACT_OVER_ROWS = (((0,), (0,)), ((), ()))
CONTRACT_LAST = (((1,), (1,)), ((), ()))


def rms_forward(value_rows, gain_vec):
    inv_scale = lax.rsqrt(jnp.mean(value_rows * value_rows, axis=-1, keepdims=True) + EPSILON)
    return (value_rows * inv_scale * gain_vec, inv_scale)


def rms_backward(value_rows, inv_scale, gain_vec, grad_in):
    weighted = grad_in * gain_vec
    inner_mean = jnp.mean(weighted * value_rows, axis=-1, keepdims=True)
    d_values = inv_scale * weighted - value_rows * (inv_scale * inv_scale * inv_scale) * inner_mean
    return (d_values, jnp.sum(grad_in * value_rows * inv_scale, axis=0))


def rope_tables(positions, head_features):
    half_dim = head_features // 2
    frequency = jnp.exp(
        jnp.arange(half_dim, dtype=jnp.float32) * (-2.0 * math.log(ROPE_BASE) / head_features)
    )
    angle = positions.astype(jnp.float32)[:, None] * frequency[None, :]
    return (jnp.cos(angle)[:, None, :], jnp.sin(angle)[:, None, :])


def rotate(value_rows, cosine_table, sine_table):
    half_dim = value_rows.shape[-1] // 2
    first_half = value_rows[..., :half_dim]
    second_half = value_rows[..., half_dim:]
    return jnp.concatenate(
        [
            first_half * cosine_table - second_half * sine_table,
            second_half * cosine_table + first_half * sine_table,
        ],
        axis=-1,
    )


def positions_of(span_order, storage, span_length):
    return jnp.take(span_order, storage // span_length) * span_length + storage % span_length


def over_rows(left_side, right_side):
    return lax.dot_general(
        left_side,
        right_side,
        CONTRACT_OVER_ROWS,
        precision=FULL_PRECISION,
        preferred_element_type=jnp.float32,
    )


def against(left_side, right_side):
    return lax.dot_general(
        left_side,
        right_side,
        CONTRACT_LAST,
        precision=FULL_PRECISION,
        preferred_element_type=jnp.float32,
    )


def local(
    tokens,
    cotangent,
    lengths,
    span_order,
    routes,
    w_query,
    w_key,
    w_value,
    w_output,
    w_router,
    gain_attn,
    gain_query,
    gain_key,
    gain_mlp,
    w_gate,
    w_up,
    w_down,
):
    gathered = (
        lax.all_gather(w_query, "exp", axis=0, tiled=True),
        lax.all_gather(w_key, "exp", axis=0, tiled=True),
        lax.all_gather(w_value, "exp", axis=0, tiled=True),
        lax.all_gather(w_output, "exp", axis=0, tiled=True),
        lax.all_gather(w_router, "exp", axis=0, tiled=True),
        lax.all_gather(gain_attn, "exp", axis=0, tiled=True),
        lax.all_gather(gain_query, "exp", axis=0, tiled=True),
        lax.all_gather(gain_key, "exp", axis=0, tiled=True),
        lax.all_gather(gain_mlp, "exp", axis=0, tiled=True),
    )
    query_w, key_w, value_w, output_w, router_w = (
        gathered[0],
        gathered[1],
        gathered[2],
        gathered[3],
        gathered[4],
    )
    attn_gain = gathered[5].astype(jnp.float32)
    query_gain = gathered[6].astype(jnp.float32)
    key_gain = gathered[7].astype(jnp.float32)
    mlp_gain = gathered[8].astype(jnp.float32)
    rows_here = tokens.shape[1]
    model_width = tokens.shape[2]
    span_length = rows_here // 2
    ctx_count = lax.axis_size("ctx")
    seq_length = lengths[0]
    positions = positions_of(
        span_order,
        lax.axis_index("ctx") * rows_here + jnp.arange(rows_here, dtype=jnp.int32),
        span_length,
    )
    key_positions = positions_of(
        span_order, jnp.arange(rows_here * ctx_count, dtype=jnp.int32), span_length
    )
    allowed = (key_positions[None, :] <= positions[:, None]) & (key_positions[None, :] < seq_length)
    cosine_table, sine_table = rope_tables(positions, HEAD_DIM)
    head_shape = (rows_here, HEADS, HEAD_DIM)
    factor = HEAD_DIM ** (-0.5)
    block_input = tokens[0].astype(jnp.float32)
    normed_in, in_scale = rms_forward(block_input, attn_gain)
    normed_low = normed_in.astype(jnp.bfloat16)
    query_proj = jnp.dot(normed_low, query_w, preferred_element_type=jnp.float32)
    key_proj = jnp.dot(normed_low, key_w, preferred_element_type=jnp.float32)
    value_proj = jnp.dot(normed_low, value_w, preferred_element_type=jnp.float32)
    query_normed, query_scale = rms_forward(query_proj, query_gain)
    key_normed, key_scale = rms_forward(key_proj, key_gain)
    query_rot = rotate(query_normed.reshape(head_shape), cosine_table, sine_table).astype(
        jnp.bfloat16
    )
    key_rot = rotate(key_normed.reshape(head_shape), cosine_table, sine_table).astype(jnp.bfloat16)
    value_low = value_proj.astype(jnp.bfloat16).reshape(head_shape)
    keys_all, values_all = (
        lax.all_gather(key_rot, "ctx", axis=0, tiled=True),
        lax.all_gather(value_low, "ctx", axis=0, tiled=True),
    )

    def scores_of(query_in):
        raw_scores = (
            jnp.einsum("thd,shd->hts", query_in, keys_all, preferred_element_type=jnp.float32)
            * factor
        )
        return jnp.where(allowed[None], raw_scores, MASKED_SCORE)

    scores = scores_of(query_rot)
    row_max = jnp.max(scores, axis=-1, keepdims=True)
    expo_scores = jnp.exp(scores - row_max)
    row_total = jnp.sum(expo_scores, axis=-1, keepdims=True)
    log_total = row_max + jnp.log(row_total)
    probs_low = (expo_scores / row_total).astype(jnp.bfloat16)
    attended = jnp.einsum(
        "hts,shd->thd", probs_low, values_all, preferred_element_type=jnp.float32
    ).reshape(rows_here, model_width)
    attn_low = attended.astype(jnp.bfloat16)
    residual = block_input + jnp.dot(attn_low, output_w, preferred_element_type=jnp.float32)
    normed_mid, mid_scale = rms_forward(residual, mlp_gain)
    mid_low = normed_mid.astype(jnp.bfloat16)
    router_probs = jax.nn.softmax(
        jnp.dot(mid_low, router_w, preferred_element_type=jnp.float32), axis=-1
    )
    experts_all = router_w.shape[1]
    route_ids = routes[0]
    top_k = route_ids.shape[1]
    capacity = rows_here * top_k * 3 // (2 * experts_all)
    choose = route_ids[:, :, None] == jnp.arange(experts_all, dtype=jnp.int32)[None, None, :]
    gate_probs = jnp.sum(jnp.where(choose, router_probs[:, None, :], 0.0), axis=-1)
    flat_routes = route_ids.reshape(-1)
    onehot = (flat_routes[:, None] == jnp.arange(experts_all, dtype=jnp.int32)[None, :]).astype(
        jnp.int32
    )
    route_rank = jnp.sum(jnp.cumsum(onehot, axis=0) * onehot, axis=1) - 1
    slot_index = flat_routes * capacity + route_rank
    source = (
        jnp.zeros((experts_all * capacity,), jnp.int32)
        .at[slot_index]
        .set(jnp.arange(rows_here * top_k, dtype=jnp.int32) // top_k)
    )
    filled = jnp.zeros((experts_all * capacity, 1), jnp.bfloat16).at[slot_index].set(1.0)
    outgoing = (jnp.take(mid_low, source, axis=0) * filled).reshape(
        experts_all, capacity, model_width
    )
    received = lax.all_to_all(outgoing, "exp", split_axis=0, concat_axis=1, tiled=True)
    gate_pre = jnp.einsum("erd,edf->erf", received, w_gate, preferred_element_type=jnp.float32)
    up_pre = jnp.einsum("erd,edf->erf", received, w_up, preferred_element_type=jnp.float32)
    sigmoid_gate = jax.nn.sigmoid(gate_pre)
    activated = gate_pre * sigmoid_gate
    hidden = (activated * up_pre).astype(jnp.bfloat16)
    expert_out = jnp.einsum(
        "erf,efd->erd", hidden, w_down, preferred_element_type=jnp.float32
    ).astype(jnp.bfloat16)
    returned = lax.all_to_all(expert_out, "exp", split_axis=1, concat_axis=0, tiled=True).reshape(
        experts_all * capacity, model_width
    )
    picked = jnp.take(returned, slot_index, axis=0).reshape(rows_here, top_k, model_width)
    mixed_out = residual
    for which_route in range(top_k):
        mixed_out = mixed_out + gate_probs[:, which_route : which_route + 1] * picked[
            :, which_route
        ].astype(jnp.float32)
    valid_rows = (positions < seq_length).astype(jnp.float32)[:, None]
    grad_out = cotangent[0].astype(jnp.float32) * valid_rows
    d_gates = jnp.stack(
        [
            jnp.sum(grad_out * picked[:, which_route].astype(jnp.float32), axis=-1)
            for which_route in range(top_k)
        ],
        axis=1,
    )
    dy_rows = (
        (gate_probs[:, :, None] * grad_out[:, None, :])
        .astype(jnp.bfloat16)
        .reshape(rows_here * top_k, model_width)
    )
    grad_send = (
        jnp.zeros((experts_all * capacity, model_width), jnp.bfloat16)
        .at[slot_index]
        .set(dy_rows)
        .reshape(experts_all, capacity, model_width)
    )
    grad_recv = lax.all_to_all(grad_send, "exp", split_axis=0, concat_axis=1, tiled=True)
    d_hidden = jnp.einsum("erd,efd->erf", grad_recv, w_down, preferred_element_type=jnp.float32)
    d_gate_pre = (
        d_hidden * up_pre * sigmoid_gate * (1.0 + gate_pre * (1.0 - sigmoid_gate))
    ).astype(jnp.bfloat16)
    d_up_pre = (d_hidden * activated).astype(jnp.bfloat16)
    g_down = jnp.einsum("erf,erd->efd", hidden, grad_recv, preferred_element_type=jnp.float32)
    g_gate = jnp.einsum("erd,erf->edf", received, d_gate_pre, preferred_element_type=jnp.float32)
    g_up = jnp.einsum("erd,erf->edf", received, d_up_pre, preferred_element_type=jnp.float32)
    expert_grads = (
        lax.psum_scatter(
            g_gate.astype(jnp.bfloat16), "ctx", scatter_dimension=1, tiled=True
        ).astype(jnp.float32),
        lax.psum_scatter(g_up.astype(jnp.bfloat16), "ctx", scatter_dimension=1, tiled=True).astype(
            jnp.float32
        ),
        lax.psum_scatter(
            g_down.astype(jnp.bfloat16), "ctx", scatter_dimension=1, tiled=True
        ).astype(jnp.float32),
    )
    d_received = (
        jnp.einsum("erf,edf->erd", d_gate_pre, w_gate, preferred_element_type=jnp.float32)
        + jnp.einsum("erf,edf->erd", d_up_pre, w_up, preferred_element_type=jnp.float32)
    ).astype(jnp.bfloat16)
    d_returned = lax.all_to_all(d_received, "exp", split_axis=1, concat_axis=0, tiled=True).reshape(
        experts_all * capacity, model_width
    )
    back_rows = jnp.take(d_returned, slot_index, axis=0).reshape(rows_here, top_k, model_width)
    d_mid = back_rows[:, 0].astype(jnp.float32)
    for which_route in range(1, top_k):
        d_mid = d_mid + back_rows[:, which_route].astype(jnp.float32)
    d_probs = jnp.sum(jnp.where(choose, d_gates[:, :, None], 0.0), axis=1)
    d_logits = router_probs * (d_probs - jnp.sum(router_probs * d_probs, axis=-1, keepdims=True))
    g_router = over_rows(mid_low.astype(jnp.float32), d_logits)
    d_mid = d_mid + against(d_logits, router_w.astype(jnp.float32))
    d_mid_norm, g_mid_gain = rms_backward(residual, mid_scale, mlp_gain, d_mid)
    d_residual = grad_out + d_mid_norm
    d_res_low = d_residual.astype(jnp.bfloat16)
    g_output = over_rows(attn_low, d_res_low)
    d_attn = against(d_res_low, output_w).astype(jnp.bfloat16).reshape(head_shape)
    probs_again = jnp.exp(scores_of(query_rot) - log_total)
    d_probs_attn = jnp.einsum(
        "thd,shd->hts", d_attn, values_all, preferred_element_type=jnp.float32
    )
    row_inner = jnp.sum(probs_again * d_probs_attn, axis=-1, keepdims=True)
    d_scores = (probs_again * (d_probs_attn - row_inner)).astype(jnp.bfloat16)
    d_query_rot = (
        jnp.einsum("hts,shd->thd", d_scores, keys_all, preferred_element_type=jnp.float32) * factor
    )
    d_keys = (
        jnp.einsum("hts,thd->shd", d_scores, query_rot, preferred_element_type=jnp.float32) * factor
    )
    d_values = jnp.einsum(
        "hts,thd->shd", probs_again.astype(jnp.bfloat16), d_attn, preferred_element_type=jnp.float32
    )
    d_key_rot, d_value = (
        lax.psum_scatter(
            d_keys.astype(jnp.bfloat16), "ctx", scatter_dimension=0, tiled=True
        ).astype(jnp.float32),
        lax.psum_scatter(
            d_values.astype(jnp.bfloat16), "ctx", scatter_dimension=0, tiled=True
        ).astype(jnp.float32),
    )
    d_query_normed = rotate(d_query_rot, cosine_table, -sine_table).reshape(rows_here, model_width)
    d_key_normed = rotate(d_key_rot, cosine_table, -sine_table).reshape(rows_here, model_width)
    d_query_proj, g_query_gain = rms_backward(query_proj, query_scale, query_gain, d_query_normed)
    d_key_proj, g_key_gain = rms_backward(key_proj, key_scale, key_gain, d_key_normed)
    d_query_low = d_query_proj.astype(jnp.bfloat16)
    d_key_low = d_key_proj.astype(jnp.bfloat16)
    value_grad_reduced = d_value.reshape(rows_here, model_width).astype(jnp.bfloat16)
    g_query = over_rows(normed_low, d_query_low)
    g_key = over_rows(normed_low, d_key_low)
    g_value = over_rows(normed_low, value_grad_reduced)
    d_normed_in = (
        against(d_query_low, query_w)
        + against(d_key_low, key_w)
        + against(value_grad_reduced, value_w)
    )
    d_in_norm, g_attn_gain = rms_backward(block_input, in_scale, attn_gain, d_normed_in)
    d_tokens = d_residual + d_in_norm
    weight_terms = (
        g_query,
        g_key,
        g_value,
        g_output,
        g_router,
        g_attn_gain,
        g_query_gain,
        g_key_gain,
        g_mid_gain,
    )
    shards = (
        lax.psum_scatter(
            weight_terms[0].astype(jnp.bfloat16), "exp", scatter_dimension=0, tiled=True
        ).astype(jnp.float32),
        lax.psum_scatter(
            weight_terms[1].astype(jnp.bfloat16), "exp", scatter_dimension=0, tiled=True
        ).astype(jnp.float32),
        lax.psum_scatter(
            weight_terms[2].astype(jnp.bfloat16), "exp", scatter_dimension=0, tiled=True
        ).astype(jnp.float32),
        lax.psum_scatter(
            weight_terms[3].astype(jnp.bfloat16), "exp", scatter_dimension=0, tiled=True
        ).astype(jnp.float32),
        lax.psum_scatter(
            weight_terms[4].astype(jnp.bfloat16), "exp", scatter_dimension=0, tiled=True
        ).astype(jnp.float32),
        lax.psum_scatter(
            weight_terms[5].astype(jnp.bfloat16), "exp", scatter_dimension=0, tiled=True
        ).astype(jnp.float32),
        lax.psum_scatter(
            weight_terms[6].astype(jnp.bfloat16), "exp", scatter_dimension=0, tiled=True
        ).astype(jnp.float32),
        lax.psum_scatter(
            weight_terms[7].astype(jnp.bfloat16), "exp", scatter_dimension=0, tiled=True
        ).astype(jnp.float32),
        lax.psum_scatter(
            weight_terms[8].astype(jnp.bfloat16), "exp", scatter_dimension=0, tiled=True
        ).astype(jnp.float32),
    )
    shards = (
        lax.psum(shards[0].astype(jnp.bfloat16), "ctx").astype(jnp.float32),
        lax.psum(shards[1].astype(jnp.bfloat16), "ctx").astype(jnp.float32),
        lax.psum(shards[2].astype(jnp.bfloat16), "ctx").astype(jnp.float32),
        lax.psum(shards[3].astype(jnp.bfloat16), "ctx").astype(jnp.float32),
        lax.psum(shards[4].astype(jnp.bfloat16), "ctx").astype(jnp.float32),
        lax.psum(shards[5].astype(jnp.bfloat16), "ctx").astype(jnp.float32),
        lax.psum(shards[6].astype(jnp.bfloat16), "ctx").astype(jnp.float32),
        lax.psum(shards[7].astype(jnp.bfloat16), "ctx").astype(jnp.float32),
        lax.psum(shards[8].astype(jnp.bfloat16), "ctx").astype(jnp.float32),
    )
    return (
        mixed_out.astype(jnp.bfloat16)[None],
        d_tokens.astype(jnp.bfloat16)[None],
        shards[0],
        shards[1],
        shards[2],
        shards[3],
        shards[4],
        shards[5],
        shards[6],
        shards[7],
        shards[8],
        expert_grads[0],
        expert_grads[1],
        expert_grads[2],
    )


def solution(mesh):
    return jax.shard_map(
        local,
        mesh=mesh,
        in_specs=(
            P("exp", "ctx", None),
            P("exp", "ctx", None),
            P("exp"),
            P(),
            P("exp", "ctx", None),
            P("exp", None),
            P("exp", None),
            P("exp", None),
            P("exp", None),
            P("exp", None),
            P("exp"),
            P("exp"),
            P("exp"),
            P("exp"),
            P("exp", None, None),
            P("exp", None, None),
            P("exp", None, None),
        ),
        out_specs=(
            P("exp", "ctx", None),
            P("exp", "ctx", None),
            P("exp", None),
            P("exp", None),
            P("exp", None),
            P("exp", None),
            P("exp", None),
            P("exp"),
            P("exp"),
            P("exp"),
            P("exp"),
            P("exp", "ctx", None),
            P("exp", "ctx", None),
            P("exp", "ctx", None),
        ),
        check_vma=False,
    )
```

profile of v0, /device:TPU:0, one launch (start us, length us, event | category | flops | bytes accessed | tf_op | source)
XLA Modules:
  0.0 2917.0 jit_solution(11749836577548426330)
XLA Ops:
  49.9 44.7 %all-gather.15.cloned.1.call-done = bf16[2048,2048]{1,0:T(8,128)(2,1)} async-done(((bf16[256,2048]{1,0:T(8,128)(2,1)}), bf16[2048,2048]{1,0:T(8,128)(2,1)}) %all-gather.15.cloned.1.call-update) | async-done | bytes 8388624 | tf_op jit(solution)/shard_map/all_gather | solution.py:98
  103.5 73.3 %all-gather.17.cloned.1.call-done = bf16[2048,2048]{1,0:T(8,128)(2,1)} async-done(((bf16[256,2048]{1,0:T(8,128)(2,1)}), bf16[2048,2048]{1,0:T(8,128)(2,1)}) %all-gather.17.cloned.1.call-update) | async-done | bytes 8388624 | tf_op jit(solution)/shard_map/all_gather | solution.py:99
  192.7 66.3 %all-gather.11.cloned.1.call-done = bf16[2048,2048]{1,0:T(8,128)(2,1)} async-done(((bf16[256,2048]{1,0:T(8,128)(2,1)}), bf16[2048,2048]{1,0:T(8,128)(2,1)}) %all-gather.11.cloned.1.call-update) | async-done | bytes 8388624 | tf_op jit(solution)/shard_map/all_gather | solution.py:100
  330.0 37.4 %all-gather.13.cloned.1.call-done = bf16[1024,16,128]{0,2,1:T(8,128)(2,1)} async-done(((bf16[256,16,128]{0,2,1:T(8,128)(2,1)}), bf16[1024,16,128]{0,2,1:T(8,128)(2,1)}) %all-gather.13.cloned.1.call-update) | async-done | bytes 4194320 | tf_op jit(solution)/shard_map/all_gather | solution.py:151
  376.5 74.5 %all-gather.21.cloned.1.call-done = bf16[2048,2048]{1,0:T(8,128)(2,1)} async-done(((bf16[256,2048]{1,0:T(8,128)(2,1)}), bf16[2048,2048]{1,0:T(8,128)(2,1)}) %all-gather.21.cloned.1.call-update) | async-done | bytes 8388624 | tf_op jit(solution)/shard_map/all_gather | solution.py:101
  481.0 277.4 %all_to_all.66 = bf16[16,192,2048]{2,1,0:T(8,128)(2,1)S(1)} all-to-all(bf16[16,192,2048]{2,1,0:T(8,128)(2,1)S(1)} %select_multiply_fusion), channel_id=1, replica_groups=mesh['ctx'=4,'exp'=8] {'exp'}, dimensions={0} | all-to-all | bytes 25165824 | tf_op jit(solution)/shard_map/all_to_all | solution.py:198
  782.1 24.7 multiply_convert_fusion.3
  806.9 20.5 convolution_convert_fusion
  827.3 23.7 copy.149
  856.6 279.8 %all_gather.43 = bf16[2048,16]{0,1:T(8,128)(2,1)S(1)} all-gather(bf16[256,16]{0,1:T(8,128)(2,1)S(1)} %copy-done.88), channel_id=1, replica_groups=mesh['ctx'=4,'exp'=8] {'exp'}, dimensions={0}, use_global_device_ids=true | all-gather | bytes 73728 | tf_op jit(solution)/shard_map/all_gather | solution.py:102
  1151.1 22.5 gather_fusion.1
  1181.1 40.1 %fusion.106 = (bf16[256,1,2048]{2,1,0:T(2,128)(2,1)S(1)}, bf16[256,1,2048]{2,1,0:T(2,128)(2,1)S(1)}, bf16[256,1,2048]{2,1,0:T(2,128)(2,1)S(1)}, bf16[256,1,2048]...) fusion(bf16[256,8,2048]{2,1,0:T(8,128)(2,1)} %select_bitcast_fu, ...), kind=kLoop, calls=%fused_computation.266 | loop fusion | bytes 16777216 | tf_op jit(solution)/shard_map/slice | solution.py:213
  1234.6 20.3 scatter_custom_fusion.2
  1255.0 278.3 %all_to_all.67 = bf16[16,192,2048]{2,1,0:T(8,128)(2,1)S(1)} all-to-all(bf16[16,192,2048]{2,1,0:T(8,128)(2,1)} %bitcast.299), channel_id=1, replica_groups=mesh['ctx'=4,'exp'=8] {'exp'}, dimensions={0} | all-to-all | bytes 25165824 | tf_op jit(solution)/shard_map/all_to_all | solution.py:236
  1538.4 25.5 multiply_convert_fusion.1
  1563.9 22.0 fusion.114
  1585.9 22.6 add_convert_fusion
  1608.5 23.7 copy.161
  1638.0 273.6 %all-to-all-done.3 = bf16[2,1536,2048]{2,0,1:T(2,128)(2,1)} async-done(((bf16[2,1536,2048]{2,0,1:T(2,128)(2,1)}), bf16[2,1536,2048]{2,0,1:T(2,128)(2,1)}, u32[]{:S(2)}, u32[]{:S(2)}) %all-to-all-start.3) | async-done | bytes 12582944 | tf_op jit(solution)/shard_map/all_to_all | solution.py:260
  1924.9 22.6 gather_fusion.2
  1955.0 40.0 %fusion.105 = (bf16[256,1,2048]{2,1,0:T(2,128)(2,1)S(1)}, bf16[256,1,2048]{2,1,0:T(2,128)(2,1)S(1)}, bf16[256,1,2048]{2,1,0:T(2,128)(2,1)S(1)}, bf16[256,1,2048]...) fusion(bf16[256,8,2048]{2,1,0:T(8,128)(2,1)} %select_bitcast_fusion), kind=kLoop, calls=%fused_computation.265 | loop fusion | bytes 16777216 | tf_op jit(solution)/shard_map/slice | solution.py:264
  2093.5 40.3 %reduce-scatter.11.cloned.1.call-done = bf16[256,16,128]{2,0,1:T(8,128)(2,1)} async-done(((bf16[1024,16,128]{2,0,1:T(8,128)(2,1)}), bf16[256,16,128]{2,0,1:T(8,128)(2,1)}) %reduce-scatter.11.cloned.1.call-update) | async-done | bytes 1048592 | tf_op jit(solution)/shard_map/reduce_scatter | solution.py:292
  2160.0 20.3 convolution_convert_fusion.5
  2201.0 20.2 convolution_convert_fusion.7
  2225.7 90.1 %reduce-scatter.19.cloned.1.call-done = bf16[256,2048]{1,0:T(8,128)(2,1)} async-done(((bf16[2048,2048]{1,0:T(8,128)(2,1)}), bf16[256,2048]{1,0:T(8,128)(2,1)}) %reduce-scatter.19.cloned.1.call-update) | async-done | bytes 1048592 | tf_op jit(solution)/shard_map/reduce_scatter | solution.py:334
  2315.9 90.3 %reduce-scatter.17.cloned.1.call-done = bf16[256,2048]{1,0:T(8,128)(2,1)} async-done(((bf16[2048,2048]{1,0:T(8,128)(2,1)}), bf16[256,2048]{1,0:T(8,128)(2,1)}) %reduce-scatter.17.cloned.1.call-update) | async-done | bytes 1048592 | tf_op jit(solution)/shard_map/reduce_scatter | solution.py:331
  2406.2 90.1 %reduce-scatter.15.cloned.1.call-done = bf16[256,2048]{1,0:T(8,128)(2,1)} async-done(((bf16[2048,2048]{1,0:T(8,128)(2,1)}), bf16[256,2048]{1,0:T(8,128)(2,1)}) %reduce-scatter.15.cloned.1.call-update) | async-done | bytes 1048592 | tf_op jit(solution)/shard_map/reduce_scatter | solution.py:328
  2511.7 72.5 %reduce-scatter.29.cloned.1.call-done = bf16[2,256,2048]{2,1,0:T(8,128)(2,1)} async-done(((bf16[2,1024,2048]{2,1,0:T(8,128)(2,1)}), bf16[2,256,2048]{2,1,0:T(8,128)(2,1)}) %reduce-scatter.29.cloned.1.call-update) | async-done | bytes 2097168 | tf_op jit(solution)/shard_map/reduce_scatter | solution.py:252
  2588.3 85.5 %reduce-scatter.27.cloned.1.call-done = bf16[2,512,1024]{2,1,0:T(8,128)(2,1)} async-done(((bf16[2,2048,1024]{2,1,0:T(8,128)(2,1)}), bf16[2,512,1024]{2,1,0:T(8,128)(2,1)}) %reduce-scatter.27.cloned.1.call-update) | async-done | bytes 2097168 | tf_op jit(solution)/shard_map/reduce_scatter | solution.py:249
  2677.9 85.3 %reduce-scatter.25.cloned.1.call-done = bf16[2,512,1024]{2,1,0:T(8,128)(2,1)} async-done(((bf16[2,2048,1024]{2,1,0:T(8,128)(2,1)}), bf16[2,512,1024]{2,1,0:T(8,128)(2,1)}) %reduce-scatter.25.cloned.1.call-update) | async-done | bytes 2097168 | tf_op jit(solution)/shard_map/reduce_scatter | solution.py:246
  2783.1 28.5 all-reduce.4
  2834.5 67.9 %all-reduce.9.cloned.1.call-done = (bf16[256,2048]{1,0:T(8,128)(2,1)}, bf16[256,2048]{1,0:T(8,128)(2,1)}, bf16[256,2048]{1,0:T(8,128)(2,1)}, bf16[256,2048]{1,0:T(8,128)(2,1)}) async-done(((bf16[256,2048]{1,0:T(8,128)(2,1)}, bf16[256,2048]{1,0:T(8,128)(2,1)}, bf16[256,2048]{1,0:T(8,128)(2,1)}, bf16[256,2048]{1,0:T(8,128)(2,1)}), (bf16[256,2048]{1,0:T(8,128)(2,1)}, bf16[256,2048]{1,0:T(8,128)(2,1)}, ...) | async-done | bytes 4194320 | tf_op jit(solution)/shard_map/psum | solution.py:357
  (390 shorter events, 495.4 us)
Async XLA Ops:
  7.2 87.3 %all-gather.15.cloned.1.call-start = ((), (), s32[]{:S(2)}) async-start(), calls=%async_computation.16 | async-start | bytes 9437184 | tf_op jit(solution)/shard_map/all_gather | solution.py:98
  8.0 168.8 %all-gather.17.cloned.1.call-start = ((), (), s32[]{:S(2)}) async-start(), calls=%async_computation.17 | async-start | bytes 9437184 | tf_op jit(solution)/shard_map/all_gather | solution.py:99
  8.7 250.3 %all-gather.11.cloned.1.call-start = ((), (), s32[]{:S(2)}) async-start(), calls=%async_computation.14 | async-start | bytes 9437184 | tf_op jit(solution)/shard_map/all_gather | solution.py:100
  9.4 304.0 %all-gather.19.cloned.1.call-start = ((), (), s32[]{:S(2)}) async-start(), calls=%async_computation.18 | async-start | bytes 5242880 | tf_op jit(solution)/shard_map/all_gather | solution.py:150
  23.0 160.2 %copy-start.53 = (f32[8,1,256]{2,1,0:T(1,128)}, f32[8,1,256]{2,1,0:T(1,128)S(1)}, u32[]{:S(2)}) copy-start(f32[8,1,256]{2,1,0:T(1,128)S(1)} %convert_element_type.439) | copy-start | bytes 24580
  42.1 216.9 %copy-start.37 = (f32[8,1,256]{2,1,0:T(1,128)}, f32[8,1,256]{2,1,0:T(1,128)S(1)}, u32[]{:S(2)}) copy-start(f32[8,1,256]{2,1,0:T(1,128)S(1)} %convert_element_type.437) | copy-start | bytes 24580
  48.0 211.0 %copy-start.69 = (f32[256]{0:T(256)}, f32[256]{0:T(256)S(1)}, u32[]{:S(2)}) copy-start(f32[256]{0:T(256)S(1)} %get-tuple-element.99) | copy-start | bytes 3076
  48.7 264.5 %copy-start.80 = (s32[256]{0:T(256)}, s32[256]{0:T(256)S(1)}, u32[]{:S(2)}) copy-start(s32[256]{0:T(256)S(1)} %get-tuple-element.49) | copy-start | bytes 3076
  49.9 137.2 %copy-start.31 = (f32[256,64]{1,0:T(8,128)}, f32[256,64]{1,0:T(8,128)S(1)}, u32[]{:S(2)}) copy-start(f32[256,64]{1,0:T(8,128)S(1)} %get-tuple-element.97) | copy-start | bytes 196612
  190.9 122.6 %copy-start.21 = (bf16[256,16,64]{2,0,1:T(8,128)(2,1)}, bf16[256,16,64]{2,0,1:T(8,128)(2,1)S(1)}, u32[]{:S(2)}) copy-start(bf16[256,16,64]{2,0,1:T(8,128)(2,1)S(1)} %get-tuple-element.68) | copy-start | bytes 1572868
  192.5 175.0 %all-gather.13.cloned.1.call-start = ((), (), s32[]{:S(2)}) async-start(), calls=%async_computation.15 | async-start | bytes 5242880 | tf_op jit(solution)/shard_map/all_gather | solution.py:151
  268.1 182.9 %all-gather.21.cloned.1.call-start = ((), (), s32[]{:S(2)}) async-start(), calls=%async_computation.19 | async-start | bytes 9437184 | tf_op jit(solution)/shard_map/all_gather | solution.py:101
  278.7 178.8 %copy-start.65 = (f32[8,1,256]{2,1,0:T(1,128)}, f32[8,1,256]{2,1,0:T(1,128)S(1)}, u32[]{:S(2)}) copy-start(f32[8,1,256]{2,1,0:T(1,128)S(1)} %convert_element_type.440) | copy-start | bytes 24580
  458.4 678.0 %copy-start = (bf16[256,2048]{1,0:T(8,128)(2,1)}, bf16[256,2048]{1,0:T(8,128)(2,1)S(1)}, u32[]{:S(2)}) copy-start(bf16[256,2048]{1,0:T(8,128)(2,1)S(1)} %multiply_convert_fusion.5) | copy-start | bytes 3145732
  851.0 285.3 %copy-start.81 = (s32[256]{0:T(256)S(1)}, s32[256]{0:T(256)}, u32[]{:S(2)}) copy-start(s32[256]{0:T(256)} %copy-done.80) | copy-start | bytes 3076
  851.1 285.3 %copy-start.56 = (s32[2048]{0:T(1024)S(1)}, s32[2048]{0:T(1024)}, u32[]{:S(2)}) copy-start(s32[2048]{0:T(1024)} %copy-done.55) | copy-start | bytes 24580
  851.1 285.3 %copy-start.64 = (s32[2048]{0:T(1024)S(1)}, s32[2048]{0:T(1024)}, u32[]{:S(2)}) copy-start(s32[2048]{0:T(1024)} %copy-done.63) | copy-start | bytes 24580
  851.1 286.5 %all-to-all-start.1 = ((bf16[2,1536,2048]{2,0,1:T(2,128)(2,1)}), bf16[2,1536,2048]{2,0,1:T(2,128)(2,1)}, u32[]{:S(2)}, u32[]{:S(2)}) async-start(bf16[2,1536,2048]{2,0,1:T(2,128)(2,1)} %copy.149), calls=%async_computation.1 | async-start | bytes 25165824 | tf_op jit(solution)/shard_map/all_to_all | solution.py:207
  1234.4 760.7 %copy-start.47 = (f32[256,16]{0,1:T(8,128)}, f32[256,16]{0,1:T(8,128)S(1)}, u32[]{:S(2)}) copy-start(f32[256,16]{0,1:T(8,128)S(1)} %get-tuple-element.31) | copy-start | bytes 49156
  1632.3 279.3 %all-to-all-start.3 = ((bf16[2,1536,2048]{2,0,1:T(2,128)(2,1)}), bf16[2,1536,2048]{2,0,1:T(2,128)(2,1)}, u32[]{:S(2)}, u32[]{:S(2)}) async-start(bf16[2,1536,2048]{2,0,1:T(2,128)(2,1)} %copy.161), calls=%async_computation.3 | async-start | bytes 25165824 | tf_op jit(solution)/shard_map/all_to_all | solution.py:260
  1637.8 439.4 %reduce-scatter.13.cloned.1.call-start = ((), (), s32[]{:S(2)}) async-start(), calls=%async_computation.21 | async-start | bytes 5242880 | tf_op jit(solution)/shard_map/reduce_scatter | solution.py:295
  1638.0 357.1 %copy-start.94 = (f32[256]{0:T(256)}, f32[256]{0:T(256)S(1)}, u32[]{:S(2)}) copy-start(f32[256]{0:T(256)S(1)} %multiply_reduce_fusion.8) | copy-start | bytes 3076
  2025.6 108.2 %reduce-scatter.11.cloned.1.call-start = ((), (), s32[]{:S(2)}) async-start(), calls=%async_computation.20 | async-start | bytes 5242880 | tf_op jit(solution)/shard_map/reduce_scatter | solution.py:292
  2060.4 165.3 %reduce-scatter.21.cloned.1.call-start = ((), (), s32[]{:S(2)}) async-start(), calls=%async_computation.25 | async-start | bytes 9437184 | tf_op jit(solution)/shard_map/reduce_scatter | solution.py:337
  2067.3 248.6 %reduce-scatter.19.cloned.1.call-start = ((), (), s32[]{:S(2)}) async-start(), calls=%async_computation.24 | async-start | bytes 9437184 | tf_op jit(solution)/shard_map/reduce_scatter | solution.py:334
  2084.3 321.8 %reduce-scatter.17.cloned.1.call-start = ((), (), s32[]{:S(2)}) async-start(), calls=%async_computation.23 | async-start | bytes 9437184 | tf_op jit(solution)/shard_map/reduce_scatter | solution.py:331
  2146.8 349.5 %reduce-scatter.15.cloned.1.call-start = ((), (), s32[]{:S(2)}) async-start(), calls=%async_computation.22 | async-start | bytes 9437184 | tf_op jit(solution)/shard_map/reduce_scatter | solution.py:328
  2159.9 424.2 %reduce-scatter.29.cloned.1.call-start = ((), (), s32[]{:S(2)}) async-start(), calls=%async_computation.29 | async-start | bytes 10485760 | tf_op jit(solution)/shard_map/reduce_scatter | solution.py:252
  2180.3 493.5 %reduce-scatter.27.cloned.1.call-start = ((), (), s32[]{:S(2)}) async-start(), calls=%async_computation.28 | async-start | bytes 10485760 | tf_op jit(solution)/shard_map/reduce_scatter | solution.py:249
  2200.7 562.4 %reduce-scatter.25.cloned.1.call-start = ((), (), s32[]{:S(2)}) async-start(), calls=%async_computation.27 | async-start | bytes 10485760 | tf_op jit(solution)/shard_map/reduce_scatter | solution.py:246
  2221.2 590.7 %reduce-scatter.23.cloned.1.call-start = ((), (), s32[]{:S(2)}) async-start(), calls=%async_computation.26 | async-start | bytes 73728 | tf_op jit(solution)/shard_map/reduce_scatter | solution.py:340
  2223.6 678.8 %all-reduce.9.cloned.1.call-start = ((), (), s32[]{:S(2)}) async-start(), calls=%async_computation.30 | async-start | bytes 8388608 | tf_op jit(solution)/shard_map/psum | solution.py:357
  (93 other events, 1597.9 us)
Sparse Core Ops, SparseCore 0:
  9.7 84.8 all-gather.14
  96.2 80.5 all-gather.16
  178.4 80.5 all-gather.10
  261.3 51.2 all-gather.18
  314.8 52.5 all-gather.12
  368.9 82.0 all-gather.20
  2025.7 51.5 reduce-scatter.12
  2081.1 52.6 reduce-scatter.10
  2136.1 89.5 reduce-scatter.20
  2227.9 87.9 reduce-scatter.18
  2318.2 87.9 reduce-scatter.16
  2408.3 87.9 reduce-scatter.14
  2499.4 84.7 reduce-scatter.28
  2587.4 86.3 reduce-scatter.26
  2676.7 86.3 reduce-scatter.24
  2765.3 30.0 reduce-scatter.22
  2799.0 103.3 all-reduce.8
where the time goes:
time: 2930 us; the launch traced here: 2920 us
  waiting for transfers between devices  1210 us (41%)
  blocking collectives  921 us (31%)
  matrix products  330 us (11%)
  local copies, waits for them, and re-layouts  279 us (10%)
  other arithmetic  151 us (5%)
    all_gather x1, blocking collectives, local(): lax.all_gather(w_router, 'exp', axis=0, tiled=True)  280 us
    all_to_all x1, blocking collectives, local(): lax.all_to_all(grad_send, 'exp', split_axis=0, concat_axis=1, tiled=True)  278 us
    all_to_all x1, blocking collectives, local(): lax.all_to_all(outgoing, 'exp', split_axis=0, concat_axis=1, tiled=True)  277 us
    all_to_all x1, waiting for transfers between devices, local(): lax.all_to_all(d_received, 'exp', split_axis=1, concat_axis=0, tiled=True)  274 us
    reduce_scatter x1, waiting for transfers between devices, local(): lax.psum_scatter(weight_terms[1].astype(jnp.bfloat16), 'exp', scatter_dim...  90.3 us
    reduce_scatter x1, waiting for transfers between devices, local(): lax.psum_scatter(weight_terms[0].astype(jnp.bfloat16), 'exp', scatter_dim...  90.1 us
    reduce_scatter x1, waiting for transfers between devices, local(): lax.psum_scatter(weight_terms[2].astype(jnp.bfloat16), 'exp', scatter_dim...  90.1 us
    reduce_scatter x1, waiting for transfers between devices, local(): lax.psum_scatter(g_up.astype(jnp.bfloat16), 'ctx', scatter_dimension=1, t...  85.5 us
  transfers between devices with their start and end apart: 19, of which 16 were waited for; matrix products, arithmetic and copies ran while one was open for 10% of the time, Pallas kernels for 0%

commit v1 on v0

v1 whole, which is shorter than its diff:
```python
import math

import jax
import jax.numpy as jnp
from jax import lax
from jax.sharding import PartitionSpec as P

HEADS = 16
HEAD_DIM = 128
EPSILON = 1e-05
ROPE_BASE = 10000.0
MASKED_SCORE = -1e30
FACTOR = HEAD_DIM ** (-0.5)
F32 = jnp.float32
BF16 = jnp.bfloat16


def mm(left, right):
    return jnp.dot(left, right, preferred_element_type=F32)


def mm_t(left, right):
    return lax.dot_general(left, right, (((1,), (1,)), ((), ())), preferred_element_type=F32)


def t_mm(left, right):
    return lax.dot_general(left, right, (((0,), (0,)), ((), ())), preferred_element_type=F32)


def rms_scale(rows):
    return lax.rsqrt(jnp.mean(rows * rows, axis=-1, keepdims=True) + EPSILON)


def rms_backward(rows, inv_scale, gain_vec, grad_in):
    weighted = grad_in * gain_vec
    inner_mean = jnp.mean(weighted * rows, axis=-1, keepdims=True)
    d_rows = inv_scale * weighted - rows * (inv_scale * inv_scale * inv_scale) * inner_mean
    return d_rows, jnp.sum(grad_in * rows * inv_scale, axis=0)


def rope_tables(positions):
    half_dim = HEAD_DIM // 2
    frequency = jnp.exp(
        jnp.arange(half_dim, dtype=F32) * (-2.0 * math.log(ROPE_BASE) / HEAD_DIM)
    )
    angle = positions.astype(F32)[:, None] * frequency[None, :]
    return jnp.cos(angle)[:, None, :], jnp.sin(angle)[:, None, :]


def rotate(rows, cosine, sine):
    half_dim = rows.shape[-1] // 2
    first, second = rows[..., :half_dim], rows[..., half_dim:]
    return jnp.concatenate([first * cosine - second * sine, second * cosine + first * sine], axis=-1)


def positions_of(span_order, storage, span_length):
    return jnp.take(span_order, storage // span_length) * span_length + storage % span_length


def gather(block, axis):
    return lax.all_gather(block, axis, axis=0, tiled=True)


def scatter_sum(block, axis, dimension=0):
    return lax.psum_scatter(block, axis, scatter_dimension=dimension, tiled=True)


def local(
    tokens, cotangent, lengths, span_order, routes,
    w_query, w_key, w_value, w_output, w_router,
    gain_attn, gain_query, gain_key, gain_mlp,
    w_gate, w_up, w_down,
):
    n_ctx, n_exp = lax.axis_size("ctx"), lax.axis_size("exp")
    c_at, e_at = lax.axis_index("ctx"), lax.axis_index("exp")
    rows = tokens.shape[1]
    width = tokens.shape[2]
    seq = rows * n_ctx
    cols = width // n_ctx
    heads = HEADS // n_ctx
    shard = width // n_exp
    own = w_gate.shape[0]
    experts = w_router.shape[1]
    seq_length = lengths[0]

    chunk = width // (n_ctx * n_exp)
    moves = []
    for g in range(n_ctx * n_exp):
        source = (g % n_ctx) * n_exp + g // n_ctx
        moves.append((source, g))
    out_piece = lax.dynamic_slice_in_dim(w_output, c_at * chunk, chunk, 0)
    out_piece = lax.ppermute(out_piece, ("ctx", "exp"), moves)

    member = jnp.sum(
        (routes[0][:, :, None] == jnp.arange(experts, dtype=jnp.int32)[None, None, :]).astype(BF16),
        axis=1,
    )
    small = jnp.concatenate(
        [
            w_router.reshape(-1), gain_attn, gain_query, gain_key, gain_mlp, member.reshape(-1),
        ]
    )
    small_all = gather(small[None], "exp")
    at = shard * experts
    router_w = small_all[:, :at].reshape(width, experts)
    gains = []
    for _ in range(4):
        gains.append(small_all[:, at : at + shard].reshape(width).astype(F32))
        at += shard
    attn_gain, query_gain_all, key_gain_all, mlp_gain = gains
    member_all = small_all[:, at:].reshape(n_exp * rows, experts).astype(F32)
    query_gain = lax.dynamic_slice_in_dim(query_gain_all, c_at * cols, cols, 0)
    key_gain = lax.dynamic_slice_in_dim(key_gain_all, c_at * cols, cols, 0)

    qkv_piece = jnp.concatenate(
        [
            lax.dynamic_slice_in_dim(w, c_at * cols, cols, 1)
            for w in (w_query, w_key, w_value)
        ],
        axis=1,
    )
    qkv_w = gather(qkv_piece, "exp")
    x_all = gather(tokens[0], "ctx").astype(F32)
    out_w = gather(out_piece, "exp")
    grad_all_raw = gather(cotangent[0], "exp")

    positions = positions_of(span_order, jnp.arange(seq, dtype=jnp.int32), rows // 2)
    allowed = (positions[None, :] <= positions[:, None]) & (positions[None, :] < seq_length)
    cosine, sine = rope_tables(positions)
    head_shape = (seq, heads, HEAD_DIM)

    in_scale_all = rms_scale(x_all)
    xn = (x_all * in_scale_all * attn_gain).astype(BF16)
    qkv = mm(xn, qkv_w)
    qp, kp, vp = qkv[:, :cols], qkv[:, cols : 2 * cols], qkv[:, 2 * cols :]
    squares = jnp.stack([jnp.sum(qp * qp, axis=-1), jnp.sum(kp * kp, axis=-1)], axis=0)
    squares = lax.psum(squares, "ctx") / width
    q_scale = lax.rsqrt(squares[0] + EPSILON)[:, None]
    k_scale = lax.rsqrt(squares[1] + EPSILON)[:, None]
    q_rot = rotate((qp * q_scale * query_gain).reshape(head_shape), cosine, sine).astype(BF16)
    k_rot = rotate((kp * k_scale * key_gain).reshape(head_shape), cosine, sine).astype(BF16)
    v_low = vp.astype(BF16).reshape(head_shape)

    def scores_of():
        raw = jnp.einsum("thd,shd->hts", q_rot, k_rot, preferred_element_type=F32) * FACTOR
        return jnp.where(allowed[None], raw, MASKED_SCORE)

    scores = scores_of()
    row_max = jnp.max(scores, axis=-1, keepdims=True)
    expo = jnp.exp(scores - row_max)
    total = jnp.sum(expo, axis=-1, keepdims=True)
    probs = expo / total
    probs_low = probs.astype(BF16)
    attended = (
        jnp.einsum("hts,shd->thd", probs_low, v_low, preferred_element_type=F32)
        .reshape(seq, cols)
        .astype(BF16)
    )
    attn_out = scatter_sum(mm(attended, out_w).astype(BF16), "ctx").astype(F32)
    block_input = tokens[0].astype(F32)
    residual = block_input + attn_out
    mid_scale = rms_scale(residual)
    mid_low = (residual * mid_scale * mlp_gain).astype(BF16)
    mid_all = gather(mid_low, "exp")

    lengths_all = gather(lengths, "exp")
    my_positions = positions_of(
        span_order, c_at * rows + jnp.arange(rows, dtype=jnp.int32), rows // 2
    )
    valid_all = (my_positions[None, :] < lengths_all[:, None]).reshape(n_exp * rows, 1)
    grad_all = jnp.where(valid_all, grad_all_raw, jnp.zeros_like(grad_all_raw))

    router = jax.nn.softmax(mm(mid_all, router_w), axis=-1)
    own_cols = e_at * own + jnp.arange(own)
    chosen = router * member_all
    gate_own = lax.dynamic_slice_in_dim(chosen, e_at * own, own, 1)
    member_own = lax.dynamic_slice_in_dim(member_all, e_at * own, own, 1)

    hiddens, d_pres, flows = [], [], []
    for j in range(own):
        gate = gate_own[:, j : j + 1]
        d_hidden = mm_t(grad_all, w_down[j])
        a = mm(mid_all, w_gate[j])
        b = mm(mid_all, w_up[j])
        sig = jax.nn.sigmoid(a)
        silu = a * sig
        hidden = silu * b
        hidden_low = hidden.astype(BF16)
        flows.append(
            gate[:, 0] * jnp.sum(hidden_low.astype(F32) * d_hidden, axis=-1)
        )
        hiddens.append((gate * hidden).astype(BF16))
        dh = gate * d_hidden
        d_pres.append(
            ((dh * b * sig * (1.0 + a * (1.0 - sig))).astype(BF16), (dh * silu).astype(BF16))
        )
    flow = jnp.stack(flows, axis=1)
    one_own = (jnp.arange(experts)[None, :] == own_cols[:, None]).astype(F32)
    d_logit = jnp.sum(flow[:, :, None] * one_own[None], axis=1) - router * jnp.sum(
        flow, axis=1, keepdims=True
    )
    dx = mm_t(d_logit, router_w.astype(F32))
    for j in range(own):
        dx = dx + mm_t(d_pres[j][0], w_gate[j]) + mm_t(d_pres[j][1], w_up[j])
    d_mid = scatter_sum(dx.astype(BF16), "exp").astype(F32)
    y = mm(hiddens[0], w_down[0])
    for j in range(1, own):
        y = y + mm(hiddens[j], w_down[j])
    y_mine = scatter_sum(y.astype(BF16), "exp").astype(F32)
    mixed = (residual + y_mine).astype(BF16)
    g_router = t_mm(mid_all.astype(F32), d_logit)
    g_gate = jnp.stack([t_mm(mid_all, d_pres[j][0]).astype(BF16) for j in range(own)])
    g_up = jnp.stack([t_mm(mid_all, d_pres[j][1]).astype(BF16) for j in range(own)])
    g_down = jnp.stack([t_mm(hiddens[j], grad_all).astype(BF16) for j in range(own)])
    expert_grads = [scatter_sum(g, "ctx", 1).astype(F32) for g in (g_gate, g_up, g_down)]

    valid_mine = (my_positions < seq_length).astype(F32)[:, None]
    grad_mine = cotangent[0].astype(F32) * valid_mine
    d_mid_norm, g_mid_gain = rms_backward(residual, mid_scale, mlp_gain, d_mid)
    d_residual = grad_mine + d_mid_norm
    dl_all = gather(d_residual.astype(BF16), "ctx")

    d_att = mm_t(dl_all, out_w).astype(BF16).reshape(head_shape)
    g_out = t_mm(attended, dl_all)
    d_probs = jnp.einsum("thd,shd->hts", d_att, v_low, preferred_element_type=F32)
    row_inner = jnp.sum(probs * d_probs, axis=-1, keepdims=True)
    d_scores = (probs * (d_probs - row_inner)).astype(BF16)
    dq_rot = jnp.einsum("hts,shd->thd", d_scores, k_rot, preferred_element_type=F32) * FACTOR
    dk_rot = jnp.einsum("hts,thd->shd", d_scores, q_rot, preferred_element_type=F32) * FACTOR
    dv = jnp.einsum("hts,thd->shd", probs_low, d_att, preferred_element_type=F32)
    dq_n = rotate(dq_rot, cosine, -sine).reshape(seq, cols)
    dk_n = rotate(dk_rot, cosine, -sine).reshape(seq, cols)
    inner = jnp.stack(
        [
            jnp.sum(dq_n * query_gain * qp, axis=-1),
            jnp.sum(dk_n * key_gain * kp, axis=-1),
        ],
        axis=0,
    )
    inner = lax.psum(inner, "ctx") / width
    dqp = q_scale * dq_n * query_gain - qp * (q_scale**3) * inner[0][:, None]
    dkp = k_scale * dk_n * key_gain - kp * (k_scale**3) * inner[1][:, None]
    g_query_gain = jnp.sum(dq_n * qp * q_scale, axis=0)
    g_key_gain = jnp.sum(dk_n * kp * k_scale, axis=0)
    d_qkv = jnp.concatenate(
        [dqp.astype(BF16), dkp.astype(BF16), dv.reshape(seq, cols).astype(BF16)], axis=1
    )
    dxn = scatter_sum(mm_t(d_qkv, qkv_w).astype(BF16), "ctx").astype(F32)
    in_scale = rms_scale(block_input)
    d_in_norm, g_attn_gain = rms_backward(block_input, in_scale, attn_gain, dxn)
    d_tokens = (d_residual + d_in_norm).astype(BF16)

    g_qkv = scatter_sum(t_mm(xn, d_qkv).astype(BF16), "exp")
    g_qkv = gather(g_qkv[None], "ctx")
    g_qkv = g_qkv.reshape(n_ctx, shard, 3, cols).transpose(2, 1, 0, 3).reshape(3, shard, width)
    g_qkv = g_qkv.astype(F32)
    g_out = scatter_sum(g_out.astype(BF16), "exp")
    g_out = lax.ppermute(g_out, ("ctx", "exp"), [(b, a) for a, b in moves])
    g_out = gather(g_out, "ctx").astype(F32)

    placed = []
    for part in (g_query_gain, g_key_gain):
        placed.append(
            lax.dynamic_update_slice_in_dim(jnp.zeros((width,), F32), part, c_at * cols, 0)
        )
    small_grads = jnp.concatenate(
        [g_router, jnp.stack([g_attn_gain, placed[0], placed[1], g_mid_gain], axis=1)], axis=1
    )
    small_grads = lax.psum(scatter_sum(small_grads, "exp"), "ctx")
    return (
        mixed[None], d_tokens[None],
        g_qkv[0], g_qkv[1], g_qkv[2], g_out,
        small_grads[:, :experts],
        small_grads[:, experts], small_grads[:, experts + 1],
        small_grads[:, experts + 2], small_grads[:, experts + 3],
        expert_grads[0], expert_grads[1], expert_grads[2],
    )


def solution(mesh):
    tok = P("exp", "ctx", None)
    two, three, one = P("exp", None), P("exp", None, None), P("exp")
    return jax.shard_map(
        local,
        mesh=mesh,
        in_specs=(tok, tok, one, P(), tok) + (two,) * 5 + (one,) * 4 + (three,) * 3,
        out_specs=(tok, tok) + (two,) * 5 + (one,) * 4 + (tok,) * 3,
        check_vma=False,
    )
```

time: 2930 us -> 1460 us (0.50)
  blocking collectives: 921 us -> 67.3 us
  waiting for transfers between devices: 1210 us -> 801 us
  local copies, waits for them, and re-layouts: 279 us -> 58.1 us
  matrix products: 330 us -> 400 us
  other arithmetic: 151 us -> 106 us
    all_to_all x2 -> x0, blocking collectives: 556 us -> none  [the longest x1 278 us: local(): lax.all_to_all(grad_send, 'exp', split_axis=0, concat_axis=1, tiled=True)]
    all_gather x5 -> x1, blocking collectives: 321 us -> 21.9 us  [gather(): return lax.all_gather(block, axis, axis=0, tiled=True)]
    all_to_all x2 -> x0, waiting for transfers between devices: 274 us -> none  [the longest x1 274 us: local(): lax.all_to_all(d_received, 'exp', split_axis=1, concat_axis=0, tiled=True)]
    psum x1 -> x0, waiting for transfers between devices: 67.9 us -> none  [local(): lax.psum(shards[0].astype(jnp.bfloat16), 'ctx').astype(jnp.float32)]
    slice x5 -> x10, local copies, waits for them, and re-layouts: 81.9 us -> 16.3 us  [the longest x2 6.35 us: local(): g_qkv[2]]
    reduce_scatter x10, waiting for transfers between devices: 565 us -> 500 us  [scatter_sum(): lax.psum_scatter(block, axis, scatter_dimension=dimension, tiled=True)]
    gather x3 -> x0, local copies, waits for them, and re-layouts: 61 us -> none  [the longest x1 22.6 us: local(): jnp.take(d_returned, slot_index, axis=0)]
    dot_general x30 -> x32, matrix products: 330 us -> 387 us  [the longest x9 148 us: mm_t(): lax.dot_general(left, right, (((1,), (1,)), ((), ())), preferred_element_...]
  transfers between devices with their start and end apart: 19 -> 20, of which waited for: 16 -> 15; matrix products, arithmetic and copies ran while one was open for 10% -> 22% of each run, Pallas kernels for 0% -> 0%
where the time goes in v1:
time: 1460 us; the launch traced here: 1450 us
  waiting for transfers between devices  801 us (55%)
  matrix products  400 us (27%)
  other arithmetic  106 us (7%)
  blocking collectives  67.3 us (5%)
  local copies, waits for them, and re-layouts  58.1 us (4%)
  between operations  16.5 us (1%)
    reduce_scatter x10, waiting for transfers between devices, scatter_sum(): lax.psum_scatter(block, axis, scatter_dimension=dimension, tiled=True)  500 us
    all_gather x8, waiting for transfers between devices, gather(): return lax.all_gather(block, axis, axis=0, tiled=True)  299 us
    dot_general x9, matrix products, mm_t(): lax.dot_general(left, right, (((1,), (1,)), ((), ())), preferred_element_...  148 us
    dot_general x9, matrix products, mm(): return jnp.dot(left, right, preferred_element_type=F32)  104 us
    dot_general x9, matrix products, t_mm(): lax.dot_general(left, right, (((0,), (0,)), ((), ())), preferred_element_...  97.4 us
  transfers between devices with their start and end apart: 20, of which 15 were waited for; matrix products, arithmetic and copies ran while one was open for 22% of the time, Pallas kernels for 0%

profile of v1, /device:TPU:0, one launch (start us, length us, event | category | flops | bytes accessed | tf_op | source)
XLA Modules:
  0.0 1453.4 jit_solution(6714426274692849206)
XLA Ops:
  14.3 21.9 %all-gather.1 = bf16[73728]{0:T(1024)(128)(2,1)S(1)} all-gather(bf16[9216]{0:T(1024)(128)(2,1)S(1)} %constant_dynamic-update-slice_fusion), channel_id=3, replica_groups=mesh['ctx'=4,'exp'=8] {'exp'}, dimensions={0}, use_global_device_ids=true | all-gather | bytes 165888 | tf_op jit(solution)/shard_map/all_gather | solution.py:61
  48.4 19.7 %all-gather.23.cloned.1.call-done = bf16[1,1024,2048]{2,1,0:T(8,128)(2,1)} async-done(((bf16[1,256,2048]{2,1,0:T(8,128)(2,1)}), bf16[1,1024,2048]{2,1,0:T(8,128)(2,1)}) %all-gather.23.cloned.1.call-update) | async-done | bytes 4194320 | tf_op jit(solution)/shard_map/all_gather | solution.py:61
  71.2 63.9 %all-gather.13.cloned.1.call-done = bf16[2048,1536]{1,0:T(8,128)(2,1)} async-done(((bf16[256,1536]{1,0:T(8,128)(2,1)}), bf16[2048,1536]{1,0:T(8,128)(2,1)}) %all-gather.13.cloned.1.call-update) | async-done | bytes 6291472 | tf_op jit(solution)/shard_map/all_gather | solution.py:61
  175.1 13.0 fusion.138
  203.8 49.0 %reduce-scatter.11.cloned.1.call-done = bf16[256,2048]{1,0:T(8,128)(2,1)} async-done(((bf16[1024,2048]{1,0:T(8,128)(2,1)}), bf16[256,2048]{1,0:T(8,128)(2,1)}) %reduce-scatter.11.cloned.1.call-update) | async-done | bytes 1048592 | tf_op jit(solution)/shard_map/reduce_scatter | solution.py:65
  276.5 63.4 %all-gather.17.cloned.1.call-done = bf16[2048,2048]{1,0:T(8,128)(2,1)} async-done(((bf16[256,2048]{1,0:T(8,128)(2,1)}), bf16[2048,2048]{1,0:T(8,128)(2,1)}) %all-gather.17.cloned.1.call-update) | async-done | bytes 8388624 | tf_op jit(solution)/shard_map/all_gather | solution.py:61
  345.9 13.6 fusion.27
  371.0 51.0 %all-gather.25.cloned.1.call-done = bf16[1,2048,2048]{2,1,0:T(8,128)(2,1)} async-done(((bf16[1,256,2048]{2,1,0:T(8,128)(2,1)}), bf16[1,2048,2048]{2,1,0:T(8,128)(2,1)}) %all-gather.25.cloned.1.call-update) | async-done | bytes 8388624 | tf_op jit(solution)/shard_map/all_gather | solution.py:61
  422.0 24.1 %multiply_reduce_fusion.2 = (f32[2048]{0:T(1024)S(1)}, bf16[2048,1024]{0,1:T(8,128)(2,1)}, bf16[2048,1024]{0,1:T(8,128)(2,1)}, bf16[2048,1024]{0,1:T(8,128)(2,1)}) fusion(f32[2048,1024]{0,1:T(8,128)} %fusion.27, f32[2048,1024]{0,1:T(8,128)} %fusion.31, f32[2048]{0:T(1024)S(1)} %bitcast.284, bf16[2,1024,2048]{2,1,0:T(8,128)(2,1)} %param.33, ...), kind=kOutput, calls=%fused_computation.22 | convolution fusion | flops 8638167040 | bytes 41961472 | tf_op jit(solution)/shard_map/dot_general | solution.py:23
  446.1 15.4 %fusion.25 = f32[2048,2048]{1,0:T(8,128)} fusion(bf16[2048,1024]{0,1:T(8,128)(2,1)} %get-tuple-element.83, bf16[2,2048,1024]{2,1,0:T(8,128)(2,1)} %param.32), kind=kOutput, calls=%fused_computation.54 | convolution fusion | flops 8589934592 | bytes 25165824 | tf_op jit(solution)/shard_map/dot_general | solution.py:23
  461.5 14.4 fusion.29
  487.5 13.6 fusion.19
  501.1 22.7 %multiply_reduce_fusion.1 = (f32[2048]{0:T(1024)S(1)}, bf16[2048,1024]{0,1:T(8,128)(2,1)}, bf16[2048,1024]{0,1:T(8,128)(2,1)}, bf16[2048,1024]{0,1:T(8,128)(2,1)}) fusion(f32[2048,1024]{0,1:T(8,128)} %fusion.15, f32[2048,1024]{0,1:T(8,128)} %fusion.19, f32[2048]{0:T(1024)S(1)} %bitcast.283, bf16[2,1024,2048]{2,1,0:T(8,128)(2,1)} %param.33, ...), kind=kOutput, calls=%fused_computation.21 | convolution fusion | flops 8638167040 | bytes 41961472 | tf_op jit(solution)/shard_map/dot_general | solution.py:23
  523.8 15.6 %fusion.13 = f32[2048,2048]{1,0:T(8,128)} fusion(bf16[2048,1024]{0,1:T(8,128)(2,1)} %get-tuple-element.85, bf16[2,2048,1024]{2,1,0:T(8,128)(2,1)} %param.32), kind=kOutput, calls=%fused_computation.42 | convolution fusion | flops 8589934592 | bytes 25165824 | tf_op jit(solution)/shard_map/dot_general | solution.py:23
  539.4 14.1 fusion.17
  553.7 24.9 %add_convert_fusion = bf16[2048,2048]{1,0:T(8,128)(2,1)} fusion(f32[2048,2048]{1,0:T(8,128)} %fusion.13, f32[2048,2048]{1,0:T(8,128)} %fusion.17, f32[2048,2048]{1,0:T(8,128)} %fusion.25, f32[2048,2048]{1,0:T(8,128)} %fusion.29, bf16[2048,16]{1,0:T(8,128)(2,1)S(1)} %copy-done.14, f32[2048,16]{0,1:T(8,128)S(1)} %multiply_reduce_fusion.6, ...), kind=kOutput, calls=%fused_computation.3 | convolution fusion | flops 155254784 | bytes 75833344 | tf_op jit(solution)/shard_map/dot_general | solution.py:23
  578.7 15.6 %fusion.23 = f32[2048,2048]{1,0:T(8,128)} fusion(bf16[2048,1024]{0,1:T(8,128)(2,1)} %get-tuple-element.82, bf16[2,1024,2048]{2,1,0:T(8,128)(2,1)} %param.33), kind=kOutput, calls=%fused_computation.52 | convolution fusion | flops 8589934592 | bytes 25165824 | tf_op jit(solution)/shard_map/dot_general | solution.py:19
  594.3 15.9 %add_convert_fusion.1 = bf16[2048,2048]{1,0:T(8,128)(2,1)} fusion(f32[2048,2048]{1,0:T(8,128)} %fusion.23, bf16[2048,1024]{0,1:T(8,128)(2,1)S(1)} %copy-done.76, bf16[2,1024,2048]{2,1,0:T(8,128)(2,1)} %param.33), kind=kOutput, calls=%fused_computation.4 | convolution fusion | flops 8598323200 | bytes 33554432 | tf_op jit(solution)/shard_map/dot_general | solution.py:19
  610.4 56.6 %reduce-scatter.15.cloned.1.call-done = bf16[256,2048]{1,0:T(8,128)(2,1)} async-done(((bf16[2048,2048]{1,0:T(8,128)(2,1)}), bf16[256,2048]{1,0:T(8,128)(2,1)}) %reduce-scatter.15.cloned.1.call-update) | async-done | bytes 1048592 | tf_op jit(solution)/shard_map/reduce_scatter | solution.py:65
  669.8 87.6 %reduce-scatter.13.cloned.1.call-done = bf16[256,2048]{1,0:T(8,128)(2,1)} async-done(((bf16[2048,2048]{1,0:T(8,128)(2,1)}), bf16[256,2048]{1,0:T(8,128)(2,1)}) %reduce-scatter.13.cloned.1.call-update) | async-done | bytes 1048592 | tf_op jit(solution)/shard_map/reduce_scatter | solution.py:65
  762.6 50.7 %all-gather.19.cloned.1.call-done = bf16[1024,2048]{1,0:T(8,128)(2,1)} async-done(((bf16[256,2048]{1,0:T(8,128)(2,1)}), bf16[1024,2048]{1,0:T(8,128)(2,1)}) %all-gather.19.cloned.1.call-update) | async-done | bytes 4194320 | tf_op jit(solution)/shard_map/all_gather | solution.py:61
  915.7 13.0 convert_bitcast_fusion
  928.7 12.8 convert_bitcast_fusion.1
  948.4 12.8 convert_bitcast_fusion.2
  980.5 12.8 convert_bitcast_fusion.4
  1032.8 99.1 %reduce-scatter.29.cloned.1.call-done = bf16[2,256,2048]{2,1,0:T(8,128)(2,1)} async-done(((bf16[2,1024,2048]{2,1,0:T(8,128)(2,1)}), bf16[2,256,2048]{2,1,0:T(8,128)(2,1)}) %reduce-scatter.29.cloned.1.call-update) | async-done | bytes 2097168 | tf_op jit(solution)/shard_map/reduce_scatter | solution.py:65
  1136.0 85.5 %reduce-scatter.27.cloned.1.call-done = bf16[2,512,1024]{2,1,0:T(8,128)(2,1)} async-done(((bf16[2,2048,1024]{2,1,0:T(8,128)(2,1)}), bf16[2,512,1024]{2,1,0:T(8,128)(2,1)}) %reduce-scatter.27.cloned.1.call-update) | async-done | bytes 2097168 | tf_op jit(solution)/shard_map/reduce_scatter | solution.py:65
  1225.6 85.3 %reduce-scatter.25.cloned.1.call-done = bf16[2,512,1024]{2,1,0:T(8,128)(2,1)} async-done(((bf16[2,2048,1024]{2,1,0:T(8,128)(2,1)}), bf16[2,512,1024]{2,1,0:T(8,128)(2,1)}) %reduce-scatter.25.cloned.1.call-update) | async-done | bytes 2097168 | tf_op jit(solution)/shard_map/reduce_scatter | solution.py:65
  1315.0 25.0 %all-gather.21.cloned.1.call-done = bf16[256,2048]{1,0:T(8,128)(2,1)} async-done(((bf16[64,2048]{1,0:T(8,128)(2,1)}), bf16[256,2048]{1,0:T(8,128)(2,1)}) %all-gather.21.cloned.1.call-update) | async-done | bytes 1048592 | tf_op jit(solution)/shard_map/all_gather | solution.py:61
  1345.6 27.4 %reduce-scatter.23.cloned.1.call-done = f32[256,20]{0,1:T(8,128)} async-done(((f32[2048,20]{0,1:T(8,128)}), f32[256,20]{0,1:T(8,128)}) %reduce-scatter.23.cloned.1.call-update) | async-done | bytes 20496 | tf_op jit(solution)/shard_map/reduce_scatter | solution.py:65
  1373.0 17.3 %psum.23 = f32[256,20]{0,1:T(8,128)S(1)} all-reduce(f32[256,20]{0,1:T(8,128)} %reduce-scatter.23.cloned.1.call-done), channel_id=1, replica_groups=mesh['ctx'=4,'exp'=8] {'ctx'}, use_global_device_ids=true, to_apply=%region_31.32 | all-reduce | flops 5120 | bytes 40960 | tf_op jit(solution)/shard_map/psum | solution.py:269
  1391.5 25.5 %all-gather.27.cloned.1.call-done = bf16[1024,1536]{1,0:T(8,128)(2,1)} async-done(((bf16[256,1536]{1,0:T(8,128)(2,1)}), bf16[1024,1536]{1,0:T(8,128)(2,1)}) %all-gather.27.cloned.1.call-update) | async-done | bytes 3145744 | tf_op jit(solution)/shard_map/all_gather | solution.py:61
  (361 shorter events, 353.7 us)
Async XLA Ops:
  7.3 60.8 %all-gather.23.cloned.1.call-start = ((), (), s32[]{:S(2)}) async-start(), calls=%async_computation.25 | async-start | bytes 5242880 | tf_op jit(solution)/shard_map/all_gather | solution.py:61
  8.0 127.1 %all-gather.13.cloned.1.call-start = ((), (), s32[]{:S(2)}) async-start(), calls=%async_computation.10 | async-start | bytes 7077888 | tf_op jit(solution)/shard_map/all_gather | solution.py:61
  10.5 185.6 %all-gather.15.cloned.1.call-start = ((), (), s32[]{:S(2)}) async-start(), calls=%async_computation.11 | async-start | bytes 2359296 | tf_op jit(solution)/shard_map/all_gather | solution.py:61
  11.5 36.1 %collective-permute-start = (bf16[64,2048]{1,0:T(8,128)(2,1)S(1)}, bf16[64,2048]{1,0:T(8,128)(2,1)S(1)}, u32[]{:S(2)}, u32[]{:S(2)}) collective-permute-start(bf16[64,2048]{1,0:T(8,128)(2,1)S(1)} %constant_dynamic-slice_fusion.1), channel_id=1, source_target_pairs={{0,0},{8,1},{16,2},{24,3},{1,4},{9,5},{17,6},{25,7},{2,8},{10,9},{... | collective-permute-start | bytes 786440 | tf_op jit(solution)/shard_map/ppermute | solution.py:92
  36.9 121.4 %copy-start.48 = (f32[512]{0:T(512)}, f32[512]{0:T(512)S(1)}, u32[]{:S(2)}) copy-start(f32[512]{0:T(512)S(1)} %dynamic_slice.25) | copy-start | bytes 6148
  37.0 121.3 %copy-start.50 = (f32[512]{0:T(512)}, f32[512]{0:T(512)S(1)}, u32[]{:S(2)}) copy-start(f32[512]{0:T(512)S(1)} %dynamic_slice.24) | copy-start | bytes 6148
  37.0 108.2 %copy-start.41 = (f32[1,2,8,128]{3,1,2,0:T(2,128)}, f32[1,2,8,128]{3,1,2,0:T(2,128)S(1)}, u32[]{:S(2)}) copy-start(f32[1,2,8,128]{3,1,2,0:T(2,128)S(1)} %copy.181) | copy-start | bytes 24580
  47.6 125.1 %copy-start.15 = (f32[1024,64]{1,0:T(8,128)}, f32[1024,64]{1,0:T(8,128)S(1)}, u32[]{:S(2)}) copy-start(f32[1024,64]{1,0:T(8,128)S(1)} %get-tuple-element.128) | copy-start | bytes 786436
  48.4 204.4 %reduce-scatter.11.cloned.1.call-start = ((), (), s32[]{:S(2)}) async-start(), calls=%async_computation.12 | async-start | bytes 5242880 | tf_op jit(solution)/shard_map/reduce_scatter | solution.py:65
  71.2 74.0 %copy-start.63 = (f32[1024]{0:T(1024)}, f32[1024]{0:T(1024)S(1)}, u32[]{:S(2)}) copy-start(f32[1024]{0:T(1024)S(1)} %add_rsqrt_fusion) | copy-start | bytes 12292
  203.1 136.7 %all-gather.17.cloned.1.call-start = ((), (), s32[]{:S(2)}) async-start(), calls=%async_computation.13 | async-start | bytes 9437184 | tf_op jit(solution)/shard_map/all_gather | solution.py:61
  203.7 71.0 %copy-start.35 = (f32[1,2,8,128]{3,1,2,0:T(2,128)}, f32[1,2,8,128]{3,1,2,0:T(2,128)S(1)}, u32[]{:S(2)}) copy-start(f32[1,2,8,128]{3,1,2,0:T(2,128)S(1)} %copy.184) | copy-start | bytes 24580
  257.6 164.4 %all-gather.25.cloned.1.call-start = ((), (), s32[]{:S(2)}) async-start(), calls=%async_computation.26 | async-start | bytes 9437184 | tf_op jit(solution)/shard_map/all_gather | solution.py:61
  258.2 408.8 %reduce-scatter.15.cloned.1.call-start = ((), (), s32[]{:S(2)}) async-start(), calls=%async_computation.15 | async-start | bytes 9437184 | tf_op jit(solution)/shard_map/reduce_scatter | solution.py:65
  274.3 226.8 %copy-start.65 = (pred[2048]{0:T(1024)(128)(4,1)}, pred[2048]{0:T(1024)(128)(4,1)S(1)}, u32[]{:S(2)}) copy-start(pred[2048]{0:T(1024)(128)(4,1)S(1)} %lt.138) | copy-start | bytes 6148
  274.8 70.9 %copy-start.13 = (bf16[2048,16]{1,0:T(8,128)(2,1)}, bf16[2048,16]{1,0:T(8,128)(2,1)S(1)}, u32[]{:S(2)}) copy-start(bf16[2048,16]{1,0:T(8,128)(2,1)S(1)} %reshape.596) | copy-start | bytes 196612
  578.7 178.7 %reduce-scatter.13.cloned.1.call-start = ((), (), s32[]{:S(2)}) async-start(), calls=%async_computation.14 | async-start | bytes 9437184 | tf_op jit(solution)/shard_map/reduce_scatter | solution.py:65
  610.2 147.2 %copy-start.17 = (bf16[1,256,2048]{2,1,0:T(8,128)(2,1)S(1)}, bf16[1,256,2048]{2,1,0:T(8,128)(2,1)}, u32[]{:S(2)}) copy-start(bf16[1,256,2048]{2,1,0:T(8,128)(2,1)} %param.18) | copy-start | bytes 3145732
  610.3 147.2 %copy-start.61 = (f32[256]{0:T(256)S(1)}, f32[256]{0:T(256)}, u32[]{:S(2)}) copy-start(f32[256]{0:T(256)} %get-tuple-element.131) | copy-start | bytes 3076
  610.3 147.1 %copy-start.62 = (f32[256]{0:T(256)S(1)}, f32[256]{0:T(256)}, u32[]{:S(2)}) copy-start(f32[256]{0:T(256)} %get-tuple-element.71) | copy-start | bytes 3076
  610.3 203.0 %all-gather.19.cloned.1.call-start = ((), (), s32[]{:S(2)}) async-start(), calls=%async_computation.16 | async-start | bytes 5242880 | tf_op jit(solution)/shard_map/all_gather | solution.py:61
  762.1 250.3 %reduce-scatter.21.cloned.1.call-start = ((), (), s32[]{:S(2)}) async-start(), calls=%async_computation.19 | async-start | bytes 2359296 | tf_op jit(solution)/shard_map/reduce_scatter | solution.py:65
  844.2 175.8 %reduce-scatter.17.cloned.1.call-start = ((), (), s32[]{:S(2)}) async-start(), calls=%async_computation.17 | async-start | bytes 5242880 | tf_op jit(solution)/shard_map/reduce_scatter | solution.py:65
  902.2 130.6 %reduce-scatter.19.cloned.1.call-start = ((), (), s32[]{:S(2)}) async-start(), calls=%async_computation.18 | async-start | bytes 7077888 | tf_op jit(solution)/shard_map/reduce_scatter | solution.py:65
  915.1 216.8 %reduce-scatter.29.cloned.1.call-start = ((), (), s32[]{:S(2)}) async-start(), calls=%async_computation.24 | async-start | bytes 10485760 | tf_op jit(solution)/shard_map/reduce_scatter | solution.py:65
  947.8 273.7 %reduce-scatter.27.cloned.1.call-start = ((), (), s32[]{:S(2)}) async-start(), calls=%async_computation.23 | async-start | bytes 10485760 | tf_op jit(solution)/shard_map/reduce_scatter | solution.py:65
  980.3 330.6 %reduce-scatter.25.cloned.1.call-start = ((), (), s32[]{:S(2)}) async-start(), calls=%async_computation.22 | async-start | bytes 10485760 | tf_op jit(solution)/shard_map/reduce_scatter | solution.py:65
  1012.3 327.7 %all-gather.21.cloned.1.call-start = ((), (), s32[]{:S(2)}) async-start(), calls=%async_computation.20 | async-start | bytes 1310720 | tf_op jit(solution)/shard_map/all_gather | solution.py:61
  1012.4 1.7 collective-permute-start.1
  1014.9 358.1 %reduce-scatter.23.cloned.1.call-start = ((), (), s32[]{:S(2)}) async-start(), calls=%async_computation.21 | async-start | bytes 221184 | tf_op jit(solution)/shard_map/reduce_scatter | solution.py:65
  1023.2 393.7 %all-gather.27.cloned.1.call-start = ((), (), s32[]{:S(2)}) async-start(), calls=%async_computation.27 | async-start | bytes 3932160 | tf_op jit(solution)/shard_map/all_gather | solution.py:61
  1225.6 117.2 %copy-start.12 = (f32[256,2048]{1,0:T(8,128)S(1)}, f32[256,2048]{1,0:T(8,128)}, u32[]{:S(2)}) copy-start(f32[256,2048]{1,0:T(8,128)} %get-tuple-element.70) | copy-start | bytes 6291460
  (80 other events, 1066.7 us)
Sparse Core Ops, SparseCore 0:
  9.9 58.1 all-gather.22
  70.3 64.7 all-gather.12
  137.3 27.7 all-gather.14
  203.2 49.5 reduce-scatter.10
  257.7 82.0 all-gather.16
  341.4 80.5 all-gather.24
  578.8 88.1 reduce-scatter.14
  669.4 87.9 reduce-scatter.12
  762.2 51.0 all-gather.18
  844.3 35.8 reduce-scatter.20
  902.3 52.8 reduce-scatter.16
  957.4 75.3 reduce-scatter.18
  1035.9 95.9 reduce-scatter.28
  1135.1 86.3 reduce-scatter.26
  1224.4 86.4 reduce-scatter.24
  1313.3 26.5 all-gather.20
  1342.7 30.2 reduce-scatter.22
  1374.7 42.1 all-gather.26

commit v2 on v1

v2 whole, which is shorter than its diff:
```python
import functools
import math

import jax
import jax.numpy as jnp
from jax import lax
from jax.experimental import pallas as pl
from jax.experimental.pallas import tpu as pltpu
from jax.sharding import PartitionSpec as P

HEADS = 16
HEAD_DIM = 128
LANES = 128
EPSILON = 1e-05
ROPE_BASE = 10000.0
MASKED_SCORE = -1e30
FACTOR = HEAD_DIM ** (-0.5)
F32 = jnp.float32
BF16 = jnp.bfloat16
MIB = 1 << 20


def mm(left, right):
    return jnp.dot(left, right, preferred_element_type=F32)


def mm_t(left, right):
    return lax.dot_general(left, right, (((1,), (1,)), ((), ())), preferred_element_type=F32)


def t_mm(left, right):
    return lax.dot_general(left, right, (((0,), (0,)), ((), ())), preferred_element_type=F32)


def rms_scale(rows):
    return lax.rsqrt(jnp.mean(rows * rows, axis=-1, keepdims=True) + EPSILON)


def rms_backward(rows, inv_scale, gain_vec, grad_in):
    weighted = grad_in * gain_vec
    inner_mean = jnp.mean(weighted * rows, axis=-1, keepdims=True)
    d_rows = inv_scale * weighted - rows * (inv_scale * inv_scale * inv_scale) * inner_mean
    return d_rows, jnp.sum(grad_in * rows * inv_scale, axis=0)


def rope_tables(positions):
    half_dim = HEAD_DIM // 2
    frequency = jnp.exp(
        jnp.arange(half_dim, dtype=F32) * (-2.0 * math.log(ROPE_BASE) / HEAD_DIM)
    )
    angle = positions.astype(F32)[:, None] * frequency[None, :]
    cosine, sine = jnp.cos(angle), jnp.sin(angle)
    return (
        jnp.concatenate([cosine, cosine], axis=1),
        jnp.concatenate([-sine, sine], axis=1),
    )


def positions_of(span_order, storage, span_length):
    return jnp.take(span_order, storage // span_length) * span_length + storage % span_length


def rotated(rows, scale, gain, cosine, sine):
    normed = rows * scale * gain
    return (normed * cosine + pltpu.roll(normed, HEAD_DIM // 2, 1) * sine).astype(BF16)


def unrotated(rows, cosine, sine):
    return rows * cosine - pltpu.roll(rows, HEAD_DIM // 2, 1) * sine


def head_probs(query, key, q_pos, k_pos):
    scores = jnp.where(k_pos <= q_pos, mm_t(query, key) * FACTOR, MASKED_SCORE)
    expo = jnp.exp(scores - jnp.max(scores, axis=1, keepdims=True))
    return expo / jnp.sum(expo, axis=1, keepdims=True)


def attend_kernel(
    q_ref, k_ref, v_ref, qs_ref, ks_ref, qg_ref, kg_ref, qc_ref, qn_ref, kc_ref, kn_ref,
    qp_ref, kp_ref, out_ref,
):
    query = rotated(q_ref[...], qs_ref[...], qg_ref[...], qc_ref[...], qn_ref[...])
    key = rotated(k_ref[...], ks_ref[...], kg_ref[...], kc_ref[...], kn_ref[...])
    probs = head_probs(query, key, qp_ref[...], kp_ref[...])
    out_ref[...] = mm(probs.astype(BF16), v_ref[...].astype(BF16)).astype(BF16)


def attend_back_kernel(
    q_ref, k_ref, v_ref, qs_ref, ks_ref, qg_ref, kg_ref, qc_ref, qn_ref, kc_ref, kn_ref,
    qp_ref, kp_ref, da_ref, dk_in, dv_in, *refs,
):
    dq_ref, dk_ref, dv_ref = refs[-3:]
    query = rotated(q_ref[...], qs_ref[...], qg_ref[...], qc_ref[...], qn_ref[...])
    key = rotated(k_ref[...], ks_ref[...], kg_ref[...], kc_ref[...], kn_ref[...])
    probs = head_probs(query, key, qp_ref[...], kp_ref[...])
    d_att = da_ref[...]
    d_probs = mm_t(d_att, v_ref[...].astype(BF16))
    inner = jnp.sum(probs * d_probs, axis=1, keepdims=True)
    d_scores = (probs * (d_probs - inner)).astype(BF16)
    dq_ref[...] = unrotated(mm(d_scores, key) * FACTOR, qc_ref[...], qn_ref[...])
    dk = unrotated(t_mm(d_scores, query) * FACTOR, kc_ref[...], kn_ref[...])
    dk_ref[...] = dk_in[...] + dk
    dv_ref[...] = dv_in[...] + t_mm(probs.astype(BF16), d_att)


def attention_specs(rows, seq, heads, h):
    def head_rows(n, at, row=0):
        return pl.BlockSpec((n, HEAD_DIM), lambda i: (row, at + i))

    def fixed(shape, row=0):
        return pl.BlockSpec(shape, lambda i: (row, 0))

    return [
        head_rows(rows, 0, h), head_rows(seq, heads), head_rows(seq, 2 * heads),
        fixed((rows, 1), h), fixed((seq, 1)), head_rows(1, 0), head_rows(1, 0),
        fixed((rows, HEAD_DIM), h), fixed((rows, HEAD_DIM), h),
        fixed((seq, HEAD_DIM)), fixed((seq, HEAD_DIM)),
        fixed((rows, 1), h), fixed((1, seq)),
    ]


def attend(base, rows, h):
    seq, cols = base[0].shape[0], base[0].shape[1] // 3
    heads = cols // HEAD_DIM
    return pl.pallas_call(
        attend_kernel,
        grid=(heads,),
        in_specs=attention_specs(rows, seq, heads, h),
        out_specs=pl.BlockSpec((rows, HEAD_DIM), lambda i: (0, i)),
        out_shape=jax.ShapeDtypeStruct((rows, cols), BF16),
        compiler_params=pltpu.CompilerParams(vmem_limit_bytes=48 * MIB),
        cost_estimate=pl.CostEstimate(
            flops=4 * rows * seq * cols, bytes_accessed=8 * MIB, transcendentals=rows * seq * heads
        ),
    )(*base)


def attend_back(base, rows, h, d_att, dk, dv, earlier):
    seq, cols = base[0].shape[0], base[0].shape[1] // 3
    heads = cols // HEAD_DIM
    q_out = pl.BlockSpec((rows, HEAD_DIM), lambda i: (0, i))
    k_out = pl.BlockSpec((seq, HEAD_DIM), lambda i: (0, i))
    return pl.pallas_call(
        attend_back_kernel,
        grid=(heads,),
        in_specs=attention_specs(rows, seq, heads, h)
        + [q_out, k_out, k_out]
        + [pl.BlockSpec(memory_space=pl.ANY)] * len(earlier),
        out_specs=[q_out, k_out, k_out],
        out_shape=[
            jax.ShapeDtypeStruct((rows, cols), F32),
            jax.ShapeDtypeStruct((seq, cols), F32),
            jax.ShapeDtypeStruct((seq, cols), F32),
        ],
        compiler_params=pltpu.CompilerParams(vmem_limit_bytes=48 * MIB),
        cost_estimate=pl.CostEstimate(
            flops=10 * rows * seq * cols, bytes_accessed=16 * MIB, transcendentals=rows * seq * heads
        ),
    )(*base, d_att, dk, dv, *earlier)


def expert_kernel(
    experts, own, step, x_ref, dh_ref, member_ref, router_ref, pick_ref, wg_hbm, wu_hbm,
    hid_ref, da_ref, db_ref, dx_ref, coef_ref, wg, wu, sems,
):
    i = pl.program_id(0)

    def loads(j):
        return (
            pltpu.make_async_copy(wg_hbm.at[j], wg.at[j], sems.at[0, j]),
            pltpu.make_async_copy(wu_hbm.at[j], wu.at[j], sems.at[1, j]),
        )

    @pl.when(i == 0)
    def _():
        for j in range(own):
            for copy in loads(j):
                copy.start()

    logits = mm(x_ref[...], router_ref[...])
    lane = lax.broadcasted_iota(jnp.int32, logits.shape, 1)
    logits = jnp.where(lane < experts, logits, MASKED_SCORE)
    expo = jnp.exp(logits - jnp.max(logits, axis=1, keepdims=True))
    router = expo / jnp.sum(expo, axis=1, keepdims=True)
    chosen = router * member_ref[...].astype(F32)
    coef = jnp.zeros_like(router)
    ff = wg.shape[2]
    for j in range(own):

        @pl.when(i == 0)
        def _():
            for copy in loads(j):
                copy.wait()

        pick = pick_ref[j : j + 1, :]
        gate = jnp.sum(chosen * pick, axis=1, keepdims=True)
        flow = jnp.zeros_like(gate)
        for f in range(0, ff, step):
            cut = slice(f, f + step)
            a = mm(x_ref[...], wg[j, :, cut])
            b = mm(x_ref[...], wu[j, :, cut])
            d_hid = dh_ref[j, :, cut].astype(F32)
            sig = jax.nn.sigmoid(a)
            silu = a * sig
            hid = silu * b
            flow = flow + jnp.sum(hid * d_hid, axis=1, keepdims=True)
            hid_ref[j, :, cut] = (gate * hid).astype(BF16)
            d_hid = d_hid * gate
            da_ref[j, :, cut] = (d_hid * b * (sig + silu * (1.0 - sig))).astype(BF16)
            db_ref[j, :, cut] = (d_hid * silu).astype(BF16)
        coef = coef + flow * gate * (pick - router)
    low = coef.astype(BF16)
    coef_ref[...] = low
    width = x_ref.shape[1]
    for n in range(0, width, step):
        cut = slice(n, n + step)
        part = mm_t(low, router_ref[cut, :])
        for j in range(own):
            part = part + mm_t(da_ref[j], wg[j, cut, :]) + mm_t(db_ref[j], wu[j, cut, :])
        dx_ref[:, cut] = part.astype(BF16)


def expert_pass(x, d_hid, member, router_w, pick, w_gate, w_up, experts):
    rows, width = x.shape
    own, _, ff = w_gate.shape
    tile = 256
    by_row = pl.BlockSpec((tile, width), lambda i: (i, 0))
    by_lane = pl.BlockSpec((tile, LANES), lambda i: (i, 0))
    by_expert = pl.BlockSpec((own, tile, ff), lambda i: (0, i, 0))
    return pl.pallas_call(
        functools.partial(expert_kernel, experts, own, 512),
        grid=(rows // tile,),
        in_specs=[
            by_row, by_expert, by_lane,
            pl.BlockSpec((width, LANES), lambda i: (0, 0)),
            pl.BlockSpec(pick.shape, lambda i: (0, 0)),
            pl.BlockSpec(memory_space=pl.ANY),
            pl.BlockSpec(memory_space=pl.ANY),
        ],
        out_specs=[by_expert] * 3 + [by_row, by_lane],
        out_shape=[jax.ShapeDtypeStruct((own, rows, ff), BF16)] * 3
        + [jax.ShapeDtypeStruct((rows, width), BF16), jax.ShapeDtypeStruct((rows, LANES), BF16)],
        scratch_shapes=[
            pltpu.VMEM((own, width, ff), BF16),
            pltpu.VMEM((own, width, ff), BF16),
            pltpu.SemaphoreType.DMA((2, own)),
        ],
        compiler_params=pltpu.CompilerParams(vmem_limit_bytes=56 * MIB),
        cost_estimate=pl.CostEstimate(
            flops=8 * rows * width * ff * own, bytes_accessed=40 * MIB, transcendentals=0
        ),
    )(x, d_hid, member, router_w, pick, w_gate, w_up)


def grad_kernel(n, count, table, *refs):
    lefts, rights, outs = refs[:n], refs[n : n + n * count], refs[len(refs) - count :]
    for k, out in enumerate(outs):
        total = None
        for h in range(n):
            left = lefts[h]
            left = left[0] if len(left.shape) == 3 else left[...]
            right = rights[k * n + h]
            right = right[0] if len(right.shape) == 3 else right[...]
            part = t_mm(left, right)
            total = part if total is None else total + part
        out[...] = total.astype(BF16)


def expert_grads(table, lefts, rights, block, j, earlier=()):
    n = len(lefts)

    def left_spec(a):
        if a.ndim == 3:
            return pl.BlockSpec((1, a.shape[1], block), lambda i, t: (j, 0, t[i]))
        return pl.BlockSpec((a.shape[0], block), lambda i, t: (0, t[i]))

    def right_spec(a):
        if a.ndim == 3:
            return pl.BlockSpec((1,) + a.shape[1:], lambda i, t: (j, 0, 0))
        return pl.BlockSpec(a.shape, lambda i, t: (0, 0))

    flat = [a for group in rights for a in group]
    blocks = table.shape[0]
    outs = [jax.ShapeDtypeStruct((blocks * block, g[0].shape[-1]), BF16) for g in rights]
    depth = sum(a.shape[-2] for a in lefts)
    return pl.pallas_call(
        functools.partial(grad_kernel, n, len(rights)),
        grid_spec=pltpu.PrefetchScalarGridSpec(
            num_scalar_prefetch=1,
            grid=(blocks,),
            in_specs=[left_spec(a) for a in lefts]
            + [right_spec(a) for a in flat]
            + [pl.BlockSpec(memory_space=pl.ANY)] * len(earlier),
            out_specs=[pl.BlockSpec((block, o.shape[1]), lambda i, t: (i, 0)) for o in outs],
        ),
        out_shape=outs,
        compiler_params=pltpu.CompilerParams(vmem_limit_bytes=56 * MIB),
        cost_estimate=pl.CostEstimate(
            flops=sum(2 * depth * o.shape[0] * o.shape[1] for o in outs),
            bytes_accessed=16 * MIB,
            transcendentals=0,
        ),
    )(table, *lefts, *flat, *earlier)


def out_kernel(own, hid_ref, w_ref, *refs):
    total = mm(hid_ref[0], w_ref[0])
    for j in range(1, own):
        total = total + mm(hid_ref[j], w_ref[j])
    refs[-1][...] = total.astype(BF16)


def experts_out(hid, w_down, earlier=()):
    own, rows, ff = hid.shape
    width = w_down.shape[2]
    tile = 512
    return pl.pallas_call(
        functools.partial(out_kernel, own),
        grid=(width // tile,),
        in_specs=[
            pl.BlockSpec((own, rows, ff), lambda i: (0, 0, 0)),
            pl.BlockSpec((own, ff, tile), lambda i: (0, 0, i)),
        ]
        + [pl.BlockSpec(memory_space=pl.ANY)] * len(earlier),
        out_specs=pl.BlockSpec((rows, tile), lambda i: (0, i)),
        out_shape=jax.ShapeDtypeStruct((rows, width), BF16),
        compiler_params=pltpu.CompilerParams(vmem_limit_bytes=48 * MIB),
        cost_estimate=pl.CostEstimate(
            flops=2 * own * rows * ff * width, bytes_accessed=16 * MIB, transcendentals=0
        ),
    )(hid, w_down, *earlier)


def mid_kernel(n, x_ref, own_ref, gain_ref, *refs):
    total = x_ref[...].astype(F32) + own_ref[...]
    for got in refs[: n - 1]:
        total = total + got[...].astype(F32)
    res_ref, scale_ref, low_ref = refs[-3:]
    scale = lax.rsqrt(jnp.mean(total * total, axis=1, keepdims=True) + EPSILON)
    res_ref[...] = total
    scale_ref[...] = scale
    low_ref[...] = (total * scale * gain_ref[...]).astype(BF16)


def middle(x, own_block, got, gain, earlier):
    rows, width = x.shape
    whole = pl.BlockSpec(memory_space=pltpu.VMEM)
    return pl.pallas_call(
        functools.partial(mid_kernel, len(got) + 1),
        in_specs=[whole] * (3 + len(got)) + [pl.BlockSpec(memory_space=pl.ANY)] * len(earlier),
        out_specs=[whole] * 3,
        out_shape=[
            jax.ShapeDtypeStruct((rows, width), F32),
            jax.ShapeDtypeStruct((rows, 1), F32),
            jax.ShapeDtypeStruct((rows, width), BF16),
        ],
        compiler_params=pltpu.CompilerParams(vmem_limit_bytes=32 * MIB),
    )(x, own_block, gain[None], *got, *earlier)


def res_kernel(res_ref, scale_ref, gain_ref, grad_ref, mid_ref, *refs):
    out_ref, low_ref, gain_out = refs[-3:]
    rows, scale = res_ref[...], scale_ref[...]
    grad_in = mid_ref[...].astype(F32)
    weighted = grad_in * gain_ref[...]
    inner = jnp.mean(weighted * rows, axis=1, keepdims=True)
    total = grad_ref[...] + scale * weighted - rows * (scale * scale * scale) * inner
    out_ref[...] = total
    low_ref[...] = total.astype(BF16)
    gain_out[...] = jnp.sum(grad_in * rows * scale, axis=0, keepdims=True)


def residual_back(residual, scale, gain, grad, d_mid, earlier):
    rows, width = residual.shape
    whole = pl.BlockSpec(memory_space=pltpu.VMEM)
    return pl.pallas_call(
        res_kernel,
        in_specs=[whole] * 5 + [pl.BlockSpec(memory_space=pl.ANY)] * len(earlier),
        out_specs=[whole] * 3,
        out_shape=[
            jax.ShapeDtypeStruct((rows, width), F32),
            jax.ShapeDtypeStruct((rows, width), BF16),
            jax.ShapeDtypeStruct((1, width), F32),
        ],
        compiler_params=pltpu.CompilerParams(vmem_limit_bytes=32 * MIB),
    )(residual, scale, gain[None], grad, d_mid, *earlier)


def meet(peers):
    barrier = pltpu.get_barrier_semaphore()
    for peer in peers:
        pl.semaphore_signal(barrier, inc=1, device_id=peer, device_id_type=pl.DeviceIdType.MESH)
    pl.semaphore_wait(barrier, len(peers))


def ctx_sum_kernel(n, x_ref, out_ref, slots, send, recv):
    me = lax.axis_index("ctx")
    peers = [{"ctx": lax.rem(me + d, n)} for d in range(1, n)]
    meet(peers)
    slots[me] = x_ref[...]
    copies = [
        pltpu.make_async_remote_copy(
            src_ref=x_ref, dst_ref=slots.at[me], send_sem=send.at[d], recv_sem=recv.at[d],
            device_id=peer, device_id_type=pl.DeviceIdType.MESH,
        )
        for d, peer in enumerate(peers)
    ]
    for copy in copies:
        copy.start()
    for copy in copies:
        copy.wait()
    total = slots[0]
    for k in range(1, n):
        total = total + slots[k]
    out_ref[...] = total


def ctx_sum(x, number):
    n = lax.axis_size("ctx")
    whole = pl.BlockSpec(memory_space=pltpu.VMEM)
    return pl.pallas_call(
        functools.partial(ctx_sum_kernel, n),
        in_specs=[whole],
        out_specs=whole,
        out_shape=jax.ShapeDtypeStruct(x.shape, F32),
        scratch_shapes=[
            pltpu.VMEM((n,) + x.shape, F32),
            pltpu.SemaphoreType.DMA((n - 1,)),
            pltpu.SemaphoreType.DMA((n - 1,)),
        ],
        compiler_params=pltpu.CompilerParams(collective_id=number, has_side_effects=True),
    )(x)


def all_sum_kernel(n_ctx, n_exp, x_ref, *refs):
    out_ref, first, second, sems = refs[-4:]
    c_at, e_at = lax.axis_index("ctx"), lax.axis_index("exp")
    across = [{"exp": lax.rem(e_at + d, n_exp)} for d in range(1, n_exp)]
    along = [{"ctx": lax.rem(c_at + d, n_ctx)} for d in range(1, n_ctx)]
    meet(across + along)
    first[e_at] = x_ref[e_at]
    copies = [
        pltpu.make_async_remote_copy(
            src_ref=x_ref.at[peer["exp"]], dst_ref=first.at[e_at],
            send_sem=sems.at[0, d], recv_sem=sems.at[1, d],
            device_id=peer, device_id_type=pl.DeviceIdType.MESH,
        )
        for d, peer in enumerate(across)
    ]
    for copy in copies:
        copy.start()
    for copy in copies:
        copy.wait()
    total = first[0]
    for k in range(1, n_exp):
        total = total + first[k]
    second[c_at] = total
    copies = [
        pltpu.make_async_remote_copy(
            src_ref=second.at[c_at], dst_ref=second.at[c_at],
            send_sem=sems.at[2, d], recv_sem=sems.at[3, d],
            device_id=peer, device_id_type=pl.DeviceIdType.MESH,
        )
        for d, peer in enumerate(along)
    ]
    for copy in copies:
        copy.start()
    for copy in copies:
        copy.wait()
    total = second[0]
    for k in range(1, n_ctx):
        total = total + second[k]
    out_ref[...] = total


def all_sum(x, number, earlier):
    n_ctx, n_exp = lax.axis_size("ctx"), lax.axis_size("exp")
    whole = pl.BlockSpec(memory_space=pltpu.VMEM)
    return pl.pallas_call(
        functools.partial(all_sum_kernel, n_ctx, n_exp),
        in_specs=[whole] + [pl.BlockSpec(memory_space=pl.ANY)] * len(earlier),
        out_specs=whole,
        out_shape=jax.ShapeDtypeStruct(x.shape[1:], F32),
        scratch_shapes=[
            pltpu.VMEM(x.shape, F32),
            pltpu.VMEM((n_ctx,) + x.shape[1:], F32),
            pltpu.SemaphoreType.DMA((4, max(n_ctx, n_exp) - 1)),
        ],
        compiler_params=pltpu.CompilerParams(collective_id=number, has_side_effects=True),
    )(x, *earlier)


def gather(block, axis):
    return lax.all_gather(block, axis, axis=0, tiled=True)


def scatter_sum(block, axis, dimension=0):
    return lax.psum_scatter(block, axis, scatter_dimension=dimension, tiled=True)


def after(value, *earlier):
    return lax.optimization_barrier((value,) + earlier)[0]


def swap(block, bits):
    n = lax.axis_size("ctx")
    return lax.ppermute(block, "ctx", [(i, i ^ bits) for i in range(n)])


def take(block, at, size=1, axis=0):
    return lax.dynamic_slice_in_dim(block, at, size, axis)


def gather_ctx(block, axis):
    n, me = lax.axis_size("ctx"), lax.axis_index("ctx")
    parts = [block] + [swap(block, d) for d in range(1, n)]
    shape = block.shape[:axis] + (n,) + block.shape[axis:]
    out = jnp.zeros(shape, block.dtype)
    for d, piece in enumerate(parts):
        out = lax.dynamic_update_slice_in_dim(out, jnp.expand_dims(piece, axis), me ^ d, axis)
    return out


def halving_masks(order):
    masks = [0]
    for bit in order[::-1]:
        masks = masks + [m | (1 << bit) for m in masks]
    return masks


def halve(keep, got, order):
    bits = list(order[1:])
    while True:
        total = keep.astype(F32) + got.astype(F32)
        if not bits:
            return total
        total = total.astype(BF16)
        rows = total.shape[0] // 2
        keep, got = total[:rows], swap(total[rows:], 1 << bits.pop(0))


def local(
    tokens, cotangent, lengths, span_order, routes,
    w_query, w_key, w_value, w_output, w_router,
    gain_attn, gain_query, gain_key, gain_mlp,
    w_gate, w_up, w_down,
):
    n_ctx, n_exp = lax.axis_size("ctx"), lax.axis_size("exp")
    c_at, e_at = lax.axis_index("ctx"), lax.axis_index("exp")
    rows = tokens.shape[1]
    width = tokens.shape[2]
    seq = rows * n_ctx
    cols = width // n_ctx
    shard = width // n_exp
    own = w_gate.shape[0]
    ff = w_gate.shape[2]
    experts = w_router.shape[1]
    seq_length = lengths[0]
    halves = 2
    part = rows // halves
    half_seq = part * n_ctx

    chunk = width // (n_ctx * n_exp)
    moves = []
    for g in range(n_ctx * n_exp):
        source = (g % n_ctx) * n_exp + g // n_ctx
        moves.append((source, g))
    out_piece = lax.ppermute(take(w_output, c_at * chunk, chunk), ("ctx", "exp"), moves)

    x_low = gather_ctx(tokens[0].reshape(halves, part, width), 1).reshape(seq, width)
    storage = jnp.arange(seq, dtype=jnp.int32)
    storage = (storage % half_seq // part) * rows + storage // half_seq * part + storage % part
    positions = positions_of(span_order, storage, rows // 2)
    my_positions = positions_of(
        span_order, c_at * rows + jnp.arange(rows, dtype=jnp.int32), rows // 2
    )
    valid = (my_positions < seq_length).astype(F32)[:, None]
    member = jnp.sum(
        (routes[0][:, :, None] == jnp.arange(LANES, dtype=jnp.int32)[None, None, :]).astype(BF16),
        axis=1,
    )
    small = jnp.concatenate(
        [
            w_router.reshape(-1), gain_attn, gain_query, gain_key, gain_mlp,
            member[:, :experts].reshape(-1),
        ]
    )
    small_all = gather(small[None], "exp")
    at = shard * experts
    router_w = small_all[:, :at].reshape(width, experts)
    router_w = jnp.pad(router_w, ((0, 0), (0, LANES - experts)))
    gains = []
    for _ in range(4):
        gains.append(small_all[:, at : at + shard].reshape(width).astype(F32))
        at += shard
    attn_gain, query_gain_all, key_gain_all, mlp_gain = gains
    member_all = small_all[:, at:].reshape(n_exp, rows, experts)
    member_all = jnp.pad(member_all, ((0, 0), (0, 0), (0, LANES - experts)))
    query_gain = take(query_gain_all, c_at * cols, cols)
    key_gain = take(key_gain_all, c_at * cols, cols)

    qkv_piece = jnp.concatenate(
        [take(w, c_at * cols, cols, 1) for w in (w_query, w_key, w_value)], axis=1
    )
    qkv_w = gather(qkv_piece, "exp")
    out_w = gather(out_piece, "exp")
    x_all = x_low.astype(F32)

    grad_mine = cotangent[0].astype(F32) * valid
    grad_low = grad_mine.astype(BF16)
    grad_parts = [gather(grad_low[h * part : (h + 1) * part], "exp") for h in range(halves)]
    d_hid_parts = [
        jnp.stack([mm_t(g, w_down[j]).astype(BF16) for j in range(own)]) for g in grad_parts
    ]

    cosine, sine = rope_tables(positions)
    xn = (x_all * rms_scale(x_all) * attn_gain).astype(BF16)
    qkv = mm(xn, qkv_w)
    qp, kp = qkv[:, :cols], qkv[:, cols : 2 * cols]
    squares = jnp.stack([jnp.sum(qp * qp, axis=-1), jnp.sum(kp * kp, axis=-1)], axis=0)
    squares = ctx_sum(jnp.pad(squares, ((0, 6), (0, 0))), 0)[:2] / width
    q_scale = lax.rsqrt(squares[0] + EPSILON)[:, None]
    k_scale = lax.rsqrt(squares[1] + EPSILON)[:, None]
    key_positions = jnp.where(positions < seq_length, positions, jnp.int32(1 << 30))
    base = (
        qkv, qkv, qkv, q_scale, k_scale, query_gain[None], key_gain[None],
        cosine, sine, cosine, sine, positions[:, None], key_positions[None],
    )

    attended_parts, mids, residual_parts, scale_parts = [], [], [], []
    for h in range(halves):
        attended = attend(base, half_seq, h)
        attended_parts.append(attended)
        got = []
        for d in range(n_ctx - 1, -1, -1):
            block = mm(take(attended, (c_at ^ d) * part, part), out_w)
            if d:
                got.append(swap(block.astype(BF16), d))
        residual, scale, mid = middle(
            tokens[0, h * part : (h + 1) * part], block, got, mlp_gain, grad_parts[-1:]
        )
        residual_parts.append(residual)
        scale_parts.append(scale)
        mids.append(gather(mid, "exp"))

    lane = jnp.arange(LANES, dtype=jnp.int32)[None, :]
    pick = (lane == e_at * own + jnp.arange(max(own, 8), dtype=jnp.int32)[:, None]).astype(F32)
    hid_parts, da_parts, db_parts, coef_parts = [], [], [], []
    dxs = []
    for h in range(halves):
        member_h = member_all[:, h * part : (h + 1) * part].reshape(n_exp * part, LANES)
        hid, da, db, dx, coef = expert_pass(
            mids[h], d_hid_parts[h], member_h, router_w, pick, w_gate, w_up, experts
        )
        hid_parts.append(hid)
        da_parts.append(da)
        db_parts.append(db)
        coef_parts.append(coef)
        dxs.append(dx)
    d_mids = [scatter_sum(after(dx, mids[-1]), "exp") for dx in dxs]

    def back_to_rows(h, *earlier):
        d_residual, low, g_gain = residual_back(
            residual_parts[h], scale_parts[h], mlp_gain,
            grad_mine[h * part : (h + 1) * part], d_mids[h], earlier,
        )
        dl = gather_ctx(low, 0).reshape(half_seq, width)
        return d_residual, low, g_gain, dl

    g_router = sum(t_mm(c, m) for m, c in zip(mids, coef_parts))[:experts]

    bits = list(range(n_ctx.bit_length() - 1))
    orders = [bits if j % 2 == 0 else bits[::-1] for j in range(own)]
    cut = n_ctx // 2
    tables = [c_at ^ jnp.asarray(halving_masks(order), jnp.int32) for order in orders]

    def down_grads(j, table, *earlier):
        return expert_grads(table, hid_parts, [grad_parts], ff // n_ctx, j, earlier)[0]

    def up_grads(j, table, *earlier):
        return expert_grads(table, mids, [da_parts, db_parts], width // n_ctx, j, earlier)

    d_res0, low0, gain0, dl0 = back_to_rows(0, dxs[-1])
    give_down = [down_grads(j, tables[j][cut:], low0) for j in range(own)]
    y_parts = [experts_out(hid_parts[0], w_down, give_down)]
    give_up = [up_grads(j, tables[j][cut:], y_parts[0]) for j in range(own)]
    d_res1, low1, gain1, dl1 = back_to_rows(1, *[g[0] for g in give_up])
    y_parts.append(experts_out(hid_parts[1], w_down, (low1,)))
    g_mid_gain = gain0 + gain1
    d_res_parts, dl_parts = [d_res0, d_res1], [dl0, dl1]
    d_att_parts = [mm_t(dl, out_w).astype(BF16) for dl in dl_parts]
    firsts = [1 << order[0] for order in orders]
    got_down = [swap(give_down[j], firsts[j]) for j in range(own)]
    got_gate = [swap(give_up[j][0], firsts[j]) for j in range(own)]
    got_up = [swap(give_up[j][1], firsts[j]) for j in range(own)]
    g_out = expert_grads(
        jnp.zeros((1,), jnp.int32), attended_parts, [dl_parts], cols, 0, (y_parts[1],)
    )[0].reshape(n_exp, chunk, width)

    dq_parts = []
    dk_n = jnp.zeros((seq, cols), F32)
    dv = jnp.zeros((seq, cols), F32)
    dq, dk_n, dv = attend_back(base, half_seq, 0, d_att_parts[0], dk_n, dv, (y_parts[1],))
    dq_parts.append(dq)
    keep_down = [down_grads(j, tables[j][:cut], dq) for j in range(own)]
    dq, dk_n, dv = attend_back(
        base, half_seq, 1, d_att_parts[1], dk_n, dv, (*keep_down, *got_down)
    )
    dq_parts.append(dq)
    dq_n = jnp.concatenate(dq_parts, axis=0)
    inner = jnp.stack(
        [
            jnp.sum(dq_n * query_gain * qp, axis=-1),
            jnp.sum(dk_n * key_gain * kp, axis=-1),
        ],
        axis=0,
    )
    inner = ctx_sum(jnp.pad(inner, ((0, 6), (0, 0))), 1)[:2] / width
    dqp = q_scale * dq_n * query_gain - qp * (q_scale**3) * inner[0][:, None]
    dkp = k_scale * dk_n * key_gain - kp * (k_scale**3) * inner[1][:, None]
    g_query_gain = jnp.sum(dq_n * qp * q_scale, axis=0)
    g_key_gain = jnp.sum(dk_n * kp * k_scale, axis=0)
    d_qkv = jnp.concatenate([dqp.astype(BF16), dkp.astype(BF16), dv.astype(BF16)], axis=1)
    d_blocks = d_qkv.reshape(halves, n_ctx, part, 3 * cols)
    dxn = 0.0
    for d in range(n_ctx - 1, -1, -1):
        block = mm_t(take(d_blocks, c_at ^ d, 1, 1).reshape(rows, 3 * cols), qkv_w)
        dxn = dxn + (swap(block.astype(BF16), d).astype(F32) if d else block)
    block_input = tokens[0].astype(F32)
    in_scale = rms_scale(block_input)
    d_in_norm, g_attn_gain = rms_backward(block_input, in_scale, attn_gain, dxn)
    d_tokens = (jnp.concatenate(d_res_parts, axis=0) + d_in_norm).astype(BF16)

    g_qkv = expert_grads(
        jnp.arange(n_ctx, dtype=jnp.int32), [xn], [[d_qkv]], width // n_ctx, 0, got_gate
    )[0]
    keep_up = [up_grads(j, tables[j][:cut], g_qkv) for j in range(own)]
    g_down = jnp.stack([halve(keep_down[j], got_down[j], orders[j]) for j in range(own)])
    g_gate = jnp.stack([halve(keep_up[j][0], got_gate[j], orders[j]) for j in range(own)])
    g_up = jnp.stack([halve(keep_up[j][1], got_up[j], orders[j]) for j in range(own)])
    g_both = jnp.concatenate(
        [g_qkv.reshape(n_exp, shard * 3 * cols), g_out.reshape(n_exp, chunk * width)], axis=1
    )
    g_both = scatter_sum(g_both.reshape(-1, width), "exp").reshape(-1)
    g_qkv = g_both[: shard * 3 * cols].reshape(shard, 3 * cols)
    g_out = g_both[shard * 3 * cols :].reshape(chunk, width)
    mixed_parts = []
    for h in range(halves):
        y = scatter_sum(y_parts[h], "exp").astype(F32)
        mixed_parts.append((residual_parts[h] + y).astype(BF16))
    mixed = jnp.concatenate(mixed_parts, axis=0)
    g_full = [jnp.zeros((shard, width), F32) for _ in range(3)]
    for d in range(n_ctx):
        piece = (swap(g_qkv, d) if d else g_qkv).astype(F32)
        for k in range(3):
            g_full[k] = lax.dynamic_update_slice_in_dim(
                g_full[k], piece[:, k * cols : (k + 1) * cols], (c_at ^ d) * cols, 1
            )
    g_out = lax.ppermute(g_out, ("ctx", "exp"), [(b, a) for a, b in moves])
    g_out = gather(g_out, "ctx").astype(F32)

    gain_grads = [g_attn_gain[None], g_mid_gain]
    for piece in (g_query_gain, g_key_gain):
        gain_grads.append(
            lax.dynamic_update_slice_in_dim(jnp.zeros((1, width), F32), piece[None], c_at * cols, 1)
        )
    spare = -(experts + 4) % 8
    smalls = jnp.concatenate([g_router] + gain_grads + [jnp.zeros((spare, width), F32)], axis=0)
    smalls = smalls.reshape(-1, n_exp, shard).transpose(1, 0, 2)
    smalls = all_sum(smalls, 2, (g_up,))
    return (
        mixed[None], d_tokens[None],
        g_full[0], g_full[1], g_full[2], g_out,
        smalls[:experts].T,
        smalls[experts], smalls[experts + 2], smalls[experts + 3], smalls[experts + 1],
        g_gate, g_up, g_down,
    )


def solution(mesh):
    tok = P("exp", "ctx", None)
    two, three, one = P("exp", None), P("exp", None, None), P("exp")
    return jax.shard_map(
        local,
        mesh=mesh,
        in_specs=(tok, tok, one, P(), tok) + (two,) * 5 + (one,) * 4 + (three,) * 3,
        out_specs=(tok, tok) + (two,) * 5 + (one,) * 4 + (tok,) * 3,
        check_vma=False,
    )
```

time: 1460 us -> 927 us (0.63)
  waiting for transfers between devices: 801 us -> 186 us
  Pallas kernels: 0 us -> 330 us
  matrix products: 400 us -> 80.3 us
  starting transfers between devices: 5.24 us -> 63.8 us
  local copies, waits for them, and re-layouts: 58.1 us -> 114 us
  blocking collectives: 67.3 us -> 15.4 us
    reduce_scatter x10 -> x5, waiting for transfers between devices: 500 us -> 0.06 us  [scatter_sum(): lax.psum_scatter(block, axis, scatter_dimension=dimension, tiled=True)]
    pallas_call x0 -> x25, Pallas kernels: none -> 330 us  [the longest x10 119 us: expert_grads(): pl.pallas_call(functools.partial(grad_kernel, n, len(rights)), grid_spec=...]
    all_gather x8 -> x7, waiting for transfers between devices: 299 us -> 39.4 us  [gather(): return lax.all_gather(block, axis, axis=0, tiled=True)]
    ppermute x1 -> x34, waiting for transfers between devices: 0.01 us -> 147 us  [the longest x33 147 us: swap(): return lax.ppermute(block, 'ctx', [(i, i ^ bits) for i in range(n)])]
    dot_general x9 -> x2, matrix products: 97.4 us -> 3.82 us  [t_mm(): lax.dot_general(left, right, (((0,), (0,)), ((), ())), preferred_element_...]
    dot_general x9 -> x10, matrix products: 148 us -> 54.3 us  [mm_t(): lax.dot_general(left, right, (((1,), (1,)), ((), ())), preferred_element_...]
    dot_general x9, matrix products: 104 us -> 22.2 us  [mm(): return jnp.dot(left, right, preferred_element_type=F32)]
    ppermute x1 -> x34, starting transfers between devices: 0.68 us -> 60.9 us  [the longest x33 60.2 us: swap(): return lax.ppermute(block, 'ctx', [(i, i ^ bits) for i in range(n)])]
  transfers between devices with their start and end apart: 20 -> 47, of which waited for: 15 -> 16; matrix products, arithmetic and copies ran while one was open for 22% -> 29% of each run, Pallas kernels for 0% -> 35%
where the time goes in v2:
time: 927 us; the launch traced here: 919 us
  Pallas kernels  330 us (36%)
  waiting for transfers between devices  186 us (20%)
  local copies, waits for them, and re-layouts  114 us (12%)
  other arithmetic  112 us (12%)
  matrix products  80.3 us (9%)
  starting transfers between devices  63.8 us (7%)
  between operations  16.6 us (2%)
  blocking collectives  15.4 us (2%)
    ppermute x33, waiting for transfers between devices, swap(): return lax.ppermute(block, 'ctx', [(i, i ^ bits) for i in range(n)])  147 us
    pallas_call x10, Pallas kernels, expert_grads(): pl.pallas_call(functools.partial(grad_kernel, n, len(rights)), grid_spec=...  119 us
    pallas_call x2, Pallas kernels, expert_pass(): pl.pallas_call(functools.partial(expert_kernel, experts, own, 512), grid=...  98.1 us
    ppermute x33, starting transfers between devices, swap(): return lax.ppermute(block, 'ctx', [(i, i ^ bits) for i in range(n)])  60.2 us
    dot_general x10, matrix products, mm_t(): lax.dot_general(left, right, (((1,), (1,)), ((), ())), preferred_element_...  54.3 us
    all_gather x7, waiting for transfers between devices, gather(): return lax.all_gather(block, axis, axis=0, tiled=True)  39.4 us
    unnamed x163, local copies, waits for them, and re-layouts  36.8 us
    pallas_call x2, Pallas kernels, attend_back(): pl.pallas_call(attend_back_kernel, grid=(heads,), in_specs=attention_spec...  28 us
  transfers between devices with their start and end apart: 47, of which 16 were waited for; matrix products, arithmetic and copies ran while one was open for 29% of the time, Pallas kernels for 35%

profile of v2, /device:TPU:0, one launch (start us, length us, event | category | flops | bytes accessed | tf_op | source)
XLA Modules:
  0.0 919.0 jit_solution(7953581709889467710)
XLA Ops:
  22.9 22.3 %collective-permute-start = (bf16[2,128,2048]{2,1,0:T(8,128)(2,1)S(1)}, bf16[2,128,2048]{2,1,0:T(8,128)(2,1)}, u32[]{:S(2)}, u32[]{:S(2)}) collective-permute-start(bf16[2,128,2048]{2,1,0:T(8,128)(2,1)S(1)} %bitcast.205), channel_id=1, source_target_pairs={{0,8},{8,0},{16,24},{24,16},{1,9},{9,1},{17,25},{25,17},{2,10},{10... | collective-permute-start | bytes 3145736 | tf_op jit(solution)/shard_map/ppermute | solution.py:507
  54.6 15.4 %all-gather = bf16[73728]{0:T(1024)(128)(2,1)S(1)} all-gather(bf16[9216]{0:T(1024)(128)(2,1)S(1)} %constant_dynamic-update-slice_fusion.6), channel_id=2, replica_groups=mesh['ctx'=4,'exp'=8] {'exp'}, dimensions={0}, use_global_device_ids=true | all-gather | bytes 165888 | tf_op jit(solution)/shard_map/all_gather | solution.py:494
  101.6 11.9 %fusion.118.q_ref.k_ref.v_ref = f32[1024,1536]{1,0:T(8,128)} fusion(bf16[1024,2048]{1,0:T(8,128)(2,1)} %fusion.1.refs_0_, bf16[2048,1536]{1,0:T(8,128)(2,1)} %all-gather.9.cloned.1.call-done), kind=kOutput, calls=%fused_computation.310 | convolution fusion | flops 6442450944 | bytes 16777216 | tf_op jit(solution)/shard_map/dot_general | solution.py:24
  146.9 13.8 %all-gather.13.cloned.1.call-done.refs_3_ = bf16[1024,2048]{1,0:T(8,128)(2,1)} async-done(((bf16[128,2048]{1,0:T(8,128)(2,1)}), bf16[1024,2048]{1,0:T(8,128)(2,1)}) %all-gather.13.cloned.1.call-update) | async-done | bytes 4194320 | tf_op jit(solution)/shard_map/all_gather | solution.py:494
  168.9 10.2 %shard_map.294.refs_1_ = bf16[512,512]{1,0:T(8,128)(2,1)S(1)} custom-call(f32[1024,1536]{1,0:T(8,128)} %fusion.118.q_ref.k_ref.v_ref, f32[1024,1536]{1,0:T(8,128)} %fusion.118.q_ref.k_ref.v_ref, f32[1024,1536]{1,0:T(8,128)} %fusion.118.q_ref.k_ref.v_ref, f32[1024,1]{1,0:T(8,128)S(1)} %copy.73.qs_ref, f32[1024,1]{1,0:T(8,128)S(1)} %copy.74.ks_ref, ...), custom_call_target="tpu_custom_call" | custom-call | flops 1073741824 | bytes 8388608 | tf_op jit(solution)/shard_map/pallas_call | solution.py:125
  184.6 10.7 %collective-permute-done.7.refs_0_ = bf16[128,2048]{1,0:T(8,128)(2,1)S(1)} collective-permute-done((bf16[128,2048]{1,0:T(8,128)(2,1)S(1)}, bf16[128,2048]{1,0:T(8,128)(2,1)S(1)}, u32[]{:S(2)}, u32[]{:S(2)}) %collective-permute-start.7) | collective-permute-done | bytes 524320 | tf_op jit(solution)/shard_map/ppermute | solution.py:507
  195.3 10.5 %collective-permute-done.8.refs_1_ = bf16[128,2048]{1,0:T(8,128)(2,1)S(1)} collective-permute-done((bf16[128,2048]{1,0:T(8,128)(2,1)S(1)}, bf16[128,2048]{1,0:T(8,128)(2,1)S(1)}, u32[]{:S(2)}, u32[]{:S(2)}) %collective-permute-start.8) | collective-permute-done | bytes 524320 | tf_op jit(solution)/shard_map/ppermute | solution.py:507
  233.5 23.0 %all-gather.15.cloned.1.call-done.x_ref.refs_0_ = bf16[1024,2048]{1,0:T(8,128)(2,1)} async-done(((bf16[128,2048]{1,0:T(8,128)(2,1)}), bf16[1024,2048]{1,0:T(8,128)(2,1)}) %all-gather.15.cloned.1.call-update) | async-done | bytes 4194320 | tf_op jit(solution)/shard_map/all_gather | solution.py:494
  256.5 49.0 %shard_map.293 = (bf16[2,1024,1024]{2,1,0:T(8,128)(2,1)}, bf16[2,1024,1024]{2,1,0:T(8,128)(2,1)}, bf16[2,1024,1024]{2,1,0:T(8,128)(2,1)}, bf16[1024,2048]{1,0:T(8,128)(2,1)}, bf16[1024,128]{1,0:T(8,128)(2,1)}) custom-call(bf16[1024,2048]{1,0:T(8,128)(2,1)} %all-gather.15.cloned.1.call-done.x_ref.refs_0_, bf16[2,1024,1024]{2,1,0:T(8,128)(2,1)} %pad_maximum_fusion.1.dh_ref, ...), custom_call_target="tpu_custom_call" | custom-call | flops 34359738368 | bytes 41943040 | tf_op jit(solution)/shard_map/pallas_call | solution.py:230
  323.6 49.1 %shard_map.296 = (bf16[2,1024,1024]{2,1,0:T(8,128)(2,1)}, bf16[2,1024,1024]{2,1,0:T(8,128)(2,1)}, bf16[2,1024,1024]{2,1,0:T(8,128)(2,1)}, bf16[1024,2048]{1,0:T(8,128)(2,1)}, bf16[1024,128]{1,0:T(8,128)(2,1)}) custom-call(bf16[1024,2048]{1,0:T(8,128)(2,1)} %all-gather.19.cloned.1.call-done.x_ref.refs_1_, bf16[2,1024,1024]{2,1,0:T(8,128)(2,1)} %pad_maximum_fusion.2.dh_ref, ...), custom_call_target="tpu_custom_call" | custom-call | flops 34359738368 | bytes 41943040 | tf_op jit(solution)/shard_map/pallas_call | solution.py:230
  385.9 10.3 %shard_map.298.refs_0_ = bf16[512,2048]{1,0:T(8,128)(2,1)} custom-call(s32[2]{0:T(128)} %get-tuple-element.150.table, bf16[2,1024,1024]{2,1,0:T(8,128)(2,1)} %get-tuple-element.54.refs_0_.hid_ref, bf16[2,1024,1024]{2,1,0:T(8,128)(2,1)} %get-tuple-element.56.refs_1_.hid_ref, bf16[1024,2048]{1,0:T(8,128)(2,1)} %all-gather.17.cloned.1.call-done.refs_2_, ...), custom_call_target="tpu_custom_call" | custom-call | flops 4294967296 | bytes 16777216 | tf_op jit(solution)/shard_map/pallas_call | solution.py:286
  396.2 10.3 %shard_map.299.refs_1_ = bf16[512,2048]{1,0:T(8,128)(2,1)} custom-call(s32[2]{0:T(128)} %get-tuple-element.148.table, bf16[2,1024,1024]{2,1,0:T(8,128)(2,1)} %get-tuple-element.54.refs_0_.hid_ref, bf16[2,1024,1024]{2,1,0:T(8,128)(2,1)} %get-tuple-element.56.refs_1_.hid_ref, bf16[1024,2048]{1,0:T(8,128)(2,1)} %all-gather.17.cloned.1.call-done.refs_2_, ...), custom_call_target="tpu_custom_call" | custom-call | flops 4294967296 | bytes 16777216 | tf_op jit(solution)/shard_map/pallas_call | solution.py:286
  406.5 13.3 %shard_map.300.refs_6_ = bf16[1024,2048]{1,0:T(8,128)(2,1)} custom-call(bf16[2,1024,1024]{2,1,0:T(8,128)(2,1)} %get-tuple-element.54.refs_0_.hid_ref, bf16[2,1024,2048]{2,1,0:T(8,128)(2,1)} %w_ref.3, bf16[512,2048]{1,0:T(8,128)(2,1)} %shard_map.298.refs_0_, bf16[512,2048]{1,0:T(8,128)(2,1)} %shard_map.299.refs_1_), custom_call_target="tpu_custom_call" | custom-call | flops 8589934592 | bytes 16777216 | tf_op jit(solution)/shard_map/pallas_call | solution.py:317
  419.8 14.9 %shard_map.301 = (bf16[1024,1024]{1,0:T(8,128)(2,1)}, bf16[1024,1024]{1,0:T(8,128)(2,1)}) custom-call(s32[2]{0:T(128)} %get-tuple-element.150.table, bf16[1024,2048]{1,0:T(8,128)(2,1)} %all-gather.15.cloned.1.call-done.x_ref.refs_0_, bf16[1024,2048]{1,0:T(8,128)(2,1)} %all-gather.19.cloned.1.call-done.x_ref.refs_1_, ...), custom_call_target="tpu_custom_call" | custom-call | flops 8589934592 | bytes 16777216 | tf_op jit(solution)/shard_map/pallas_call | solution.py:286
  434.7 14.9 %shard_map.302 = (bf16[1024,1024]{1,0:T(8,128)(2,1)}, bf16[1024,1024]{1,0:T(8,128)(2,1)}) custom-call(s32[2]{0:T(128)} %get-tuple-element.148.table, bf16[1024,2048]{1,0:T(8,128)(2,1)} %all-gather.15.cloned.1.call-done.x_ref.refs_0_, bf16[1024,2048]{1,0:T(8,128)(2,1)} %all-gather.19.cloned.1.call-done.x_ref.refs_1_, ...), custom_call_target="tpu_custom_call" | custom-call | flops 8589934592 | bytes 16777216 | tf_op jit(solution)/shard_map/pallas_call | solution.py:286
  454.8 12.6 %shard_map.304.refs_0_.refs_4_ = bf16[1024,2048]{1,0:T(8,128)(2,1)S(1)} custom-call(bf16[2,1024,1024]{2,1,0:T(8,128)(2,1)} %get-tuple-element.56.refs_1_.hid_ref, bf16[2,1024,2048]{2,1,0:T(8,128)(2,1)} %w_ref.3, bf16[128,2048]{1,0:T(8,128)(2,1)S(1)} %get-tuple-element.71.refs_0_), custom_call_target="tpu_custom_call" | custom-call | flops 8589934592 | bytes 16777216 | tf_op jit(solution)/shard_map/pallas_call | solution.py:317
  539.8 14.3 %shard_map.305 = (f32[512,512]{1,0:T(8,128)S(1)}, f32[1024,512]{1,0:T(8,128)}, f32[1024,512]{1,0:T(8,128)}) custom-call(f32[1024,1536]{1,0:T(8,128)} %fusion.118.q_ref.k_ref.v_ref, f32[1024,1536]{1,0:T(8,128)} %fusion.118.q_ref.k_ref.v_ref, f32[1024,1536]{1,0:T(8,128)} %fusion.118.q_ref.k_ref.v_ref, f32[1024,1]{1,0:T(8,128)S(1)} %copy.73.qs_ref, ...), custom_call_target="tpu_custom_call" | custom-call | flops 2684354560 | bytes 16777216 | tf_op jit(solution)/shard_map/pallas_call | solution.py:143
  555.0 10.2 %shard_map.306.refs_0_ = bf16[512,2048]{1,0:T(8,128)(2,1)} custom-call(s32[2]{0:T(128)} %get-tuple-element.149.table, bf16[2,1024,1024]{2,1,0:T(8,128)(2,1)} %get-tuple-element.54.refs_0_.hid_ref, bf16[2,1024,1024]{2,1,0:T(8,128)(2,1)} %get-tuple-element.56.refs_1_.hid_ref, bf16[1024,2048]{1,0:T(8,128)(2,1)} %all-gather.17.cloned.1.call-done.refs_2_, ...), custom_call_target="tpu_custom_call" | custom-call | flops 4294967296 | bytes 16777216 | tf_op jit(solution)/shard_map/pallas_call | solution.py:286
  565.3 10.4 %shard_map.307.refs_1_ = bf16[512,2048]{1,0:T(8,128)(2,1)} custom-call(s32[2]{0:T(128)} %get-tuple-element.147.table, bf16[2,1024,1024]{2,1,0:T(8,128)(2,1)} %get-tuple-element.54.refs_0_.hid_ref, bf16[2,1024,1024]{2,1,0:T(8,128)(2,1)} %get-tuple-element.56.refs_1_.hid_ref, bf16[1024,2048]{1,0:T(8,128)(2,1)} %all-gather.17.cloned.1.call-done.refs_2_, ...), custom_call_target="tpu_custom_call" | custom-call | flops 4294967296 | bytes 16777216 | tf_op jit(solution)/shard_map/pallas_call | solution.py:286
  578.6 13.7 %shard_map.308 = (f32[512,512]{1,0:T(8,128)S(1)}, f32[1024,512]{1,0:T(8,128)}, f32[1024,512]{1,0:T(8,128)}) custom-call(f32[1024,1536]{1,0:T(8,128)} %fusion.118.q_ref.k_ref.v_ref, f32[1024,1536]{1,0:T(8,128)} %fusion.118.q_ref.k_ref.v_ref, f32[1024,1536]{1,0:T(8,128)} %fusion.118.q_ref.k_ref.v_ref, f32[1024,1]{1,0:T(8,128)S(1)} %copy.73.qs_ref, ...), custom_call_target="tpu_custom_call" | custom-call | flops 2684354560 | bytes 16777216 | tf_op jit(solution)/shard_map/pallas_call | solution.py:143
  598.5 12.8 %shard_map.309 = f32[8,1024]{1,0:T(8,128)} custom-call(f32[8,1024]{1,0:T(8,128)} %select_maximum_fusion.x_ref), custom_call_target="tpu_custom_call" | custom-call | tf_op jit(solution)/shard_map/pallas_call | solution.py:421
  617.9 11.6 %shard_map.310.refs_6_ = bf16[2048,1536]{1,0:T(8,128)(2,1)} custom-call(s32[4]{0:T(128)} %iota.57.table, bf16[1024,2048]{1,0:T(8,128)(2,1)} %fusion.1.refs_0_, bf16[1024,1536]{1,0:T(8,128)(2,1)} %pad_maximum_fusion.6.refs_1_, bf16[1024,1024]{1,0:T(8,128)(2,1)} %collective-permute-done.21.refs_2_, bf16[1024,1024]{1,0:T(8,128)(2,1)} %collective-permute-done.22.refs_3_), custom_call_target="tpu_custom_call" | custom-call | flops 6442450944 | bytes 16777216 | tf_op jit(solution)/shard_map/pallas_call | solution.py:286
  637.9 19.4 %pad_maximum_fusion = bf16[8,524288]{1,0:T(8,128)(2,1)} fusion(bf16[8,131072]{1,0:T(8,128)(2,1)S(1)} %copy-done.49, bf16[8,393216]{1,0:T(8,128)(2,1)} %reshape.791), kind=kLoop, calls=%fused_computation | loop fusion | flops 16777216 | bytes 16777216 | tf_op jit(solution)/shard_map/concatenate | solution.py:741
  657.2 10.5 %reshape.792 = bf16[2048,2048]{1,0:T(8,128)(2,1)} reshape(bf16[8,524288]{1,0:T(8,128)(2,1)} %pad_maximum_fusion) | data formatting | bytes 16777216 | tf_op jit(solution)/shard_map/reshape | solution.py:744
  693.8 15.3 %shard_map.313 = (bf16[1024,1024]{1,0:T(8,128)(2,1)}, bf16[1024,1024]{1,0:T(8,128)(2,1)}) custom-call(s32[2]{0:T(128)} %get-tuple-element.147.table, bf16[1024,2048]{1,0:T(8,128)(2,1)} %all-gather.15.cloned.1.call-done.x_ref.refs_0_, bf16[1024,2048]{1,0:T(8,128)(2,1)} %all-gather.19.cloned.1.call-done.x_ref.refs_1_, ...), custom_call_target="tpu_custom_call" | custom-call | flops 8589934592 | bytes 16777216 | tf_op jit(solution)/shard_map/pallas_call | solution.py:286
  709.1 14.1 %collective-permute-done.29 = bf16[1024,1024]{1,0:T(8,128)(2,1)S(1)} collective-permute-done((bf16[1024,1024]{1,0:T(8,128)(2,1)}, bf16[1024,1024]{1,0:T(8,128)(2,1)S(1)}, u32[]{:S(2)}, u32[]{:S(2)}) %collective-permute-start.29) | collective-permute-done | bytes 2097184 | tf_op jit(solution)/shard_map/ppermute | solution.py:507
  729.8 15.1 %shard_map.312 = (bf16[1024,1024]{1,0:T(8,128)(2,1)}, bf16[1024,1024]{1,0:T(8,128)(2,1)}) custom-call(s32[2]{0:T(128)} %get-tuple-element.149.table, bf16[1024,2048]{1,0:T(8,128)(2,1)} %all-gather.15.cloned.1.call-done.x_ref.refs_0_, bf16[1024,2048]{1,0:T(8,128)(2,1)} %all-gather.19.cloned.1.call-done.x_ref.refs_1_, ...), custom_call_target="tpu_custom_call" | custom-call | flops 8589934592 | bytes 16777216 | tf_op jit(solution)/shard_map/pallas_call | solution.py:286
  776.3 15.9 %collective-permute-done.30 = bf16[512,1024]{1,0:T(8,128)(2,1)} collective-permute-done((bf16[512,1024]{1,0:T(8,128)(2,1)}, bf16[512,1024]{1,0:T(8,128)(2,1)}, u32[]{:S(2)}, u32[]{:S(2)}) %collective-permute-start.30) | collective-permute-done | bytes 1048608 | tf_op jit(solution)/shard_map/ppermute | solution.py:507
  794.8 19.7 %collective-permute-done.32 = bf16[512,1024]{1,0:T(8,128)(2,1)S(1)} collective-permute-done((bf16[512,1024]{1,0:T(8,128)(2,1)S(1)}, bf16[512,1024]{1,0:T(8,128)(2,1)S(1)}, u32[]{:S(2)}, u32[]{:S(2)}) %collective-permute-start.32) | collective-permute-done | bytes 1048608 | tf_op jit(solution)/shard_map/ppermute | solution.py:507
  821.3 14.8 %shard_map.314 = f32[24,256]{1,0:T(8,128)} custom-call(f32[8,24,256]{2,1,0:T(8,128)} %bitcast.214, f32[2,512,1024]{2,1,0:T(8,128)} %pad_maximum_fusion.3.refs_0_), custom_call_target="tpu_custom_call" | custom-call | tf_op jit(solution)/shard_map/pallas_call | solution.py:479
  868.5 14.3 %collective-permute-done.23 = bf16[256,1536]{1,0:T(8,128)(2,1)} collective-permute-done((bf16[256,1536]{1,0:T(8,128)(2,1)S(1)}, bf16[256,1536]{1,0:T(8,128)(2,1)}, u32[]{:S(2)}, u32[]{:S(2)}) %collective-permute-start.23) | collective-permute-done | bytes 786464 | tf_op jit(solution)/shard_map/ppermute | solution.py:507
  884.1 16.2 %collective-permute-done.24 = bf16[256,1536]{1,0:T(8,128)(2,1)} collective-permute-done((bf16[256,1536]{1,0:T(8,128)(2,1)S(1)}, bf16[256,1536]{1,0:T(8,128)(2,1)}, u32[]{:S(2)}, u32[]{:S(2)}) %collective-permute-start.24) | collective-permute-done | bytes 786464 | tf_op jit(solution)/shard_map/ppermute | solution.py:507
  (426 shorter events, 381.9 us)
Async XLA Ops:
  7.2 94.4 %all-gather.9.cloned.1.call-start = ((), (), s32[]{:S(2)}) async-start(), calls=%async_computation.5 | async-start | bytes 7077888 | tf_op jit(solution)/shard_map/all_gather | solution.py:494
  10.6 123.1 %all-gather.11.cloned.1.call-start = ((), (), s32[]{:S(2)}) async-start(), calls=%async_computation.6 | async-start | bytes 2359296 | tf_op jit(solution)/shard_map/all_gather | solution.py:494
  13.0 147.7 %all-gather.13.cloned.1.call-start = ((), (), s32[]{:S(2)}) async-start(), calls=%async_computation.7 | async-start | bytes 4718592 | tf_op jit(solution)/shard_map/all_gather | solution.py:494
  22.4 192.8 %all-gather.17.cloned.1.call-start = ((), (), s32[]{:S(2)}) async-start(), calls=%async_computation.9 | async-start | bytes 4718592 | tf_op jit(solution)/shard_map/all_gather | solution.py:494
  22.9 55.5 %collective-permute-start = (bf16[2,128,2048]{2,1,0:T(8,128)(2,1)S(1)}, bf16[2,128,2048]{2,1,0:T(8,128)(2,1)}, u32[]{:S(2)}, u32[]{:S(2)}) collective-permute-start(bf16[2,128,2048]{2,1,0:T(8,128)(2,1)S(1)} %bitcast.205), channel_id=1, source_target_pairs={{0,8},{8,0},{16,24},{24,16},{1,9},{9,1},{17,25},{25,17},{2,10},{10... | collective-permute-start | bytes 3145736 | tf_op jit(solution)/shard_map/ppermute | solution.py:507
  45.2 45.1 %collective-permute-start.1 = (bf16[2,128,2048]{2,1,0:T(8,128)(2,1)S(1)}, bf16[2,128,2048]{2,1,0:T(8,128)(2,1)}, u32[]{:S(2)}, u32[]{:S(2)}) collective-permute-start(bf16[2,128,2048]{2,1,0:T(8,128)(2,1)S(1)} %bitcast.206), channel_id=1, source_target_pairs={{0,16},{8,24},{16,0},{24,8},{1,17},{9,25},{17,1},{25,9},{2,18},{10... | collective-permute-start | bytes 3145736 | tf_op jit(solution)/shard_map/ppermute | solution.py:507
  45.2 47.5 %collective-permute-start.2 = (bf16[2,128,2048]{2,1,0:T(8,128)(2,1)S(1)}, bf16[2,128,2048]{2,1,0:T(8,128)(2,1)}, u32[]{:S(2)}, u32[]{:S(2)}) collective-permute-start(bf16[2,128,2048]{2,1,0:T(8,128)(2,1)S(1)} %bitcast.207), channel_id=1, source_target_pairs={{0,24},{8,16},{16,8},{24,0},{1,25},{9,17},{17,9},{25,1},{2,26},{10... | collective-permute-start | bytes 3145736 | tf_op jit(solution)/shard_map/ppermute | solution.py:507
  46.7 209.8 %all-gather.15.cloned.1.call-start = ((), (), s32[]{:S(2)}) async-start(), calls=%async_computation.8 | async-start | bytes 4718592 | tf_op jit(solution)/shard_map/all_gather | solution.py:494
  168.8 136.7 %all-gather.19.cloned.1.call-start = ((), (), s32[]{:S(2)}) async-start(), calls=%async_computation.10 | async-start | bytes 4718592 | tf_op jit(solution)/shard_map/all_gather | solution.py:494
  208.1 169.6 %reduce-scatter.6.cloned.1.call-start = ((), (), s32[]{:S(2)}) async-start(), calls=%async_computation.11 | async-start | bytes 4718592 | tf_op jit(solution)/shard_map/reduce_scatter | solution.py:498
  305.6 144.0 %reduce-scatter.10.cloned.1.call-start = ((), (), s32[]{:S(2)}) async-start(), calls=%async_computation.13 | async-start | bytes 4718592 | tf_op jit(solution)/shard_map/reduce_scatter | solution.py:498
  372.8 475.2 %reduce-scatter.12.cloned.1.call-start = ((), (), s32[]{:S(2)}) async-start(), calls=%async_computation.14 | async-start | bytes 4718592 | tf_op jit(solution)/shard_map/reduce_scatter | solution.py:498
  475.2 45.3 %collective-permute-start.11 = (bf16[128,2048]{1,0:T(8,128)(2,1)S(1)}, bf16[128,2048]{1,0:T(8,128)(2,1)}, u32[]{:S(2)}, u32[]{:S(2)}) collective-permute-start(bf16[128,2048]{1,0:T(8,128)(2,1)S(1)} %copy-done.9), channel_id=1, source_target_pairs={{0,16},{8,24},{16,0},{24,8},{1,17},{9,25},{17,1},{25,9},{2,18},{10... | collective-permute-start | bytes 1572872 | tf_op jit(solution)/shard_map/ppermute | solution.py:507
  476.7 372.5 %reduce-scatter.14.cloned.1.call-start = ((), (), s32[]{:S(2)}) async-start(), calls=%async_computation.15 | async-start | bytes 9437184 | tf_op jit(solution)/shard_map/reduce_scatter | solution.py:498
  498.1 80.5 %collective-permute-start.16 = (bf16[512,2048]{1,0:T(8,128)(2,1)}, bf16[512,2048]{1,0:T(8,128)(2,1)}, u32[]{:S(2)}, u32[]{:S(2)}) collective-permute-start(bf16[512,2048]{1,0:T(8,128)(2,1)} %shard_map.298.refs_0_), channel_id=1, source_target_pairs={{0,8},{8,0},{16,24},{24,16},{1,9},{9,1},{17,25},{25,17},{2,10},{10... | collective-permute-start | bytes 6291464 | tf_op jit(solution)/shard_map/ppermute | solution.py:507
  499.2 79.4 %collective-permute-start.17 = (bf16[512,2048]{1,0:T(8,128)(2,1)}, bf16[512,2048]{1,0:T(8,128)(2,1)}, u32[]{:S(2)}, u32[]{:S(2)}) collective-permute-start(bf16[512,2048]{1,0:T(8,128)(2,1)} %shard_map.299.refs_1_), channel_id=1, source_target_pairs={{0,16},{8,24},{16,0},{24,8},{1,17},{9,25},{17,1},{25,9},{2,18},{10... | collective-permute-start | bytes 6291464 | tf_op jit(solution)/shard_map/ppermute | solution.py:507
  507.8 109.6 %collective-permute-start.21 = (bf16[1024,1024]{1,0:T(8,128)(2,1)}, bf16[1024,1024]{1,0:T(8,128)(2,1)}, u32[]{:S(2)}, u32[]{:S(2)}) collective-permute-start(bf16[1024,1024]{1,0:T(8,128)(2,1)} %get-tuple-element.69.refs_0_), channel_id=1, source_target_pairs={{0,8},{8,0},{16,24},{24,16},{1,9},{9,1},{17,25},{25,17},{2,10},{10... | collective-permute-start | bytes 6291464 | tf_op jit(solution)/shard_map/ppermute | solution.py:507
  520.6 96.8 %collective-permute-start.22 = (bf16[1024,1024]{1,0:T(8,128)(2,1)}, bf16[1024,1024]{1,0:T(8,128)(2,1)}, u32[]{:S(2)}, u32[]{:S(2)}) collective-permute-start(bf16[1024,1024]{1,0:T(8,128)(2,1)} %get-tuple-element.70.refs_1_), channel_id=1, source_target_pairs={{0,16},{8,24},{16,0},{24,8},{1,17},{9,25},{17,1},{25,9},{2,18},{10... | collective-permute-start | bytes 6291464 | tf_op jit(solution)/shard_map/ppermute | solution.py:507
  667.8 185.1 %reduce-scatter.8.cloned.1.call-start = ((), (), s32[]{:S(2)}) async-start(), calls=%async_computation.12 | async-start | bytes 4718592 | tf_op jit(solution)/shard_map/reduce_scatter | solution.py:498
  674.3 234.9 %all-gather.21.cloned.1.call-start = ((), (), s32[]{:S(2)}) async-start(), calls=%async_computation.16 | async-start | bytes 1310720 | tf_op jit(solution)/shard_map/all_gather | solution.py:494
  674.4 48.8 %collective-permute-start.29 = (bf16[1024,1024]{1,0:T(8,128)(2,1)}, bf16[1024,1024]{1,0:T(8,128)(2,1)S(1)}, u32[]{:S(2)}, u32[]{:S(2)}) collective-permute-start(bf16[1024,1024]{1,0:T(8,128)(2,1)} %get-tuple-element.87), channel_id=1, source_target_pairs={{0,16},{8,24},{16,0},{24,8},{1,17},{9,25},{17,1},{25,9},{2,18},{10... | collective-permute-start | bytes 6291464 | tf_op jit(solution)/shard_map/ppermute | solution.py:507
  675.8 69.1 %collective-permute-start.27 = (bf16[1024,1024]{1,0:T(8,128)(2,1)}, bf16[1024,1024]{1,0:T(8,128)(2,1)S(1)}, u32[]{:S(2)}, u32[]{:S(2)}) collective-permute-start(bf16[1024,1024]{1,0:T(8,128)(2,1)} %get-tuple-element.85), channel_id=1, source_target_pairs={{0,8},{8,0},{16,24},{24,16},{1,9},{9,1},{17,25},{25,17},{2,10},{10... | collective-permute-start | bytes 6291464 | tf_op jit(solution)/shard_map/ppermute | solution.py:507
  684.7 78.6 %collective-permute-start.20 = (bf16[256,2048]{1,0:T(8,128)(2,1)}, bf16[256,2048]{1,0:T(8,128)(2,1)}, u32[]{:S(2)}, u32[]{:S(2)}) collective-permute-start(bf16[256,2048]{1,0:T(8,128)(2,1)} %convolution_convert_fusion), channel_id=1, source_target_pairs={{0,8},{8,0},{16,24},{24,16},{1,9},{9,1},{17,25},{25,17},{2,10},{10... | collective-permute-start | bytes 3145736 | tf_op jit(solution)/shard_map/ppermute | solution.py:507
  689.5 75.0 %collective-permute-start.19 = (bf16[256,2048]{1,0:T(8,128)(2,1)}, bf16[256,2048]{1,0:T(8,128)(2,1)}, u32[]{:S(2)}, u32[]{:S(2)}) collective-permute-start(bf16[256,2048]{1,0:T(8,128)(2,1)} %convolution_convert_fusion.1), channel_id=1, source_target_pairs={{0,16},{8,24},{16,0},{24,8},{1,17},{9,25},{17,1},{25,9},{2,18},{10... | collective-permute-start | bytes 3145736 | tf_op jit(solution)/shard_map/ppermute | solution.py:507
  693.0 76.7 %collective-permute-start.18 = (bf16[256,2048]{1,0:T(8,128)(2,1)}, bf16[256,2048]{1,0:T(8,128)(2,1)}, u32[]{:S(2)}, u32[]{:S(2)}) collective-permute-start(bf16[256,2048]{1,0:T(8,128)(2,1)} %convolution_convert_fusion.2), channel_id=1, source_target_pairs={{0,24},{8,16},{16,8},{24,0},{1,25},{9,17},{17,9},{25,1},{2,26},{10... | collective-permute-start | bytes 3145736 | tf_op jit(solution)/shard_map/ppermute | solution.py:507
  728.8 63.3 %collective-permute-start.30 = (bf16[512,1024]{1,0:T(8,128)(2,1)}, bf16[512,1024]{1,0:T(8,128)(2,1)}, u32[]{:S(2)}, u32[]{:S(2)}) collective-permute-start(bf16[512,1024]{1,0:T(8,128)(2,1)} %slice.306), channel_id=1, source_target_pairs={{0,8},{8,0},{16,24},{24,16},{1,9},{9,1},{17,25},{25,17},{2,10},{10... | collective-permute-start | bytes 3145736 | tf_op jit(solution)/shard_map/ppermute | solution.py:507
  749.6 44.8 %collective-permute-start.28 = (bf16[512,1024]{1,0:T(8,128)(2,1)S(1)}, bf16[512,1024]{1,0:T(8,128)(2,1)S(1)}, u32[]{:S(2)}, u32[]{:S(2)}) collective-permute-start(bf16[512,1024]{1,0:T(8,128)(2,1)S(1)} %slice.304), channel_id=1, source_target_pairs={{0,16},{8,24},{16,0},{24,8},{1,17},{9,25},{17,1},{25,9},{2,18},{10... | collective-permute-start | bytes 3145736 | tf_op jit(solution)/shard_map/ppermute | solution.py:507
  763.4 51.1 %collective-permute-start.32 = (bf16[512,1024]{1,0:T(8,128)(2,1)S(1)}, bf16[512,1024]{1,0:T(8,128)(2,1)S(1)}, u32[]{:S(2)}, u32[]{:S(2)}) collective-permute-start(bf16[512,1024]{1,0:T(8,128)(2,1)S(1)} %slice.310), channel_id=1, source_target_pairs={{0,8},{8,0},{16,24},{24,16},{1,9},{9,1},{17,25},{25,17},{2,10},{10... | collective-permute-start | bytes 3145736 | tf_op jit(solution)/shard_map/ppermute | solution.py:507
  764.4 52.8 %collective-permute-start.31 = (bf16[512,1024]{1,0:T(8,128)(2,1)S(1)}, bf16[512,1024]{1,0:T(8,128)(2,1)S(1)}, u32[]{:S(2)}, u32[]{:S(2)}) collective-permute-start(bf16[512,1024]{1,0:T(8,128)(2,1)S(1)} %slice.308), channel_id=1, source_target_pairs={{0,16},{8,24},{16,0},{24,8},{1,17},{9,25},{17,1},{25,9},{2,18},{10... | collective-permute-start | bytes 3145736 | tf_op jit(solution)/shard_map/ppermute | solution.py:507
  769.8 69.1 %collective-permute-start.34 = (bf16[256,2048]{1,0:T(8,128)(2,1)S(1)}, bf16[256,2048]{1,0:T(8,128)(2,1)}, u32[]{:S(2)}, u32[]{:S(2)}) collective-permute-start(bf16[256,2048]{1,0:T(8,128)(2,1)S(1)} %slice.314), channel_id=1, source_target_pairs={{0,8},{8,0},{16,24},{24,16},{1,9},{9,1},{17,25},{25,17},{2,10},{10... | collective-permute-start | bytes 3145736 | tf_op jit(solution)/shard_map/ppermute | solution.py:507
  792.1 48.8 %collective-permute-start.33 = (bf16[256,2048]{1,0:T(8,128)(2,1)S(1)}, bf16[256,2048]{1,0:T(8,128)(2,1)}, u32[]{:S(2)}, u32[]{:S(2)}) collective-permute-start(bf16[256,2048]{1,0:T(8,128)(2,1)S(1)} %slice.312), channel_id=1, source_target_pairs={{0,16},{8,24},{16,0},{24,8},{1,17},{9,25},{17,1},{25,9},{2,18},{10... | collective-permute-start | bytes 3145736 | tf_op jit(solution)/shard_map/ppermute | solution.py:507
  856.7 43.6 %collective-permute-start.24 = (bf16[256,1536]{1,0:T(8,128)(2,1)S(1)}, bf16[256,1536]{1,0:T(8,128)(2,1)}, u32[]{:S(2)}, u32[]{:S(2)}) collective-permute-start(bf16[256,1536]{1,0:T(8,128)(2,1)S(1)} %reshape.793), channel_id=1, source_target_pairs={{0,16},{8,24},{16,0},{24,8},{1,17},{9,25},{17,1},{25,9},{2,18},{10... | collective-permute-start | bytes 2359304 | tf_op jit(solution)/shard_map/ppermute | solution.py:507
  (92 other events, 899.8 us)
Sparse Core Ops, SparseCore 0:
  10.7 70.5 all-gather.8
  83.5 28.2 all-gather.10
  114.0 46.6 all-gather.12
  162.7 45.8 all-gather.16
  210.6 45.8 all-gather.14
  258.6 45.8 all-gather.18
  306.8 48.7 reduce-scatter.5
  372.9 48.7 reduce-scatter.9
  476.8 46.9 reduce-scatter.11
  667.9 87.5 reduce-scatter.13
  757.8 48.3 reduce-scatter.7
  861.4 47.6 all-gather.20

commit v3 on v2

--- a/solution.py
+++ b/solution.py
@@ -252,83 +252,95 @@
     )(x, d_hid, member, router_w, pick, w_gate, w_up)
 
 
-def grad_kernel(n, count, table, *refs):
-    lefts, rights, outs = refs[:n], refs[n : n + n * count], refs[len(refs) - count :]
-    for k, out in enumerate(outs):
-        total = None
-        for h in range(n):
-            left = lefts[h]
-            left = left[0] if len(left.shape) == 3 else left[...]
-            right = rights[k * n + h]
-            right = right[0] if len(right.shape) == 3 else right[...]
-            part = t_mm(left, right)
-            total = part if total is None else total + part
-        out[...] = total.astype(BF16)
-
-
-def expert_grads(table, lefts, rights, block, j, earlier=()):
-    n = len(lefts)
-
-    def left_spec(a):
-        if a.ndim == 3:
-            return pl.BlockSpec((1, a.shape[1], block), lambda i, t: (j, 0, t[i]))
-        return pl.BlockSpec((a.shape[0], block), lambda i, t: (0, t[i]))
-
-    def right_spec(a):
-        if a.ndim == 3:
-            return pl.BlockSpec((1,) + a.shape[1:], lambda i, t: (j, 0, 0))
-        return pl.BlockSpec(a.shape, lambda i, t: (0, 0))
-
-    flat = [a for group in rights for a in group]
-    blocks = table.shape[0]
-    outs = [jax.ShapeDtypeStruct((blocks * block, g[0].shape[-1]), BF16) for g in rights]
-    depth = sum(a.shape[-2] for a in lefts)
+def weight_kernel(n, x_ref, d_ref, *refs):
+    out_ref = refs[-1]
+    width = d_ref.shape[1]
+    out_ref[:, :width] = t_mm(x_ref[...], d_ref[...]).astype(BF16)
+    total = t_mm(refs[0][...], refs[n][...])
+    for h in range(1, n):
+        total = total + t_mm(refs[h][...], refs[n + h][...])
+    out_ref[:, width:] = total.astype(BF16)
+
+
+def attention_grads(xn, d_qkv, attended, dl, cols, earlier):
+    seq, width = xn.shape
+    n = len(attended)
+
+    def by_column(a):
+        return pl.BlockSpec((a.shape[0], cols), lambda i: (0, i))
+
+    def fixed(a):
+        return pl.BlockSpec(a.shape, lambda i: (0, 0))
+
     return pl.pallas_call(
-        functools.partial(grad_kernel, n, len(rights)),
+        functools.partial(weight_kernel, n),
+        grid=(width // cols,),
+        in_specs=[by_column(xn), fixed(d_qkv)]
+        + [fixed(a) for a in attended]
+        + [by_column(a) for a in dl]
+        + [pl.BlockSpec(memory_space=pl.ANY)] * len(earlier),
+        out_specs=pl.BlockSpec((cols, 4 * cols), lambda i: (i, 0)),
+        out_shape=jax.ShapeDtypeStruct((width, 4 * cols), BF16),
+        compiler_params=pltpu.CompilerParams(vmem_limit_bytes=48 * MIB),
+        cost_estimate=pl.CostEstimate(
+            flops=8 * seq * width * cols, bytes_accessed=20 * MIB, transcendentals=0
+        ),
+    )(xn, d_qkv, *attended, *dl, *earlier)
+
+
+def partial_kernel(n, part, d_ref, w_ref, *refs):
+    out_ref = refs[-1]
+    rows, halves = n * part, d_ref.shape[0] // (n * part)
+    for h in range(halves):
+        total = mm_t(d_ref[h * rows : (h + 1) * rows, :], w_ref[...]).astype(BF16)
+        for c in range(n):
+            out_ref[0, c, h * part : (h + 1) * part, :] = total[c * part : (c + 1) * part, :]
+
+
+def input_partial(d_qkv, weights, part, earlier):
+    n = lax.axis_size("ctx")
+    seq, depth = d_qkv.shape
+    width = weights.shape[0]
+    rows = seq // n
+    return pl.pallas_call(
+        functools.partial(partial_kernel, n, part),
+        grid=(2,),
+        in_specs=[
+            pl.BlockSpec((seq, depth), lambda i: (0, 0)),
+            pl.BlockSpec((width // 2, depth), lambda i: (i, 0)),
+        ]
+        + [pl.BlockSpec(memory_space=pl.ANY)] * len(earlier),
+        out_specs=pl.BlockSpec((1, n, rows, width // 2), lambda i: (i, 0, 0, 0)),
+        out_shape=jax.ShapeDtypeStruct((2, n, rows, width // 2), BF16),
+        compiler_params=pltpu.CompilerParams(vmem_limit_bytes=48 * MIB),
+    )(d_qkv, weights, *earlier)
+
+
+def give_kernel(n, count, table, *refs):
+    for k in range(count):
+        total = t_mm(refs[0][...], refs[(k + 1) * n][0])
+        for h in range(1, n):
+            total = total + t_mm(refs[h][...], refs[(k + 1) * n + h][0])
+        refs[len(refs) - count + k][0] = total.astype(BF16)
+
+
+def given_grads(table, lefts, rights, block, j, earlier):
+    n, blocks = len(lefts), table.shape[0]
+    flat = [a for right in rights for a in right]
+    columns = flat[0].shape[2]
+    return pl.pallas_call(
+        functools.partial(give_kernel, n, len(rights)),
         grid_spec=pltpu.PrefetchScalarGridSpec(
             num_scalar_prefetch=1,
             grid=(blocks,),
-            in_specs=[left_spec(a) for a in lefts]
-            + [right_spec(a) for a in flat]
+            in_specs=[pl.BlockSpec((a.shape[0], block), lambda i, t: (0, t[i])) for a in lefts]
+            + [pl.BlockSpec((1,) + a.shape[1:], lambda i, t: (j, 0, 0)) for a in flat]
             + [pl.BlockSpec(memory_space=pl.ANY)] * len(earlier),
-            out_specs=[pl.BlockSpec((block, o.shape[1]), lambda i, t: (i, 0)) for o in outs],
+            out_specs=[pl.BlockSpec((1, block, columns), lambda i, t: (i, 0, 0))] * len(rights),
         ),
-        out_shape=outs,
-        compiler_params=pltpu.CompilerParams(vmem_limit_bytes=56 * MIB),
-        cost_estimate=pl.CostEstimate(
-            flops=sum(2 * depth * o.shape[0] * o.shape[1] for o in outs),
-            bytes_accessed=16 * MIB,
-            transcendentals=0,
-        ),
+        out_shape=[jax.ShapeDtypeStruct((blocks, block, columns), BF16)] * len(rights),
+        compiler_params=pltpu.CompilerParams(vmem_limit_bytes=48 * MIB),
     )(table, *lefts, *flat, *earlier)
-
-
-def out_kernel(own, hid_ref, w_ref, *refs):
-    total = mm(hid_ref[0], w_ref[0])
-    for j in range(1, own):
-        total = total + mm(hid_ref[j], w_ref[j])
-    refs[-1][...] = total.astype(BF16)
-
-
-def experts_out(hid, w_down, earlier=()):
-    own, rows, ff = hid.shape
-    width = w_down.shape[2]
-    tile = 512
-    return pl.pallas_call(
-        functools.partial(out_kernel, own),
-        grid=(width // tile,),
-        in_specs=[
-            pl.BlockSpec((own, rows, ff), lambda i: (0, 0, 0)),
-            pl.BlockSpec((own, ff, tile), lambda i: (0, 0, i)),
-        ]
-        + [pl.BlockSpec(memory_space=pl.ANY)] * len(earlier),
-        out_specs=pl.BlockSpec((rows, tile), lambda i: (0, i)),
-        out_shape=jax.ShapeDtypeStruct((rows, width), BF16),
-        compiler_params=pltpu.CompilerParams(vmem_limit_bytes=48 * MIB),
-        cost_estimate=pl.CostEstimate(
-            flops=2 * own * rows * ff * width, bytes_accessed=16 * MIB, transcendentals=0
-        ),
-    )(hid, w_down, *earlier)
 
 
 def mid_kernel(n, x_ref, own_ref, gain_ref, *refs):
@@ -393,7 +405,8 @@
     pl.semaphore_wait(barrier, len(peers))
 
 
-def ctx_sum_kernel(n, x_ref, out_ref, slots, send, recv):
+def ctx_sum_kernel(n, x_ref, *refs):
+    out_ref, slots, send, recv = refs[-4:]
     me = lax.axis_index("ctx")
     peers = [{"ctx": lax.rem(me + d, n)} for d in range(1, n)]
     meet(peers)
@@ -415,12 +428,12 @@
     out_ref[...] = total
 
 
-def ctx_sum(x, number):
+def ctx_sum(x, number, earlier=()):
     n = lax.axis_size("ctx")
     whole = pl.BlockSpec(memory_space=pltpu.VMEM)
     return pl.pallas_call(
         functools.partial(ctx_sum_kernel, n),
-        in_specs=[whole],
+        in_specs=[whole] + [pl.BlockSpec(memory_space=pl.ANY)] * len(earlier),
         out_specs=whole,
         out_shape=jax.ShapeDtypeStruct(x.shape, F32),
         scratch_shapes=[
@@ -429,65 +442,354 @@
             pltpu.SemaphoreType.DMA((n - 1,)),
         ],
         compiler_params=pltpu.CompilerParams(collective_id=number, has_side_effects=True),
-    )(x)
-
-
-def all_sum_kernel(n_ctx, n_exp, x_ref, *refs):
-    out_ref, first, second, sems = refs[-4:]
-    c_at, e_at = lax.axis_index("ctx"), lax.axis_index("exp")
-    across = [{"exp": lax.rem(e_at + d, n_exp)} for d in range(1, n_exp)]
-    along = [{"ctx": lax.rem(c_at + d, n_ctx)} for d in range(1, n_ctx)]
-    meet(across + along)
-    first[e_at] = x_ref[e_at]
-    copies = [
-        pltpu.make_async_remote_copy(
-            src_ref=x_ref.at[peer["exp"]], dst_ref=first.at[e_at],
-            send_sem=sems.at[0, d], recv_sem=sems.at[1, d],
-            device_id=peer, device_id_type=pl.DeviceIdType.MESH,
+    )(x, *earlier)
+
+
+class SmallSum:
+    def __init__(self, n_ctx, n_exp, x, first, second, sems):
+        self.x, self.first, self.second, self.sems = x, first, second, sems
+        self.c_at, self.e_at = lax.axis_index("ctx"), lax.axis_index("exp")
+        self.across = [{"exp": lax.rem(self.e_at + d, n_exp)} for d in range(1, n_exp)]
+        self.along = [{"ctx": lax.rem(self.c_at + d, n_ctx)} for d in range(1, n_ctx)]
+
+    def copy(self, src, dst, step, d, peer):
+        return pltpu.make_async_remote_copy(
+            src_ref=src, dst_ref=dst, send_sem=self.sems.at[2 * step, d],
+            recv_sem=self.sems.at[2 * step + 1, d], device_id=peer,
+            device_id_type=pl.DeviceIdType.MESH,
         )
-        for d, peer in enumerate(across)
+
+    def over_exp(self):
+        return [
+            self.copy(self.x.at[peer["exp"]], self.first.at[self.e_at], 0, d, peer)
+            for d, peer in enumerate(self.across)
+        ]
+
+    def over_ctx(self):
+        mine = self.second.at[self.c_at]
+        return [self.copy(mine, mine, 1, d, peer) for d, peer in enumerate(self.along)]
+
+    def begin(self):
+        for copy in self.over_exp():
+            copy.start()
+        self.first[self.e_at] = self.x[self.e_at]
+
+    def pass_on(self):
+        for copy in self.over_exp():
+            copy.wait()
+        total = self.first[0]
+        for k in range(1, self.first.shape[0]):
+            total = total + self.first[k]
+        self.second[self.c_at] = total
+        for copy in self.over_ctx():
+            copy.start()
+
+    def finish(self, out):
+        for copy in self.over_ctx():
+            copy.wait()
+        total = self.second[0]
+        for k in range(1, self.second.shape[0]):
+            total = total + self.second[k]
+        out[...] = total
+
+    @staticmethod
+    def scratch(n_ctx, shape):
+        return [
+            pltpu.VMEM(shape, F32),
+            pltpu.VMEM((n_ctx,) + shape[1:], F32),
+            pltpu.SemaphoreType.DMA((4, max(n_ctx, shape[0]) - 1)),
+        ]
+
+
+def halving_masks(order):
+    masks = [0]
+    for bit in order[::-1]:
+        masks = masks + [m | (1 << bit) for m in masks]
+    return masks
+
+
+def flip(value, mask):
+    bit = 0
+    while mask >> bit:
+        if (mask >> bit) & 1:
+            value = value + (1 << bit) * (1 - 2 * lax.rem(lax.div(value, 1 << bit), 2))
+        bit += 1
+    return value
+
+
+class Halving:
+    def __init__(self, n, me, source, blocks, got, send, recv, out, first=None):
+        self.n, self.me, self.source, self.blocks, self.got = n, me, source, blocks, got
+        self.send, self.recv, self.out = send, recv, out
+        self.first = first
+        bits = list(range(n.bit_length() - 1))
+        self.own = out.shape[0]
+        self.orders = [bits if j % 2 == 0 else bits[::-1] for j in range(self.own)]
+        self.masks = [halving_masks(order) for order in self.orders]
+        self.steps = len(bits)
+
+    def target(self, j, k):
+        return flip(self.me, self.masks[j][k])
+
+    def slot(self, s, k):
+        return self.n - (self.n >> s) + k - (self.n >> (s + 1))
+
+    def copy(self, j, s, k):
+        given = self.source is not None and s == 0
+        at = self.slot(s, k)
+        return pltpu.make_async_remote_copy(
+            src_ref=self.source.at[j, self.target(j, k)] if given else self.blocks.at[j, k - 1],
+            dst_ref=self.got.at[j, at],
+            send_sem=self.send.at[j, at],
+            recv_sem=self.recv.at[j, at],
+            device_id={"ctx": flip(self.me, 1 << self.orders[j][s])},
+            device_id_type=pl.DeviceIdType.MESH,
+        )
+
+    def going(self, s):
+        return [
+            (j, k)
+            for k in range((self.n >> s) - 1, (self.n >> (s + 1)) - 1, -1)
+            for j in range(self.own)
+        ]
+
+    def begin(self, value=None):
+        for j, k in self.going(0) if self.first is None else []:
+            if value is not None:
+                self.blocks[j, k - 1] = value(j, self.target(j, k)).astype(BF16)
+            self.copy(j, 0, k).start()
+        for k in range(self.n // 2 - 1, 0, -1):
+            for j in range(self.own):
+                at = self.target(j, k)
+                mine = self.source[j, at] if value is None else value(j, at)
+                self.blocks[j, k - 1] = mine.astype(BF16)
+
+    def rest(self, value=None):
+        for j in range(self.own):
+            self.out[j] = self.source[j, self.me].astype(F32) if value is None else value(j, self.me)
+
+    def arrived(self, j, k, steps):
+        total = None
+        for s in range(steps):
+            sent = k + (self.n >> (s + 1))
+            if s == 0 and self.first is not None:
+                part = self.first[j][k].astype(F32)
+            else:
+                self.copy(j, s, sent).wait_recv()
+                part = self.got[j, self.slot(s, sent)].astype(F32)
+            total = part if total is None else total + part
+        return total
+
+    def pass_on(self):
+        for s in range(1, self.steps):
+            for j, k in self.going(s):
+                total = self.blocks[j, k - 1].astype(F32) + self.arrived(j, k, s)
+                self.blocks[j, k - 1] = total.astype(BF16)
+                self.copy(j, s, k).start()
+
+    def finish(self):
+        for j in range(self.own):
+            self.out[j] += self.arrived(j, 0, self.steps)
+        for s in range(0 if self.first is None else 1, self.steps):
+            for j, k in self.going(s):
+                self.copy(j, s, k).wait_send()
+
+    @staticmethod
+    def scratch(own, n, rows, columns):
+        return [
+            pltpu.VMEM((own, n - 1, rows, columns), BF16),
+            pltpu.VMEM((own, n - 1, rows, columns), BF16),
+            pltpu.SemaphoreType.DMA((own, n - 1)),
+            pltpu.SemaphoreType.DMA((own, n - 1)),
+        ]
+
+
+def ctx_peers(n, me):
+    return [{"ctx": lax.rem(me + d, n)} for d in range(1, n)]
+
+
+def entry(ref, j):
+    return ref.at[j] if len(ref.shape) == 3 else ref
+
+
+def product(lefts, rights, block):
+    def value(j, at):
+        total = None
+        for left, right in zip(lefts, rights):
+            columns = pl.ds(pl.multiple_of(at * block, LANES), block)
+            part = t_mm(entry(left, j)[:, columns], entry(right, j)[...])
+            total = part if total is None else total + part
+        return total
+
+    return value
+
+
+def down_kernel(n, halves, *refs):
+    hid, grad, w_down = refs[:halves], refs[halves : 2 * halves], refs[2 * halves]
+    refs = refs[2 * halves + 1 :]
+    out, ys, scratch = refs[0], refs[1 : 1 + halves], refs[1 + halves :]
+    me = lax.axis_index("ctx")
+    meet(ctx_peers(n, me))
+    sums = Halving(n, me, None, *scratch, out)
+    value = product(hid, grad, hid[0].shape[2] // n)
+    sums.begin(value)
+    sums.rest(value)
+    width = w_down.shape[2]
+    for h in range(halves):
+        for start in range(0, width, 512):
+            cut = slice(start, start + 512)
+            total = mm(hid[h][0], w_down[0, :, cut])
+            for j in range(1, w_down.shape[0]):
+                total = total + mm(hid[h][j], w_down[j, :, cut])
+            ys[h][:, cut] = total.astype(BF16)
+    sums.pass_on()
+    sums.finish()
+
+
+def gate_kernel(n, halves, *refs):
+    mids, pres = refs[:halves], refs[halves : 2 * halves]
+    partial, out, dxn = refs[2 * halves], refs[-10], refs[-9]
+    first = refs[2 * halves + 1 : 2 * halves + 1 + out.shape[0]]
+    me = lax.axis_index("ctx")
+    meet(ctx_peers(n, me))
+    rows = Halving(n, me, partial, *refs[-8:-4], dxn)
+    rows.begin()
+    sums = Halving(n, me, None, *refs[-4:], out, first)
+    value = product(mids, pres, mids[0].shape[1] // n)
+    sums.begin(value)
+    sums.pass_on()
+    rows.pass_on()
+    sums.rest(value)
+    rows.rest()
+    rows.finish()
+    sums.finish()
+
+
+def up_kernel(n, halves, *refs):
+    mids, pres = refs[:halves], refs[halves : 2 * halves]
+    piece, x = refs[2 * halves], refs[2 * halves + 1]
+    out, *whole = refs[-16:-11]
+    small_out, slots, send, recv = refs[-11:-7]
+    me = lax.axis_index("ctx")
+    smalls = SmallSum(n, x.shape[0], x, *refs[-7:-4])
+    meet(smalls.across + smalls.along)
+    smalls.begin()
+    bits = list(range(n.bit_length() - 1))
+    half = piece.shape[0] // 2
+
+    def doubling(i, s):
+        order = bits if i == 0 else bits[::-1]
+        lines = pl.ds(i * half, half)
+        copies = []
+        for m in halving_masks(order[:s]):
+            at = flip(me, m)
+            sem = i, (1 << s) - 1 + len(copies)
+            copies.append(
+                pltpu.make_async_remote_copy(
+                    src_ref=slots.at[at, lines] if m else piece.at[lines],
+                    dst_ref=slots.at[at, lines],
+                    send_sem=send.at[sem],
+                    recv_sem=recv.at[sem],
+                    device_id={"ctx": flip(me, 1 << order[s])},
+                    device_id_type=pl.DeviceIdType.MESH,
+                )
+            )
+        return copies
+
+    first = refs[2 * halves + 2 : 2 * halves + 2 + out.shape[0]]
+    sums = Halving(n, me, None, *refs[-4:], out, first)
+    for i in range(2):
+        for copy in doubling(i, 0):
+            copy.start()
+    value = product(mids, pres, mids[0].shape[1] // n)
+    sums.begin(value)
+    sums.pass_on()
+    smalls.pass_on()
+    slots[me] = piece[...]
+    for s in range(1, len(bits)):
+        for i in range(2):
+            for copy in doubling(i, s - 1):
+                copy.wait_recv()
+            for copy in doubling(i, s):
+                copy.start()
+    sums.rest(value)
+    smalls.finish(small_out)
+    sums.finish()
+    for i in range(2):
+        for copy in doubling(i, len(bits) - 1):
+            copy.wait_recv()
+        for s in range(len(bits)):
+            for copy in doubling(i, s):
+                copy.wait_send()
+    cols = piece.shape[1] // len(whole)
+    for c in range(n):
+        for k, ref in enumerate(whole):
+            ref[:, c * cols : (c + 1) * cols] = slots[c, :, k * cols : (k + 1) * cols].astype(F32)
+
+
+VMEM = pl.BlockSpec(memory_space=pltpu.VMEM)
+ANY = pl.BlockSpec(memory_space=pl.ANY)
+
+
+def exchange(kernel, number, operands, earlier, outs, scratch):
+    n = lax.axis_size("ctx")
+    return pl.pallas_call(
+        kernel,
+        in_specs=[VMEM] * len(operands) + [ANY] * len(earlier),
+        out_specs=[VMEM] * len(outs),
+        out_shape=outs,
+        scratch_shapes=scratch,
+        compiler_params=pltpu.CompilerParams(
+            collective_id=number, has_side_effects=True, vmem_limit_bytes=60 * MIB
+        ),
+    )(*operands, *earlier)
+
+
+def down_sums(hid, grad, w_down):
+    n, halves = lax.axis_size("ctx"), len(hid)
+    own, ff, width = w_down.shape
+    outs = [jax.ShapeDtypeStruct((own, ff // n, width), F32)]
+    outs += [jax.ShapeDtypeStruct((h.shape[1], width), BF16) for h in hid]
+    return exchange(
+        functools.partial(down_kernel, n, halves), 3, [*hid, *grad, w_down], (), outs,
+        Halving.scratch(own, n, ff // n, width),
+    )
+
+
+def gate_sums(mids, pres, partial, first, earlier):
+    n, halves = lax.axis_size("ctx"), len(mids)
+    own, _, ff = pres[0].shape
+    rows = mids[0].shape[1] // n
+    shape = partial.shape
+    outs = [
+        jax.ShapeDtypeStruct((own, rows, ff), F32),
+        jax.ShapeDtypeStruct((shape[0],) + shape[2:], F32),
     ]
-    for copy in copies:
-        copy.start()
-    for copy in copies:
-        copy.wait()
-    total = first[0]
-    for k in range(1, n_exp):
-        total = total + first[k]
-    second[c_at] = total
-    copies = [
-        pltpu.make_async_remote_copy(
-            src_ref=second.at[c_at], dst_ref=second.at[c_at],
-            send_sem=sems.at[2, d], recv_sem=sems.at[3, d],
-            device_id=peer, device_id_type=pl.DeviceIdType.MESH,
-        )
-        for d, peer in enumerate(along)
-    ]
-    for copy in copies:
-        copy.start()
-    for copy in copies:
-        copy.wait()
-    total = second[0]
-    for k in range(1, n_ctx):
-        total = total + second[k]
-    out_ref[...] = total
-
-
-def all_sum(x, number, earlier):
-    n_ctx, n_exp = lax.axis_size("ctx"), lax.axis_size("exp")
-    whole = pl.BlockSpec(memory_space=pltpu.VMEM)
-    return pl.pallas_call(
-        functools.partial(all_sum_kernel, n_ctx, n_exp),
-        in_specs=[whole] + [pl.BlockSpec(memory_space=pl.ANY)] * len(earlier),
-        out_specs=whole,
-        out_shape=jax.ShapeDtypeStruct(x.shape[1:], F32),
-        scratch_shapes=[
-            pltpu.VMEM(x.shape, F32),
-            pltpu.VMEM((n_ctx,) + x.shape[1:], F32),
-            pltpu.SemaphoreType.DMA((4, max(n_ctx, n_exp) - 1)),
-        ],
-        compiler_params=pltpu.CompilerParams(collective_id=number, has_side_effects=True),
-    )(x, *earlier)
+    return exchange(
+        functools.partial(gate_kernel, n, halves), 4, [*mids, *pres, partial, *first], earlier, outs,
+        Halving.scratch(shape[0], n, *shape[2:]) + Halving.scratch(own, n, rows, ff),
+    )
+
+
+def up_sums(mids, pres, piece, smalls, first, earlier):
+    n, halves = lax.axis_size("ctx"), len(mids)
+    own, _, ff = pres[0].shape
+    rows = mids[0].shape[1] // n
+    shard, width = piece.shape
+    outs = [jax.ShapeDtypeStruct((own, rows, ff), F32)]
+    outs += [jax.ShapeDtypeStruct((shard, n * width // 4), F32) for _ in range(4)]
+    outs += [jax.ShapeDtypeStruct(smalls.shape[1:], F32)]
+    return exchange(
+        functools.partial(up_kernel, n, halves), 5, [*mids, *pres, piece, smalls, *first], earlier,
+        outs,
+        [
+            pltpu.VMEM((n,) + piece.shape, BF16),
+            pltpu.SemaphoreType.DMA((2, n - 1)),
+            pltpu.SemaphoreType.DMA((2, n - 1)),
+        ]
+        + SmallSum.scratch(n, smalls.shape)
+        + Halving.scratch(own, n, rows, ff),
+    )
 
 
 def gather(block, axis):
@@ -519,24 +821,6 @@
     for d, piece in enumerate(parts):
         out = lax.dynamic_update_slice_in_dim(out, jnp.expand_dims(piece, axis), me ^ d, axis)
     return out
-
-
-def halving_masks(order):
-    masks = [0]
-    for bit in order[::-1]:
-        masks = masks + [m | (1 << bit) for m in masks]
-    return masks
-
-
-def halve(keep, got, order):
-    bits = list(order[1:])
-    while True:
-        total = keep.astype(F32) + got.astype(F32)
-        if not bits:
-            return total
-        total = total.astype(BF16)
-        rows = total.shape[0] // 2
-        keep, got = total[:rows], swap(total[rows:], 1 << bits.pop(0))
 
 
 def local(
@@ -560,12 +844,12 @@
     part = rows // halves
     half_seq = part * n_ctx
 
-    chunk = width // (n_ctx * n_exp)
+    ratio = n_exp // n_ctx
     moves = []
-    for g in range(n_ctx * n_exp):
-        source = (g % n_ctx) * n_exp + g // n_ctx
-        moves.append((source, g))
-    out_piece = lax.ppermute(take(w_output, c_at * chunk, chunk), ("ctx", "exp"), moves)
+    for c in range(n_ctx):
+        for e in range(n_exp):
+            moves.append(((e // ratio) * n_exp + c * ratio + e % ratio, c * n_exp + e))
+    out_piece = lax.ppermute(take(w_output, c_at * cols, cols, 1), ("ctx", "exp"), moves)
 
     x_low = gather_ctx(tokens[0].reshape(halves, part, width), 1).reshape(seq, width)
     storage = jnp.arange(seq, dtype=jnp.int32)
@@ -599,11 +883,10 @@
     query_gain = take(query_gain_all, c_at * cols, cols)
     key_gain = take(key_gain_all, c_at * cols, cols)
 
-    qkv_piece = jnp.concatenate(
-        [take(w, c_at * cols, cols, 1) for w in (w_query, w_key, w_value)], axis=1
-    )
-    qkv_w = gather(qkv_piece, "exp")
-    out_w = gather(out_piece, "exp")
+    pieces = [take(w, c_at * cols, cols, 1) for w in (w_query, w_key, w_value)]
+    weights = gather(jnp.concatenate(pieces + [out_piece], axis=1), "exp")
+    qkv_w = weights[:, : 3 * cols]
+    out_w = weights[:, 3 * cols :].reshape(n_ctx, cols, cols).transpose(1, 0, 2).reshape(cols, width)
     x_all = x_low.astype(F32)
 
     grad_mine = cotangent[0].astype(F32) * valid
@@ -669,44 +952,34 @@
 
     g_router = sum(t_mm(c, m) for m, c in zip(mids, coef_parts))[:experts]
 
+    g_down, *y_parts = down_sums(hid_parts, grad_parts, w_down)
+    d_res0, low0, gain0, dl0 = back_to_rows(0, y_parts[0])
+    d_res1, low1, gain1, dl1 = back_to_rows(1, y_parts[0])
     bits = list(range(n_ctx.bit_length() - 1))
-    orders = [bits if j % 2 == 0 else bits[::-1] for j in range(own)]
-    cut = n_ctx // 2
-    tables = [c_at ^ jnp.asarray(halving_masks(order), jnp.int32) for order in orders]
-
-    def down_grads(j, table, *earlier):
-        return expert_grads(table, hid_parts, [grad_parts], ff // n_ctx, j, earlier)[0]
-
-    def up_grads(j, table, *earlier):
-        return expert_grads(table, mids, [da_parts, db_parts], width // n_ctx, j, earlier)
-
-    d_res0, low0, gain0, dl0 = back_to_rows(0, dxs[-1])
-    give_down = [down_grads(j, tables[j][cut:], low0) for j in range(own)]
-    y_parts = [experts_out(hid_parts[0], w_down, give_down)]
-    give_up = [up_grads(j, tables[j][cut:], y_parts[0]) for j in range(own)]
-    d_res1, low1, gain1, dl1 = back_to_rows(1, *[g[0] for g in give_up])
-    y_parts.append(experts_out(hid_parts[1], w_down, (low1,)))
+    gives, first_gate, first_up = [], [], []
+    for j in range(own):
+        order = bits if j % 2 == 0 else bits[::-1]
+        table = c_at ^ jnp.asarray(halving_masks(order)[n_ctx // 2 :], jnp.int32)
+        give = given_grads(
+            table, mids, [da_parts, db_parts], width // n_ctx, j, (low0, low1, *gives)
+        )
+        first_gate.append(swap(give[0], 1 << order[0]))
+        first_up.append(swap(give[1], 1 << order[0]))
+        gives.append(give[0])
     g_mid_gain = gain0 + gain1
     d_res_parts, dl_parts = [d_res0, d_res1], [dl0, dl1]
     d_att_parts = [mm_t(dl, out_w).astype(BF16) for dl in dl_parts]
-    firsts = [1 << order[0] for order in orders]
-    got_down = [swap(give_down[j], firsts[j]) for j in range(own)]
-    got_gate = [swap(give_up[j][0], firsts[j]) for j in range(own)]
-    got_up = [swap(give_up[j][1], firsts[j]) for j in range(own)]
-    g_out = expert_grads(
-        jnp.zeros((1,), jnp.int32), attended_parts, [dl_parts], cols, 0, (y_parts[1],)
-    )[0].reshape(n_exp, chunk, width)
+    y_mine = [scatter_sum(y, "exp") for y in y_parts]
+    mixed = jnp.concatenate(
+        [(r + y.astype(F32)).astype(BF16) for r, y in zip(residual_parts, y_mine)], axis=0
+    )
 
     dq_parts = []
     dk_n = jnp.zeros((seq, cols), F32)
     dv = jnp.zeros((seq, cols), F32)
-    dq, dk_n, dv = attend_back(base, half_seq, 0, d_att_parts[0], dk_n, dv, (y_parts[1],))
-    dq_parts.append(dq)
-    keep_down = [down_grads(j, tables[j][:cut], dq) for j in range(own)]
-    dq, dk_n, dv = attend_back(
-        base, half_seq, 1, d_att_parts[1], dk_n, dv, (*keep_down, *got_down)
-    )
-    dq_parts.append(dq)
+    for h in range(halves):
+        dq, dk_n, dv = attend_back(base, half_seq, h, d_att_parts[h], dk_n, dv, gives)
+        dq_parts.append(dq)
     dq_n = jnp.concatenate(dq_parts, axis=0)
     inner = jnp.stack(
         [
@@ -715,50 +988,26 @@
         ],
         axis=0,
     )
-    inner = ctx_sum(jnp.pad(inner, ((0, 6), (0, 0))), 1)[:2] / width
+    inner = ctx_sum(jnp.pad(inner, ((0, 6), (0, 0))), 1, first_gate)[:2] / width
     dqp = q_scale * dq_n * query_gain - qp * (q_scale**3) * inner[0][:, None]
     dkp = k_scale * dk_n * key_gain - kp * (k_scale**3) * inner[1][:, None]
     g_query_gain = jnp.sum(dq_n * qp * q_scale, axis=0)
     g_key_gain = jnp.sum(dk_n * kp * k_scale, axis=0)
     d_qkv = jnp.concatenate([dqp.astype(BF16), dkp.astype(BF16), dv.astype(BF16)], axis=1)
-    d_blocks = d_qkv.reshape(halves, n_ctx, part, 3 * cols)
-    dxn = 0.0
-    for d in range(n_ctx - 1, -1, -1):
-        block = mm_t(take(d_blocks, c_at ^ d, 1, 1).reshape(rows, 3 * cols), qkv_w)
-        dxn = dxn + (swap(block.astype(BF16), d).astype(F32) if d else block)
+    g_mine = attention_grads(xn, d_qkv, attended_parts, dl_parts, cols, first_up)
+    partial = input_partial(d_qkv, weights, part, ())
+    g_gate, dxn = gate_sums(
+        mids, da_parts, partial, first_gate, (g_mine,)
+    )
+    dxn = jnp.concatenate([dxn[0], dxn[1]], axis=1)
     block_input = tokens[0].astype(F32)
     in_scale = rms_scale(block_input)
     d_in_norm, g_attn_gain = rms_backward(block_input, in_scale, attn_gain, dxn)
     d_tokens = (jnp.concatenate(d_res_parts, axis=0) + d_in_norm).astype(BF16)
 
-    g_qkv = expert_grads(
-        jnp.arange(n_ctx, dtype=jnp.int32), [xn], [[d_qkv]], width // n_ctx, 0, got_gate
-    )[0]
-    keep_up = [up_grads(j, tables[j][:cut], g_qkv) for j in range(own)]
-    g_down = jnp.stack([halve(keep_down[j], got_down[j], orders[j]) for j in range(own)])
-    g_gate = jnp.stack([halve(keep_up[j][0], got_gate[j], orders[j]) for j in range(own)])
-    g_up = jnp.stack([halve(keep_up[j][1], got_up[j], orders[j]) for j in range(own)])
-    g_both = jnp.concatenate(
-        [g_qkv.reshape(n_exp, shard * 3 * cols), g_out.reshape(n_exp, chunk * width)], axis=1
-    )
-    g_both = scatter_sum(g_both.reshape(-1, width), "exp").reshape(-1)
-    g_qkv = g_both[: shard * 3 * cols].reshape(shard, 3 * cols)
-    g_out = g_both[shard * 3 * cols :].reshape(chunk, width)
-    mixed_parts = []
-    for h in range(halves):
-        y = scatter_sum(y_parts[h], "exp").astype(F32)
-        mixed_parts.append((residual_parts[h] + y).astype(BF16))
-    mixed = jnp.concatenate(mixed_parts, axis=0)
-    g_full = [jnp.zeros((shard, width), F32) for _ in range(3)]
-    for d in range(n_ctx):
-        piece = (swap(g_qkv, d) if d else g_qkv).astype(F32)
-        for k in range(3):
-            g_full[k] = lax.dynamic_update_slice_in_dim(
-                g_full[k], piece[:, k * cols : (k + 1) * cols], (c_at ^ d) * cols, 1
-            )
-    g_out = lax.ppermute(g_out, ("ctx", "exp"), [(b, a) for a, b in moves])
-    g_out = gather(g_out, "ctx").astype(F32)
-
+    g_mine = scatter_sum(g_mine, "exp")
+    g_out = lax.ppermute(g_mine[:, 3 * cols :], ("ctx", "exp"), [(b, a) for a, b in moves])
+    g_mine = jnp.concatenate([g_mine[:, : 3 * cols], g_out], axis=1)
     gain_grads = [g_attn_gain[None], g_mid_gain]
     for piece in (g_query_gain, g_key_gain):
         gain_grads.append(
@@ -767,10 +1016,10 @@
     spare = -(experts + 4) % 8
     smalls = jnp.concatenate([g_router] + gain_grads + [jnp.zeros((spare, width), F32)], axis=0)
     smalls = smalls.reshape(-1, n_exp, shard).transpose(1, 0, 2)
-    smalls = all_sum(smalls, 2, (g_up,))
+    g_up, *g_full, smalls = up_sums(mids, db_parts, g_mine, smalls, first_up, (g_gate,))
     return (
         mixed[None], d_tokens[None],
-        g_full[0], g_full[1], g_full[2], g_out,
+        *g_full,
         smalls[:experts].T,
         smalls[experts], smalls[experts + 2], smalls[experts + 3], smalls[experts + 1],
         g_gate, g_up, g_down,

time: 927 us -> 882 us (0.951)
  Pallas kernels: 330 us -> 505 us
  waiting for transfers between devices: 186 us -> 71.4 us
  other arithmetic: 112 us -> 58.5 us
  starting transfers between devices: 63.8 us -> 44.8 us
  matrix products: 80.3 us -> 62.4 us
  local copies, waits for them, and re-layouts: 114 us -> 102 us
    pallas_call x15 -> x9, Pallas kernels: 179 us -> 356 us  [the longest x3 251 us: exchange(): pl.pallas_call(kernel, in_specs=[VMEM] * len(operands) + [ANY] * len(earl...]
    ppermute x33 -> x19, waiting for transfers between devices: 147 us -> 52.2 us  [swap(): return lax.ppermute(block, 'ctx', [(i, i ^ bits) for i in range(n)])]
    convert_element_type x13 -> x3, other arithmetic: 27.5 us -> 6.37 us  [the longest x2 3.24 us: local(): (r + y.astype(F32)).astype(BF16)]
    all_gather x7 -> x5, waiting for transfers between devices: 39.4 us -> 18.9 us  [gather(): return lax.all_gather(block, axis, axis=0, tiled=True)]
    dot_general x10 -> x6, matrix products: 54.3 us -> 34.8 us  [mm_t(): lax.dot_general(left, right, (((1,), (1,)), ((), ())), preferred_element_...]
    ppermute x33 -> x19, starting transfers between devices: 60.2 us -> 42 us  [swap(): return lax.ppermute(block, 'ctx', [(i, i ^ bits) for i in range(n)])]
    concatenate x2, other arithmetic: 20.3 us -> 2.21 us  [the longest x1 1.11 us: local(): weights = gather(jnp.concatenate(pieces + [out_piece], axis=1), 'exp')]
    unnamed x163 -> x164, local copies, waits for them, and re-layouts: 36.8 us -> 52.3 us
  transfers between devices with their start and end apart: 47 -> 31, of which waited for: 16 -> 10; matrix products, arithmetic and copies ran while one was open for 29% -> 19% of each run, Pallas kernels for 35% -> 48%
where the time goes in v3:
time: 882 us; the launch traced here: 876 us
  Pallas kernels  505 us (57%)
  local copies, waits for them, and re-layouts  102 us (12%)
  waiting for transfers between devices  71.4 us (8%)
  matrix products  62.4 us (7%)
  other arithmetic  58.5 us (7%)
  starting transfers between devices  44.8 us (5%)
  between operations  16.1 us (2%)
  blocking collectives  15 us (2%)
    pallas_call x3, Pallas kernels, exchange(): pl.pallas_call(kernel, in_specs=[VMEM] * len(operands) + [ANY] * len(earl...  251 us
    pallas_call x2, Pallas kernels, expert_pass(): pl.pallas_call(functools.partial(expert_kernel, experts, own, 512), grid=...  98.1 us
    unnamed x164, local copies, waits for them, and re-layouts  52.3 us
    ppermute x19, waiting for transfers between devices, swap(): return lax.ppermute(block, 'ctx', [(i, i ^ bits) for i in range(n)])  52.2 us
    pallas_call x2, Pallas kernels, ctx_sum(): pl.pallas_call(functools.partial(ctx_sum_kernel, n), in_specs=[whole] + [...  51.7 us
    ppermute x19, starting transfers between devices, swap(): return lax.ppermute(block, 'ctx', [(i, i ^ bits) for i in range(n)])  42 us
    dot_general x6, matrix products, mm_t(): lax.dot_general(left, right, (((1,), (1,)), ((), ())), preferred_element_...  34.8 us
    pallas_call x2, Pallas kernels, given_grads(): pl.pallas_call(functools.partial(give_kernel, n, len(rights)), grid_spec=...  29.7 us
  transfers between devices with their start and end apart: 31, of which 10 were waited for; matrix products, arithmetic and copies ran while one was open for 19% of the time, Pallas kernels for 48%

profile of v3, /device:TPU:0, one launch (start us, length us, event | category | flops | bytes accessed | tf_op | source)
XLA Modules:
  0.0 875.6 jit_solution(936281177912114755)
XLA Ops:
  13.8 4.5 compare_select_fusion.11
  22.2 22.3 %collective-permute-start = (bf16[2,128,2048]{2,1,0:T(8,128)(2,1)S(1)}, bf16[2,128,2048]{2,1,0:T(8,128)(2,1)}, u32[]{:S(2)}, u32[]{:S(2)}) collective-permute-start(bf16[2,128,2048]{2,1,0:T(8,128)(2,1)S(1)} %bitcast.209), channel_id=1, source_target_pairs={{0,8},{8,0},{16,24},{24,16},{1,9},{9,1},{17,25},{25,17},{2,10},{10... | collective-permute-start | bytes 3145736 | tf_op jit(solution)/shard_map/ppermute | solution.py:809
  46.0 5.3 select_reduce_fusion
  53.8 15.0 %all-gather = bf16[73728]{0:T(1024)(128)(2,1)S(1)} all-gather(bf16[9216]{0:T(1024)(128)(2,1)S(1)} %constant_dynamic-update-slice_fusion.6), channel_id=2, replica_groups=mesh['ctx'=4,'exp'=8] {'exp'}, dimensions={0}, use_global_device_ids=true | all-gather | bytes 165888 | tf_op jit(solution)/shard_map/all_gather | solution.py:796
  79.1 11.8 %collective-permute-done.1 = bf16[2,128,2048]{2,1,0:T(8,128)(2,1)} collective-permute-done((bf16[2,128,2048]{2,1,0:T(8,128)(2,1)S(1)}, bf16[2,128,2048]{2,1,0:T(8,128)(2,1)}, u32[]{:S(2)}, u32[]{:S(2)}) %collective-permute-start.1) | collective-permute-done | bytes 1048608 | tf_op jit(solution)/shard_map/ppermute | solution.py:809
  102.0 14.7 %all-gather.7.cloned.1.call-done.w_ref = bf16[2048,2048]{1,0:T(8,128)(2,1)} async-done(((bf16[256,2048]{1,0:T(8,128)(2,1)}), bf16[2048,2048]{1,0:T(8,128)(2,1)}) %all-gather.7.cloned.1.call-update) | async-done | bytes 8388624 | tf_op jit(solution)/shard_map/all_gather | solution.py:796
  116.7 11.7 %fusion.2.q_ref.k_ref.v_ref = f32[1024,1536]{1,0:T(8,128)} fusion(bf16[1024,2048]{1,0:T(8,128)(2,1)} %fusion.1.x_ref, bf16[2048,2048]{1,0:T(8,128)(2,1)} %all-gather.7.cloned.1.call-done.w_ref), kind=kOutput, calls=%fused_computation.4 | convolution fusion | flops 6442450944 | bytes 16777216 | tf_op jit(solution)/shard_map/dot_general | solution.py:24
  131.6 6.7 shard_map.290
  142.6 4.1 copy.77
  146.8 9.9 %shard_map.291.refs_0_ = bf16[512,512]{1,0:T(8,128)(2,1)S(1)} custom-call(f32[1024,1536]{1,0:T(8,128)} %fusion.2.q_ref.k_ref.v_ref, f32[1024,1536]{1,0:T(8,128)} %fusion.2.q_ref.k_ref.v_ref, f32[1024,1536]{1,0:T(8,128)} %fusion.2.q_ref.k_ref.v_ref, f32[1024,1]{1,0:T(8,128)S(1)} %copy.75.qs_ref, f32[1024,1]{1,0:T(8,128)S(1)} %copy.76.ks_ref, ...), custom_call_target="tpu_custom_call" | custom-call | flops 1073741824 | bytes 8388608 | tf_op jit(solution)/shard_map/pallas_call | solution.py:125
  169.4 4.1 collective-permute-done.6.refs_2_
  173.5 12.6 %collective-permute-done.5.refs_1_ = bf16[128,2048]{1,0:T(8,128)(2,1)} collective-permute-done((bf16[128,2048]{1,0:T(8,128)(2,1)}, bf16[128,2048]{1,0:T(8,128)(2,1)}, u32[]{:S(2)}, u32[]{:S(2)}) %collective-permute-start.5) | collective-permute-done | bytes 524320 | tf_op jit(solution)/shard_map/ppermute | solution.py:809
  194.3 9.7 %shard_map.294.refs_1_ = bf16[512,512]{1,0:T(8,128)(2,1)S(1)} custom-call(f32[1024,1536]{1,0:T(8,128)} %fusion.2.q_ref.k_ref.v_ref, f32[1024,1536]{1,0:T(8,128)} %fusion.2.q_ref.k_ref.v_ref, f32[1024,1536]{1,0:T(8,128)} %fusion.2.q_ref.k_ref.v_ref, f32[1024,1]{1,0:T(8,128)S(1)} %copy.75.qs_ref, f32[1024,1]{1,0:T(8,128)S(1)} %copy.76.ks_ref, ...), custom_call_target="tpu_custom_call" | custom-call | flops 1073741824 | bytes 8388608 | tf_op jit(solution)/shard_map/pallas_call | solution.py:125
  210.9 10.6 %collective-permute-done.9.refs_2_ = bf16[128,2048]{1,0:T(8,128)(2,1)S(1)} collective-permute-done((bf16[128,2048]{1,0:T(8,128)(2,1)S(1)}, bf16[128,2048]{1,0:T(8,128)(2,1)S(1)}, u32[]{:S(2)}, u32[]{:S(2)}) %collective-permute-start.9) | collective-permute-done | bytes 524320 | tf_op jit(solution)/shard_map/ppermute | solution.py:809
  221.4 8.1 collective-permute-done.8.refs_1_
  238.5 8.2 convert_bitcast_fusion.3
  246.7 7.4 convert_bitcast_fusion.4
  256.5 4.2 all-gather.11.cloned.1.call-done.x_ref.refs_0_
  260.7 49.0 %shard_map.293 = (bf16[2,1024,1024]{2,1,0:T(8,128)(2,1)}, bf16[2,1024,1024]{2,1,0:T(8,128)(2,1)}, bf16[2,1024,1024]{2,1,0:T(8,128)(2,1)}, bf16[1024,2048]{1,0:T(8,128)(2,1)}, bf16[1024,128]{1,0:T(8,128)(2,1)}) custom-call(bf16[1024,2048]{1,0:T(8,128)(2,1)} %all-gather.11.cloned.1.call-done.x_ref.refs_0_, bf16[2,1024,1024]{2,1,0:T(8,128)(2,1)} %pad_maximum_fusion.dh_ref, ...), custom_call_target="tpu_custom_call" | custom-call | flops 34359738368 | bytes 41943040 | tf_op jit(solution)/shard_map/pallas_call | solution.py:230
  310.0 8.1 convert_bitcast_fusion.1
  318.1 7.0 convert_bitcast_fusion.2
  327.5 49.1 %shard_map.296 = (bf16[2,1024,1024]{2,1,0:T(8,128)(2,1)}, bf16[2,1024,1024]{2,1,0:T(8,128)(2,1)}, bf16[2,1024,1024]{2,1,0:T(8,128)(2,1)}, bf16[1024,2048]{1,0:T(8,128)(2,1)}, bf16[1024,128]{1,0:T(8,128)(2,1)}) custom-call(bf16[1024,2048]{1,0:T(8,128)(2,1)} %all-gather.15.cloned.1.call-done.x_ref.refs_1_, bf16[2,1024,1024]{2,1,0:T(8,128)(2,1)} %pad_maximum_fusion.1.dh_ref, ...), custom_call_target="tpu_custom_call" | custom-call | flops 34359738368 | bytes 41943040 | tf_op jit(solution)/shard_map/pallas_call | solution.py:230
  377.0 90.4 %shard_map.297 = (f32[2,256,2048]{2,1,0:T(8,128)}, bf16[1024,2048]{1,0:T(8,128)(2,1)}, bf16[1024,2048]{1,0:T(8,128)(2,1)}) custom-call(bf16[2,1024,1024]{2,1,0:T(8,128)(2,1)} %get-tuple-element.61.refs_0_, bf16[2,1024,1024]{2,1,0:T(8,128)(2,1)} %get-tuple-element.63.refs_1_, bf16[1024,2048]{1,0:T(8,128)(2,1)} %all-gather.13.cloned.1.call-done.refs_2_, ...), custom_call_target="tpu_custom_call" | custom-call | tf_op jit(solution)/shard_map/pallas_call | solution.py:736
  494.2 14.9 %shard_map.300 = (bf16[2,512,1024]{2,1,0:T(8,128)(2,1)S(1)}, bf16[2,512,1024]{2,1,0:T(8,128)(2,1)}) custom-call(s32[2]{0:T(128)S(1)} %get-tuple-element.160.table, bf16[1024,2048]{1,0:T(8,128)(2,1)} %all-gather.11.cloned.1.call-done.x_ref.refs_0_, bf16[1024,2048]{1,0:T(8,128)(2,1)} %all-gather.15.cloned.1.call-done.x_ref.refs_1_, ...), custom_call_target="tpu_custom_call" | custom-call | tf_op jit(solution)/shard_map/pallas_call | solution.py:331
  510.4 14.9 %shard_map.301 = (bf16[2,512,1024]{2,1,0:T(8,128)(2,1)S(1)}, bf16[2,512,1024]{2,1,0:T(8,128)(2,1)}) custom-call(s32[2]{0:T(128)S(1)} %get-tuple-element.159.table, bf16[1024,2048]{1,0:T(8,128)(2,1)} %all-gather.11.cloned.1.call-done.x_ref.refs_0_, bf16[1024,2048]{1,0:T(8,128)(2,1)} %all-gather.15.cloned.1.call-done.x_ref.refs_1_, ...), custom_call_target="tpu_custom_call" | custom-call | tf_op jit(solution)/shard_map/pallas_call | solution.py:331
  542.1 13.8 %shard_map.302 = (f32[512,512]{1,0:T(8,128)S(1)}, f32[1024,512]{1,0:T(8,128)}, f32[1024,512]{1,0:T(8,128)}) custom-call(f32[1024,1536]{1,0:T(8,128)} %fusion.2.q_ref.k_ref.v_ref, f32[1024,1536]{1,0:T(8,128)} %fusion.2.q_ref.k_ref.v_ref, f32[1024,1536]{1,0:T(8,128)} %fusion.2.q_ref.k_ref.v_ref, f32[1024,1]{1,0:T(8,128)S(1)} %copy.75.qs_ref, ...), custom_call_target="tpu_custom_call" | custom-call | flops 2684354560 | bytes 16777216 | tf_op jit(solution)/shard_map/pallas_call | solution.py:143
  558.3 14.1 %shard_map.303 = (f32[512,512]{1,0:T(8,128)S(1)}, f32[1024,512]{1,0:T(8,128)}, f32[1024,512]{1,0:T(8,128)}) custom-call(f32[1024,1536]{1,0:T(8,128)} %fusion.2.q_ref.k_ref.v_ref, f32[1024,1536]{1,0:T(8,128)} %fusion.2.q_ref.k_ref.v_ref, f32[1024,1536]{1,0:T(8,128)} %fusion.2.q_ref.k_ref.v_ref, f32[1024,1]{1,0:T(8,128)S(1)} %copy.75.qs_ref, ...), custom_call_target="tpu_custom_call" | custom-call | flops 2684354560 | bytes 16777216 | tf_op jit(solution)/shard_map/pallas_call | solution.py:143
  585.3 45.1 %shard_map.304 = f32[8,1024]{1,0:T(8,128)} custom-call(f32[8,1024]{1,0:T(8,128)} %select_maximum_fusion.x_ref, bf16[2,512,1024]{2,1,0:T(8,128)(2,1)} %collective-permute-done.16.refs_0_.refs_5_, bf16[2,512,1024]{2,1,0:T(8,128)(2,1)} %copy-done.45), custom_call_target="tpu_custom_call" | custom-call | tf_op jit(solution)/shard_map/pallas_call | solution.py:434
  637.6 13.4 %shard_map.306.refs_7_ = bf16[2048,2048]{1,0:T(8,128)(2,1)} custom-call(bf16[1024,2048]{1,0:T(8,128)(2,1)} %fusion.1.x_ref, bf16[1024,1536]{1,0:T(8,128)(2,1)} %pad_maximum_fusion.2.d_ref, bf16[512,512]{1,0:T(8,128)(2,1)S(1)} %copy-done.24, bf16[512,512]{1,0:T(8,128)(2,1)S(1)} %copy-done.26, bf16[512,2048]{1,0:T(8,128)(2,1)} %bitcast.53.refs_2_, ...), custom_call_target="tpu_custom_call" | custom-call | flops 8589934592 | bytes 20971520 | tf_op jit(solution)/shard_map/pallas_call | solution.py:275
  662.3 10.3 %shard_map.305.refs_4_ = bf16[2,4,256,1024]{3,2,1,0:T(8,128)(2,1)} custom-call(bf16[1024,1536]{1,0:T(8,128)(2,1)S(1)} %copy-done.9, bf16[2048,2048]{1,0:T(8,128)(2,1)} %all-gather.7.cloned.1.call-done.w_ref), custom_call_target="tpu_custom_call" | custom-call | tf_op jit(solution)/shard_map/pallas_call | solution.py:305
  672.6 71.6 %shard_map.307 = (f32[2,512,1024]{2,1,0:T(8,128)}, f32[2,256,1024]{2,1,0:T(8,128)}) custom-call(bf16[1024,2048]{1,0:T(8,128)(2,1)} %all-gather.11.cloned.1.call-done.x_ref.refs_0_, bf16[1024,2048]{1,0:T(8,128)(2,1)} %all-gather.15.cloned.1.call-done.x_ref.refs_1_, bf16[2,1024,1024]{2,1,0:T(8,128)(2,1)} %get-tuple-element.75.refs_2_, ...), custom_call_target="tpu_custom_call" | custom-call | tf_op jit(solution)/shard_map/pallas_call | solution.py:736
  756.6 88.8 %shard_map.308 = (f32[2,512,1024]{2,1,0:T(8,128)}, f32[256,2048]{1,0:T(8,128)}, f32[256,2048]{1,0:T(8,128)}, f32[256,2048]{1,0:T(8,128)}, f32[256,2048]{1,0:T(8,128)}, /*index=5*/f32[24,256]{1,0:T(8,128)}) custom-call(bf16[1024,2048]{1,0:T(8,128)(2,1)} %all-gather.11.cloned.1.call-done.x_ref.refs_0_, ...), custom_call_target="tpu_custom_call" | custom-call | tf_op jit(solution)/shard_map/pallas_call | solution.py:736
  (342 shorter events, 198.4 us)
Async XLA Ops:
  7.2 109.5 %all-gather.7.cloned.1.call-start = ((), (), s32[]{:S(2)}) async-start(), calls=%async_computation.5 | async-start | bytes 9437184 | tf_op jit(solution)/shard_map/all_gather | solution.py:796
  8.4 2.9 collective-permute-start.3
  12.4 157.0 %all-gather.9.cloned.1.call-start = ((), (), s32[]{:S(2)}) async-start(), calls=%async_computation.6 | async-start | bytes 4718592 | tf_op jit(solution)/shard_map/all_gather | solution.py:796
  20.6 32.9 %copy-start.70 = (bf16[256]{0:T(256)(128)(2,1)S(1)}, bf16[256]{0:T(256)(128)(2,1)}, u32[]{:S(2)}) copy-start(bf16[256]{0:T(256)(128)(2,1)} %param.32) | copy-start | bytes 1540
  21.7 216.8 %all-gather.13.cloned.1.call-start = ((), (), s32[]{:S(2)}) async-start(), calls=%async_computation.8 | async-start | bytes 4718592 | tf_op jit(solution)/shard_map/all_gather | solution.py:796
  22.2 54.6 %collective-permute-start = (bf16[2,128,2048]{2,1,0:T(8,128)(2,1)S(1)}, bf16[2,128,2048]{2,1,0:T(8,128)(2,1)}, u32[]{:S(2)}, u32[]{:S(2)}) collective-permute-start(bf16[2,128,2048]{2,1,0:T(8,128)(2,1)S(1)} %bitcast.209), channel_id=1, source_target_pairs={{0,8},{8,0},{16,24},{24,16},{1,9},{9,1},{17,25},{25,17},{2,10},{10... | collective-permute-start | bytes 3145736 | tf_op jit(solution)/shard_map/ppermute | solution.py:809
  44.4 46.4 %collective-permute-start.1 = (bf16[2,128,2048]{2,1,0:T(8,128)(2,1)S(1)}, bf16[2,128,2048]{2,1,0:T(8,128)(2,1)}, u32[]{:S(2)}, u32[]{:S(2)}) collective-permute-start(bf16[2,128,2048]{2,1,0:T(8,128)(2,1)S(1)} %bitcast.210), channel_id=1, source_target_pairs={{0,16},{8,24},{16,0},{24,8},{1,17},{9,25},{17,1},{25,9},{2,18},{10... | collective-permute-start | bytes 3145736 | tf_op jit(solution)/shard_map/ppermute | solution.py:809
  44.4 48.7 %collective-permute-start.2 = (bf16[2,128,2048]{2,1,0:T(8,128)(2,1)S(1)}, bf16[2,128,2048]{2,1,0:T(8,128)(2,1)}, u32[]{:S(2)}, u32[]{:S(2)}) collective-permute-start(bf16[2,128,2048]{2,1,0:T(8,128)(2,1)S(1)} %bitcast.211), channel_id=1, source_target_pairs={{0,24},{8,16},{16,8},{24,0},{1,25},{9,17},{17,9},{25,1},{2,26},{10... | collective-permute-start | bytes 3145736 | tf_op jit(solution)/shard_map/ppermute | solution.py:809
  45.9 214.8 %all-gather.11.cloned.1.call-start = ((), (), s32[]{:S(2)}) async-start(), calls=%async_computation.7 | async-start | bytes 4718592 | tf_op jit(solution)/shard_map/all_gather | solution.py:796
  158.3 15.1 %collective-permute-start.6 = (bf16[128,2048]{1,0:T(8,128)(2,1)}, bf16[128,2048]{1,0:T(8,128)(2,1)}, u32[]{:S(2)}, u32[]{:S(2)}) collective-permute-start(bf16[128,2048]{1,0:T(8,128)(2,1)} %convolution_convert_fusion.3), channel_id=1, source_target_pairs={{0,8},{8,0},{16,24},{24,16},{1,9},{9,1},{17,25},{25,17},{2,10},{10... | collective-permute-start | bytes 1572872 | tf_op jit(solution)/shard_map/ppermute | solution.py:809
  161.4 24.7 %collective-permute-start.5 = (bf16[128,2048]{1,0:T(8,128)(2,1)}, bf16[128,2048]{1,0:T(8,128)(2,1)}, u32[]{:S(2)}, u32[]{:S(2)}) collective-permute-start(bf16[128,2048]{1,0:T(8,128)(2,1)} %convolution_convert_fusion.4), channel_id=1, source_target_pairs={{0,16},{8,24},{16,0},{24,8},{1,17},{9,25},{17,1},{25,9},{2,18},{10... | collective-permute-start | bytes 1572872 | tf_op jit(solution)/shard_map/ppermute | solution.py:809
  164.5 21.6 %collective-permute-start.4 = (bf16[128,2048]{1,0:T(8,128)(2,1)}, bf16[128,2048]{1,0:T(8,128)(2,1)}, u32[]{:S(2)}, u32[]{:S(2)}) collective-permute-start(bf16[128,2048]{1,0:T(8,128)(2,1)} %convolution_convert_fusion.5), channel_id=1, source_target_pairs={{0,24},{8,16},{16,8},{24,0},{1,25},{9,17},{17,9},{25,1},{2,26},{10... | collective-permute-start | bytes 1572872 | tf_op jit(solution)/shard_map/ppermute | solution.py:809
  194.3 115.4 %all-gather.15.cloned.1.call-start = ((), (), s32[]{:S(2)}) async-start(), calls=%async_computation.9 | async-start | bytes 4718592 | tf_op jit(solution)/shard_map/all_gather | solution.py:796
  206.5 14.9 %collective-permute-start.9 = (bf16[128,2048]{1,0:T(8,128)(2,1)S(1)}, bf16[128,2048]{1,0:T(8,128)(2,1)S(1)}, u32[]{:S(2)}, u32[]{:S(2)}) collective-permute-start(bf16[128,2048]{1,0:T(8,128)(2,1)S(1)} %convolution_convert_fusion), channel_id=1, source_target_pairs={{0,8},{8,0},{16,24},{24,16},{1,9},{9,1},{17,25},{25,17},{2,10},{10... | collective-permute-start | bytes 1572872 | tf_op jit(solution)/shard_map/ppermute | solution.py:809
  207.2 22.3 %collective-permute-start.8 = (bf16[128,2048]{1,0:T(8,128)(2,1)S(1)}, bf16[128,2048]{1,0:T(8,128)(2,1)S(1)}, u32[]{:S(2)}, u32[]{:S(2)}) collective-permute-start(bf16[128,2048]{1,0:T(8,128)(2,1)S(1)} %convolution_convert_fusion.1), channel_id=1, source_target_pairs={{0,16},{8,24},{16,0},{24,8},{1,17},{9,25},{17,1},{25,9},{2,18},{10... | collective-permute-start | bytes 1572872 | tf_op jit(solution)/shard_map/ppermute | solution.py:809
  208.8 22.1 %collective-permute-start.7 = (bf16[128,2048]{1,0:T(8,128)(2,1)S(1)}, bf16[128,2048]{1,0:T(8,128)(2,1)S(1)}, u32[]{:S(2)}, u32[]{:S(2)}) collective-permute-start(bf16[128,2048]{1,0:T(8,128)(2,1)S(1)} %convolution_convert_fusion.2), channel_id=1, source_target_pairs={{0,24},{8,16},{16,8},{24,0},{1,25},{9,17},{17,9},{25,1},{2,26},{10... | collective-permute-start | bytes 1572872 | tf_op jit(solution)/shard_map/ppermute | solution.py:809
  233.3 238.6 %reduce-scatter.10.cloned.1.call-start = ((), (), s32[]{:S(2)}) async-start(), calls=%async_computation.12 | async-start | bytes 4718592 | tf_op jit(solution)/shard_map/reduce_scatter | solution.py:800
  309.8 173.0 %reduce-scatter.12.cloned.1.call-start = ((), (), s32[]{:S(2)}) async-start(), calls=%async_computation.13 | async-start | bytes 4718592 | tf_op jit(solution)/shard_map/reduce_scatter | solution.py:800
  376.6 281.0 %reduce-scatter.6.cloned.1.call-start = ((), (), s32[]{:S(2)}) async-start(), calls=%async_computation.10 | async-start | bytes 4718592 | tf_op jit(solution)/shard_map/reduce_scatter | solution.py:800
  467.5 192.4 %reduce-scatter.8.cloned.1.call-start = ((), (), s32[]{:S(2)}) async-start(), calls=%async_computation.11 | async-start | bytes 4718592 | tf_op jit(solution)/shard_map/reduce_scatter | solution.py:800
  471.2 278.2 %reduce-scatter.14.cloned.1.call-start = ((), (), s32[]{:S(2)}) async-start(), calls=%async_computation.14 | async-start | bytes 9437184 | tf_op jit(solution)/shard_map/reduce_scatter | solution.py:800
  479.3 46.0 %collective-permute-start.10 = (bf16[128,2048]{1,0:T(8,128)(2,1)S(1)}, bf16[128,2048]{1,0:T(8,128)(2,1)}, u32[]{:S(2)}, u32[]{:S(2)}) collective-permute-start(bf16[128,2048]{1,0:T(8,128)(2,1)S(1)} %get-tuple-element.77.refs_6_), channel_id=1, source_target_pairs={{0,8},{8,0},{16,24},{24,16},{1,9},{9,1},{17,25},{25,17},{2,10},{10... | collective-permute-start | bytes 1572872 | tf_op jit(solution)/shard_map/ppermute | solution.py:809
  480.0 48.5 %collective-permute-start.11 = (bf16[128,2048]{1,0:T(8,128)(2,1)S(1)}, bf16[128,2048]{1,0:T(8,128)(2,1)}, u32[]{:S(2)}, u32[]{:S(2)}) collective-permute-start(bf16[128,2048]{1,0:T(8,128)(2,1)S(1)} %get-tuple-element.77.refs_6_), channel_id=1, source_target_pairs={{0,16},{8,24},{16,0},{24,8},{1,17},{9,25},{17,1},{25,9},{2,18},{10... | collective-permute-start | bytes 1572872 | tf_op jit(solution)/shard_map/ppermute | solution.py:809
  481.4 49.7 %collective-permute-start.12 = (bf16[128,2048]{1,0:T(8,128)(2,1)S(1)}, bf16[128,2048]{1,0:T(8,128)(2,1)}, u32[]{:S(2)}, u32[]{:S(2)}) collective-permute-start(bf16[128,2048]{1,0:T(8,128)(2,1)S(1)} %get-tuple-element.77.refs_6_), channel_id=1, source_target_pairs={{0,24},{8,16},{16,8},{24,0},{1,25},{9,17},{17,9},{25,1},{2,26},{10... | collective-permute-start | bytes 1572872 | tf_op jit(solution)/shard_map/ppermute | solution.py:809
  489.2 45.3 %collective-permute-start.13 = (bf16[128,2048]{1,0:T(8,128)(2,1)S(1)}, bf16[128,2048]{1,0:T(8,128)(2,1)}, u32[]{:S(2)}, u32[]{:S(2)}) collective-permute-start(bf16[128,2048]{1,0:T(8,128)(2,1)S(1)} %get-tuple-element.80.refs_7_), channel_id=1, source_target_pairs={{0,8},{8,0},{16,24},{24,16},{1,9},{9,1},{17,25},{25,17},{2,10},{10... | collective-permute-start | bytes 1572872 | tf_op jit(solution)/shard_map/ppermute | solution.py:809
  490.0 46.2 %collective-permute-start.14 = (bf16[128,2048]{1,0:T(8,128)(2,1)S(1)}, bf16[128,2048]{1,0:T(8,128)(2,1)S(1)}, u32[]{:S(2)}, u32[]{:S(2)}) collective-permute-start(bf16[128,2048]{1,0:T(8,128)(2,1)S(1)} %get-tuple-element.80.refs_7_), channel_id=1, source_target_pairs={{0,16},{8,24},{16,0},{24,8},{1,17},{9,25},{17,1},{25,9},{2,18},{10... | collective-permute-start | bytes 1572872 | tf_op jit(solution)/shard_map/ppermute | solution.py:809
  525.3 30.6 %collective-permute-start.15 = (bf16[128,2048]{1,0:T(8,128)(2,1)S(1)}, bf16[128,2048]{1,0:T(8,128)(2,1)}, u32[]{:S(2)}, u32[]{:S(2)}) collective-permute-start(bf16[128,2048]{1,0:T(8,128)(2,1)S(1)} %get-tuple-element.80.refs_7_), channel_id=1, source_target_pairs={{0,24},{8,16},{16,8},{24,0},{1,25},{9,17},{17,9},{25,1},{2,26},{10... | collective-permute-start | bytes 1572872 | tf_op jit(solution)/shard_map/ppermute | solution.py:809
  528.5 56.8 %collective-permute-start.16 = (bf16[2,512,1024]{2,1,0:T(8,128)(2,1)S(1)}, bf16[2,512,1024]{2,1,0:T(8,128)(2,1)}, u32[]{:S(2)}, u32[]{:S(2)}) collective-permute-start(bf16[2,512,1024]{2,1,0:T(8,128)(2,1)S(1)} %copy-done.8), channel_id=1, source_target_pairs={{0,8},{8,0},{16,24},{24,16},{1,9},{9,1},{17,25},{25,17},{2,10},{10... | collective-permute-start | bytes 6291464 | tf_op jit(solution)/shard_map/ppermute | solution.py:809
  531.2 52.2 %collective-permute-start.17 = (bf16[2,512,1024]{2,1,0:T(8,128)(2,1)S(1)}, bf16[2,512,1024]{2,1,0:T(8,128)(2,1)S(1)}, u32[]{:S(2)}, u32[]{:S(2)}) collective-permute-start(bf16[2,512,1024]{2,1,0:T(8,128)(2,1)S(1)} %get-tuple-element.82.refs_1_), channel_id=1, source_target_pairs={{0,16},{8,24},{16,0},{24,8},{1,17},{9,25},{17,1},{25,9},{2,18},{10... | collective-permute-start | bytes 6291464 | tf_op jit(solution)/shard_map/ppermute | solution.py:809
  534.6 101.9 %collective-permute-start.19 = (bf16[2,512,1024]{2,1,0:T(8,128)(2,1)}, bf16[2,512,1024]{2,1,0:T(8,128)(2,1)}, u32[]{:S(2)}, u32[]{:S(2)}) collective-permute-start(bf16[2,512,1024]{2,1,0:T(8,128)(2,1)} %get-tuple-element.90), channel_id=1, source_target_pairs={{0,16},{8,24},{16,0},{24,8},{1,17},{9,25},{17,1},{25,9},{2,18},{10... | collective-permute-start | bytes 6291464 | tf_op jit(solution)/shard_map/ppermute | solution.py:809
  536.2 100.2 %collective-permute-start.18 = (bf16[2,512,1024]{2,1,0:T(8,128)(2,1)}, bf16[2,512,1024]{2,1,0:T(8,128)(2,1)}, u32[]{:S(2)}, u32[]{:S(2)}) collective-permute-start(bf16[2,512,1024]{2,1,0:T(8,128)(2,1)} %get-tuple-element.89), channel_id=1, source_target_pairs={{0,8},{8,0},{16,24},{24,16},{1,9},{9,1},{17,25},{25,17},{2,10},{10... | collective-permute-start | bytes 6291464 | tf_op jit(solution)/shard_map/ppermute | solution.py:809
  750.3 4.0 collective-permute-start.20
  (73 other events, 427.0 us)
Sparse Core Ops, SparseCore 0:
  12.6 104.1 all-gather.6
  118.9 45.7 all-gather.8
  166.8 45.8 all-gather.12
  214.8 45.8 all-gather.10
  262.1 45.8 all-gather.14
  310.2 48.6 reduce-scatter.9
  376.7 48.7 reduce-scatter.11
  467.6 47.6 reduce-scatter.5
  517.6 48.1 reduce-scatter.7
  651.1 86.9 reduce-scatter.13

commit v4 on v3

--- a/solution.py
+++ b/solution.py
@@ -366,7 +366,7 @@
             jax.ShapeDtypeStruct((rows, 1), F32),
             jax.ShapeDtypeStruct((rows, width), BF16),
         ],
-        compiler_params=pltpu.CompilerParams(vmem_limit_bytes=32 * MIB),
+        compiler_params=pltpu.CompilerParams(vmem_limit_bytes=60 * MIB),
     )(x, own_block, gain[None], *got, *earlier)
 
 
@@ -394,7 +394,7 @@
             jax.ShapeDtypeStruct((rows, width), BF16),
             jax.ShapeDtypeStruct((1, width), F32),
         ],
-        compiler_params=pltpu.CompilerParams(vmem_limit_bytes=32 * MIB),
+        compiler_params=pltpu.CompilerParams(vmem_limit_bytes=60 * MIB),
     )(residual, scale, gain[None], grad, d_mid, *earlier)
 
 
@@ -727,6 +727,139 @@
             ref[:, c * cols : (c + 1) * cols] = slots[c, :, k * cols : (k + 1) * cols].astype(F32)
 
 
+class Doubling:
+    def __init__(self, axis, order, last, block, slot, sems, base):
+        self.me, self.axis, self.order, self.last = lax.axis_index(axis), axis, order, last
+        self.block, self.slot, self.sems, self.base = block, slot, sems, base
+        self.steps = [halving_masks(order[:s]) for s in range(len(order) + 1)]
+        self.keys = [(bit, m) for bit, ms in zip(order, self.steps) for m in ms]
+        if last is not None:
+            self.keys += [(last, m) for m in self.steps[-1]]
+
+    def copy(self, bit, m):
+        at = self.base + self.keys.index((bit, m))
+        place = self.slot(flip(self.me, m))
+        return pltpu.make_async_remote_copy(
+            src_ref=place if m else self.block,
+            dst_ref=place,
+            send_sem=self.sems.at[0, at],
+            recv_sem=self.sems.at[1, at],
+            device_id={self.axis: flip(self.me, 1 << bit)},
+            device_id_type=pl.DeviceIdType.MESH,
+        )
+
+    def step(self, s):
+        fresh = [0]
+        if s:
+            fresh = [m | (1 << self.order[s - 1]) for m in self.steps[s - 1]]
+            for m in self.steps[s - 1]:
+                self.copy(self.order[s - 1], m).wait_recv()
+        if s < len(self.order):
+            for m in self.steps[s]:
+                self.copy(self.order[s], m).start()
+        if self.last is not None:
+            for m in fresh:
+                self.copy(self.last, m).start()
+
+    def finish(self):
+        if self.last is not None:
+            for m in self.steps[-1]:
+                self.copy(self.last, m).wait_recv()
+        for key in self.keys:
+            self.copy(*key).wait_send()
+
+
+def start_kernel(n_ctx, n_exp, w_ref, x_ref, small_ref, w_out, x_out, small_out, sems, local_sems):
+    c_at, e_at = lax.axis_index("ctx"), lax.axis_index("exp")
+    c_bits, e_bits = n_ctx.bit_length() - 1, n_exp.bit_length() - 1
+    meet(
+        [{"ctx": flip(c_at, 1 << b)} for b in range(c_bits)]
+        + [{"exp": flip(e_at, 1 << b)} for b in range(e_bits)]
+    )
+    far = list(range(1, e_bits))
+    near = list(range(c_bits))
+    half = w_ref.shape[0] // 2
+    moves, base = [], 0
+
+    def add(axis, order, last, block, slot):
+        moves.append(Doubling(axis, order, last, block, slot, sems, base))
+        return base + len(moves[-1].keys)
+
+    base = add("exp", far, 0, small_ref, lambda at: small_out.at[at])
+    for i, order in enumerate((far[::-1], far)):
+        lines = pl.ds(i * half, half)
+        base = add(
+            "exp", order, 0, w_ref.at[lines], lambda at, lines=lines: w_out.at[at, lines]
+        )
+    for i, order in enumerate((near[::-1], near)):
+        base = add("ctx", order, None, x_ref.at[i], lambda at, i=i: x_out.at[i, at])
+    own = [
+        pltpu.make_async_copy(w_ref, w_out.at[e_at], local_sems.at[0]),
+        pltpu.make_async_copy(small_ref, small_out.at[e_at], local_sems.at[1]),
+        pltpu.make_async_copy(x_ref.at[0], x_out.at[0, c_at], local_sems.at[2]),
+        pltpu.make_async_copy(x_ref.at[1], x_out.at[1, c_at], local_sems.at[3]),
+    ]
+    for s in range(max(len(far), len(near)) + 1):
+        for move in moves:
+            if s <= len(move.order):
+                move.step(s)
+        if s == 0:
+            for copy in own:
+                copy.start()
+    for move in moves:
+        move.finish()
+    for copy in own:
+        copy.wait()
+
+
+def gather_start(w, x, small):
+    n_ctx, n_exp = lax.axis_size("ctx"), lax.axis_size("exp")
+    count = 3 * (n_exp - 1) + 2 * (n_ctx - 1)
+    return pl.pallas_call(
+        functools.partial(start_kernel, n_ctx, n_exp),
+        in_specs=[ANY] * 3,
+        out_specs=[ANY] * 3,
+        out_shape=[
+            jax.ShapeDtypeStruct((n_exp,) + w.shape, BF16),
+            jax.ShapeDtypeStruct((x.shape[0], n_ctx) + x.shape[1:], BF16),
+            jax.ShapeDtypeStruct((n_exp,) + small.shape, BF16),
+        ],
+        scratch_shapes=[pltpu.SemaphoreType.DMA((2, count)), pltpu.SemaphoreType.DMA((4,))],
+        compiler_params=pltpu.CompilerParams(collective_id=6, has_side_effects=True),
+    )(w, x, small)
+
+
+def hold_kernel(*refs):
+    pass
+
+
+def held(arrays, earlier):
+    n = len(arrays)
+    return pl.pallas_call(
+        hold_kernel,
+        in_specs=[ANY] * (n + len(earlier)),
+        out_specs=[ANY] * n,
+        out_shape=[jax.ShapeDtypeStruct(a.shape, a.dtype) for a in arrays],
+        input_output_aliases={i: i for i in range(n)},
+        compiler_params=pltpu.CompilerParams(vmem_limit_bytes=60 * MIB),
+    )(*arrays, *earlier)
+
+
+def mask_kernel(x_ref, valid_ref, *refs):
+    refs[-1][...] = (x_ref[...].astype(F32) * valid_ref[...]).astype(BF16)
+
+
+def masked(x, valid, earlier):
+    blocks = [pl.BlockSpec(a.shape, lambda i: (0, 0)) for a in (x, valid)]
+    return pl.pallas_call(
+        mask_kernel,
+        grid=(1,),
+        in_specs=blocks + [ANY] * len(earlier),
+        out_specs=blocks[0],
+        out_shape=jax.ShapeDtypeStruct(x.shape, BF16),
+    )(x, valid, *earlier)
+
+
 VMEM = pl.BlockSpec(memory_space=pltpu.VMEM)
 ANY = pl.BlockSpec(memory_space=pl.ANY)
 
@@ -851,7 +984,6 @@
             moves.append(((e // ratio) * n_exp + c * ratio + e % ratio, c * n_exp + e))
     out_piece = lax.ppermute(take(w_output, c_at * cols, cols, 1), ("ctx", "exp"), moves)
 
-    x_low = gather_ctx(tokens[0].reshape(halves, part, width), 1).reshape(seq, width)
     storage = jnp.arange(seq, dtype=jnp.int32)
     storage = (storage % half_seq // part) * rows + storage // half_seq * part + storage % part
     positions = positions_of(span_order, storage, rows // 2)
@@ -860,16 +992,25 @@
     )
     valid = (my_positions < seq_length).astype(F32)[:, None]
     member = jnp.sum(
-        (routes[0][:, :, None] == jnp.arange(LANES, dtype=jnp.int32)[None, None, :]).astype(BF16),
-        axis=1,
+        (routes[0][:, None, :] == jnp.arange(experts, dtype=jnp.int32)[None, :, None]).astype(BF16),
+        axis=2,
     )
     small = jnp.concatenate(
         [
             w_router.reshape(-1), gain_attn, gain_query, gain_key, gain_mlp,
-            member[:, :experts].reshape(-1),
+            member.reshape(-1),
         ]
     )
-    small_all = gather(small[None], "exp")
+    used = small.shape[0]
+    lines = -(-used // (16 * LANES)) * 16
+    small = jnp.pad(small, (0, lines * LANES - used)).reshape(lines, LANES)
+    pieces = [take(w, c_at * cols, cols, 1) for w in (w_query, w_key, w_value)]
+    weights, x_low, small_all = gather_start(
+        jnp.concatenate(pieces + [out_piece], axis=1), tokens[0].reshape(halves, part, width), small
+    )
+    weights = weights.reshape(width, 4 * cols)
+    x_low = x_low.reshape(seq, width)
+    small_all = small_all.reshape(n_exp, lines * LANES)[:, :used]
     at = shard * experts
     router_w = small_all[:, :at].reshape(width, experts)
     router_w = jnp.pad(router_w, ((0, 0), (0, LANES - experts)))
@@ -883,14 +1024,12 @@
     query_gain = take(query_gain_all, c_at * cols, cols)
     key_gain = take(key_gain_all, c_at * cols, cols)
 
-    pieces = [take(w, c_at * cols, cols, 1) for w in (w_query, w_key, w_value)]
-    weights = gather(jnp.concatenate(pieces + [out_piece], axis=1), "exp")
     qkv_w = weights[:, : 3 * cols]
     out_w = weights[:, 3 * cols :].reshape(n_ctx, cols, cols).transpose(1, 0, 2).reshape(cols, width)
     x_all = x_low.astype(F32)
 
-    grad_mine = cotangent[0].astype(F32) * valid
-    grad_low = grad_mine.astype(BF16)
+    grad_low = masked(cotangent[0], valid, (weights,))
+    grad_mine = grad_low.astype(F32)
     grad_parts = [gather(grad_low[h * part : (h + 1) * part], "exp") for h in range(halves)]
     d_hid_parts = [
         jnp.stack([mm_t(g, w_down[j]).astype(BF16) for j in range(own)]) for g in grad_parts
@@ -920,7 +1059,8 @@
             if d:
                 got.append(swap(block.astype(BF16), d))
         residual, scale, mid = middle(
-            tokens[0, h * part : (h + 1) * part], block, got, mlp_gain, grad_parts[-1:]
+            tokens[0, h * part : (h + 1) * part], block, got, mlp_gain,
+            (d_hid_parts[h],),
         )
         residual_parts.append(residual)
         scale_parts.append(scale)
@@ -956,7 +1096,7 @@
     d_res0, low0, gain0, dl0 = back_to_rows(0, y_parts[0])
     d_res1, low1, gain1, dl1 = back_to_rows(1, y_parts[0])
     bits = list(range(n_ctx.bit_length() - 1))
-    gives, first_gate, first_up = [], [], []
+    gives, first_gate, give_up = [], [], []
     for j in range(own):
         order = bits if j % 2 == 0 else bits[::-1]
         table = c_at ^ jnp.asarray(halving_masks(order)[n_ctx // 2 :], jnp.int32)
@@ -964,7 +1104,7 @@
             table, mids, [da_parts, db_parts], width // n_ctx, j, (low0, low1, *gives)
         )
         first_gate.append(swap(give[0], 1 << order[0]))
-        first_up.append(swap(give[1], 1 << order[0]))
+        give_up.append(give[1])
         gives.append(give[0])
     g_mid_gain = gain0 + gain1
     d_res_parts, dl_parts = [d_res0, d_res1], [dl0, dl1]
@@ -988,14 +1128,17 @@
         ],
         axis=0,
     )
-    inner = ctx_sum(jnp.pad(inner, ((0, 6), (0, 0))), 1, first_gate)[:2] / width
+    inner = ctx_sum(jnp.pad(inner, ((0, 6), (0, 0))), 1, first_gate)
+    give_up = held(give_up, (inner,))
+    first_up = [swap(g, 1 << (bits[0] if j % 2 == 0 else bits[-1])) for j, g in enumerate(give_up)]
+    inner = inner[:2] / width
     dqp = q_scale * dq_n * query_gain - qp * (q_scale**3) * inner[0][:, None]
     dkp = k_scale * dk_n * key_gain - kp * (k_scale**3) * inner[1][:, None]
     g_query_gain = jnp.sum(dq_n * qp * q_scale, axis=0)
     g_key_gain = jnp.sum(dk_n * kp * k_scale, axis=0)
     d_qkv = jnp.concatenate([dqp.astype(BF16), dkp.astype(BF16), dv.astype(BF16)], axis=1)
-    g_mine = attention_grads(xn, d_qkv, attended_parts, dl_parts, cols, first_up)
-    partial = input_partial(d_qkv, weights, part, ())
+    g_mine = attention_grads(xn, d_qkv, attended_parts, dl_parts, cols, ())
+    partial = input_partial(d_qkv, weights, part, first_up)
     g_gate, dxn = gate_sums(
         mids, da_parts, partial, first_gate, (g_mine,)
     )

time: 882 us -> 852 us (0.966)
  Pallas kernels: 505 us -> 561 us
  local copies, waits for them, and re-layouts: 102 us -> 77.5 us
  starting transfers between devices: 44.8 us -> 21 us
  waiting for transfers between devices: 71.4 us -> 50.3 us
  blocking collectives: 15 us -> 0 us
    pallas_call x0 -> x3, Pallas kernels: none -> 85.2 us  [the longest x1 82.8 us: gather_start(): pl.pallas_call(functools.partial(start_kernel, n_ctx, n_exp), in_specs=[A...]
    pallas_call x2, Pallas kernels: 51.7 us -> 17.4 us  [ctx_sum(): pl.pallas_call(functools.partial(ctx_sum_kernel, n), in_specs=[whole] + [...]
    ppermute x19 -> x16, starting transfers between devices: 42 us -> 18.3 us  [swap(): return lax.ppermute(block, 'ctx', [(i, i ^ bits) for i in range(n)])]
    unnamed x164 -> x127, local copies, waits for them, and re-layouts: 52.3 us -> 36.8 us
    all_gather x1 -> x0, blocking collectives: 15 us -> none  [gather(): return lax.all_gather(block, axis, axis=0, tiled=True)]
    all_gather x5 -> x4, waiting for transfers between devices: 18.9 us -> 5.15 us  [gather(): return lax.all_gather(block, axis, axis=0, tiled=True)]
    dynamic_update_slice x12 -> x8, local copies, waits for them, and re-layouts: 15.9 us -> 5.75 us  [gather_ctx(): lax.dynamic_update_slice_in_dim(out, jnp.expand_dims(piece, axis), me ^ d...]
    ppermute x19 -> x16, waiting for transfers between devices: 52.2 us -> 45 us  [swap(): return lax.ppermute(block, 'ctx', [(i, i ^ bits) for i in range(n)])]
  transfers between devices with their start and end apart: 31 -> 27, of which waited for: 10 -> 4; matrix products, arithmetic and copies ran while one was open for 19% -> 18% of each run, Pallas kernels for 48% -> 46%
where the time goes in v4:
time: 852 us; the launch traced here: 843 us
  Pallas kernels  561 us (66%)
  local copies, waits for them, and re-layouts  77.5 us (9%)
  matrix products  65.2 us (8%)
  other arithmetic  52.2 us (6%)
  waiting for transfers between devices  50.3 us (6%)
  starting transfers between devices  21 us (2%)
  between operations  15.7 us (2%)
    pallas_call x3, Pallas kernels, exchange(): pl.pallas_call(kernel, in_specs=[VMEM] * len(operands) + [ANY] * len(earl...  247 us
    pallas_call x2, Pallas kernels, expert_pass(): pl.pallas_call(functools.partial(expert_kernel, experts, own, 512), grid=...  98.8 us
    pallas_call x1, Pallas kernels, gather_start(): pl.pallas_call(functools.partial(start_kernel, n_ctx, n_exp), in_specs=[A...  82.8 us
    ppermute x16, waiting for transfers between devices, swap(): return lax.ppermute(block, 'ctx', [(i, i ^ bits) for i in range(n)])  45 us
    unnamed x127, local copies, waits for them, and re-layouts  36.8 us
    dot_general x6, matrix products, mm_t(): lax.dot_general(left, right, (((1,), (1,)), ((), ())), preferred_element_...  34.8 us
    pallas_call x2, Pallas kernels, given_grads(): pl.pallas_call(functools.partial(give_kernel, n, len(rights)), grid_spec=...  27.8 us
    pallas_call x2, Pallas kernels, attend_back(): pl.pallas_call(attend_back_kernel, grid=(heads,), in_specs=attention_spec...  27.7 us
  transfers between devices with their start and end apart: 27, of which 4 were waited for; matrix products, arithmetic and copies ran while one was open for 18% of the time, Pallas kernels for 46%

profile of v4, /device:TPU:0, one launch (start us, length us, event | category | flops | bytes accessed | tf_op | source)
XLA Modules:
  0.0 843.2 jit_solution(9688435519773390706)
XLA Ops:
  15.8 4.8 select_reduce_fusion.1
  24.5 82.8 %shard_map.290 = (bf16[8,256,2048]{2,1,0:T(8,128)(2,1)}, bf16[2,4,128,2048]{3,2,1,0:T(8,128)(2,1)}, bf16[8,80,128]{2,1,0:T(8,128)(2,1)}) custom-call(bf16[256,2048]{1,0:T(8,128)(2,1)} %pad_maximum_fusion.4.w_ref, bf16[2,128,2048]{2,1,0:T(8,128)(2,1)} %bitcast.196, bf16[80,128]{1,0:T(8,128)(2,1)} %pad_bitcast_fusion.small_ref), custom_call_target="tpu_custom_call" | custom-call | tf_op jit(solution)/shard_map/pallas_call | solution.py:818
  112.8 5.3 select_reduce_fusion
  131.3 10.3 %fusion.2.q_ref.k_ref.v_ref = f32[1024,1536]{1,0:T(8,128)S(1)} fusion(bf16[1024,2048]{1,0:T(8,128)(2,1)S(1)} %fusion.1.x_ref, bf16[2048,2048]{1,0:T(8,128)(2,1)} %bitcast.194), kind=kOutput, calls=%fused_computation.4 | convolution fusion | flops 6442450944 | bytes 16777216 | tf_op jit(solution)/shard_map/dot_general | solution.py:24
  145.2 10.5 %shard_map.291 = f32[8,1024]{1,0:T(8,128)} custom-call(f32[8,1024]{1,0:T(8,128)} %select_maximum_fusion.1.x_ref), custom_call_target="tpu_custom_call" | custom-call | tf_op jit(solution)/shard_map/pallas_call | solution.py:434
  157.3 4.1 copy.55
  161.4 9.7 %shard_map.292.refs_0_ = bf16[512,512]{1,0:T(8,128)(2,1)S(1)} custom-call(f32[1024,1536]{1,0:T(8,128)} %copy-done.16, f32[1024,1536]{1,0:T(8,128)} %copy-done.16, f32[1024,1536]{1,0:T(8,128)} %copy-done.16, f32[1024,1]{1,0:T(8,128)S(1)} %copy.53.qs_ref, f32[1024,1]{1,0:T(8,128)S(1)} %copy.54.ks_ref, f32[1,512]{1,0:T(1,128)S(1)} %bitcast.174, ...), custom_call_target="tpu_custom_call" | custom-call | flops 1073741824 | bytes 8388608 | tf_op jit(solution)/shard_map/pallas_call | solution.py:125
  181.8 8.2 convert_bitcast_fusion.3
  190.1 7.2 convert_bitcast_fusion.4
  200.5 3.4 shard_map.294
  203.9 9.7 %shard_map.296.refs_1_ = bf16[512,512]{1,0:T(8,128)(2,1)S(1)} custom-call(f32[1024,1536]{1,0:T(8,128)} %copy-done.16, f32[1024,1536]{1,0:T(8,128)} %copy-done.16, f32[1024,1536]{1,0:T(8,128)} %copy-done.16, f32[1024,1]{1,0:T(8,128)S(1)} %copy.53.qs_ref, f32[1024,1]{1,0:T(8,128)S(1)} %copy.54.ks_ref, f32[1,512]{1,0:T(1,128)S(1)} %bitcast.175, ...), custom_call_target="tpu_custom_call" | custom-call | flops 1073741824 | bytes 8388608 | tf_op jit(solution)/shard_map/pallas_call | solution.py:125
  223.7 8.2 convert_bitcast_fusion.1
  232.0 7.0 convert_bitcast_fusion.2
  250.8 5.1 all-gather.7.cloned.1.call-done.x_ref.refs_0_
  255.9 49.3 %shard_map.295 = (bf16[2,1024,1024]{2,1,0:T(8,128)(2,1)}, bf16[2,1024,1024]{2,1,0:T(8,128)(2,1)}, bf16[2,1024,1024]{2,1,0:T(8,128)(2,1)}, bf16[1024,2048]{1,0:T(8,128)(2,1)}, bf16[1024,128]{1,0:T(8,128)(2,1)}) custom-call(bf16[1024,2048]{1,0:T(8,128)(2,1)} %all-gather.7.cloned.1.call-done.x_ref.refs_0_, ...), custom_call_target="tpu_custom_call" | custom-call | flops 34359738368 | bytes 41943040 | tf_op jit(solution)/shard_map/pallas_call | solution.py:230
  305.3 49.5 %shard_map.298 = (bf16[2,1024,1024]{2,1,0:T(8,128)(2,1)}, bf16[2,1024,1024]{2,1,0:T(8,128)(2,1)}, bf16[2,1024,1024]{2,1,0:T(8,128)(2,1)}, bf16[1024,2048]{1,0:T(8,128)(2,1)}, bf16[1024,128]{1,0:T(8,128)(2,1)}) custom-call(bf16[1024,2048]{1,0:T(8,128)(2,1)} %all-gather.11.cloned.1.call-done.x_ref.refs_1_, ...), custom_call_target="tpu_custom_call" | custom-call | flops 34359738368 | bytes 41943040 | tf_op jit(solution)/shard_map/pallas_call | solution.py:230
  355.0 90.4 %shard_map.299 = (f32[2,256,2048]{2,1,0:T(8,128)}, bf16[1024,2048]{1,0:T(8,128)(2,1)}, bf16[1024,2048]{1,0:T(8,128)(2,1)}) custom-call(bf16[2,1024,1024]{2,1,0:T(8,128)(2,1)} %get-tuple-element.69.refs_0_, bf16[2,1024,1024]{2,1,0:T(8,128)(2,1)} %get-tuple-element.71.refs_1_, bf16[1024,2048]{1,0:T(8,128)(2,1)} %all-gather.5.cloned.1.call-done.refs_2_, ...), custom_call_target="tpu_custom_call" | custom-call | tf_op jit(solution)/shard_map/pallas_call | solution.py:869
  449.6 3.5 shard_map.300
  456.6 3.5 shard_map.301
  465.2 13.9 %shard_map.302 = (bf16[2,512,1024]{2,1,0:T(8,128)(2,1)S(1)}, bf16[2,512,1024]{2,1,0:T(8,128)(2,1)S(1)}) custom-call(s32[2]{0:T(128)S(1)} %get-tuple-element.168.table, bf16[1024,2048]{1,0:T(8,128)(2,1)} %all-gather.7.cloned.1.call-done.x_ref.refs_0_, bf16[1024,2048]{1,0:T(8,128)(2,1)} %all-gather.11.cloned.1.call-done.x_ref.refs_1_, ...), custom_call_target="tpu_custom_call" | custom-call | tf_op jit(solution)/shard_map/pallas_call | solution.py:331
  481.7 14.0 %shard_map.303 = (bf16[2,512,1024]{2,1,0:T(8,128)(2,1)S(1)}, bf16[2,512,1024]{2,1,0:T(8,128)(2,1)S(1)}) custom-call(s32[2]{0:T(128)S(1)} %get-tuple-element.167.table, bf16[1024,2048]{1,0:T(8,128)(2,1)} %all-gather.7.cloned.1.call-done.x_ref.refs_0_, bf16[1024,2048]{1,0:T(8,128)(2,1)} %all-gather.11.cloned.1.call-done.x_ref.refs_1_, ...), custom_call_target="tpu_custom_call" | custom-call | tf_op jit(solution)/shard_map/pallas_call | solution.py:331
  508.6 13.7 %shard_map.304 = (f32[512,512]{1,0:T(8,128)S(1)}, f32[1024,512]{1,0:T(8,128)}, f32[1024,512]{1,0:T(8,128)}) custom-call(f32[1024,1536]{1,0:T(8,128)} %copy-done.16, f32[1024,1536]{1,0:T(8,128)} %copy-done.16, f32[1024,1536]{1,0:T(8,128)} %copy-done.16, f32[1024,1]{1,0:T(8,128)S(1)} %copy.53.qs_ref, f32[1024,1]{1,0:T(8,128)S(1)} %copy.54.ks_ref, ...), custom_call_target="tpu_custom_call" | custom-call | flops 2684354560 | bytes 16777216 | tf_op jit(solution)/shard_map/pallas_call | solution.py:143
  523.7 14.0 %shard_map.305 = (f32[512,512]{1,0:T(8,128)S(1)}, f32[1024,512]{1,0:T(8,128)}, f32[1024,512]{1,0:T(8,128)}) custom-call(f32[1024,1536]{1,0:T(8,128)} %copy-done.16, f32[1024,1536]{1,0:T(8,128)} %copy-done.16, f32[1024,1536]{1,0:T(8,128)} %copy-done.16, f32[1024,1]{1,0:T(8,128)S(1)} %copy.53.qs_ref, f32[1024,1]{1,0:T(8,128)S(1)} %copy.54.ks_ref, ...), custom_call_target="tpu_custom_call" | custom-call | flops 2684354560 | bytes 16777216 | tf_op jit(solution)/shard_map/pallas_call | solution.py:143
  545.3 8.0 collective-permute-done.14.refs_1_.refs_6_
  553.4 6.9 shard_map.306.refs_2_
  561.0 4.0 subtract_convert_fusion.1
  568.0 13.3 %shard_map.309.refs_7_ = bf16[2048,2048]{1,0:T(8,128)(2,1)} custom-call(bf16[1024,2048]{1,0:T(8,128)(2,1)} %copy-done.26, bf16[1024,1536]{1,0:T(8,128)(2,1)} %pad_maximum_fusion.2.d_ref, bf16[512,512]{1,0:T(8,128)(2,1)S(1)} %copy-done.13, bf16[512,512]{1,0:T(8,128)(2,1)S(1)} %copy-done.15, bf16[512,2048]{1,0:T(8,128)(2,1)} %bitcast.48.refs_2_, ...), custom_call_target="tpu_custom_call" | custom-call | flops 8589934592 | bytes 20971520 | tf_op jit(solution)/shard_map/pallas_call | solution.py:275
  582.8 4.0 fusion.127
  597.7 35.9 %collective-permute-done.15.refs_0_.refs_6_ = bf16[2,512,1024]{2,1,0:T(8,128)(2,1)S(1)} collective-permute-done((bf16[2,512,1024]{2,1,0:T(8,128)(2,1)}, bf16[2,512,1024]{2,1,0:T(8,128)(2,1)S(1)}, u32[]{:S(2)}, u32[]{:S(2)}) %collective-permute-start.15) | collective-permute-done | bytes 2097184 | tf_op jit(solution)/shard_map/ppermute | solution.py:942
  634.7 11.5 %shard_map.308.refs_4_ = bf16[2,4,256,1024]{3,2,1,0:T(8,128)(2,1)} custom-call(bf16[1024,1536]{1,0:T(8,128)(2,1)} %pad_maximum_fusion.2.d_ref, bf16[2048,2048]{1,0:T(8,128)(2,1)} %bitcast.195, bf16[2,512,1024]{2,1,0:T(8,128)(2,1)S(1)} %collective-permute-done.15.refs_0_.refs_6_, bf16[2,512,1024]{2,1,0:T(8,128)(2,1)} %collective-permute-done.16.refs_1_.refs_7_), custom_call_target="tpu_custom_call" | custom-call | tf_op jit(solution)/shard_map/pallas_call | solution.py:305
  646.2 70.0 %shard_map.310 = (f32[2,512,1024]{2,1,0:T(8,128)}, f32[2,256,1024]{2,1,0:T(8,128)}) custom-call(bf16[1024,2048]{1,0:T(8,128)(2,1)} %all-gather.7.cloned.1.call-done.x_ref.refs_0_, bf16[1024,2048]{1,0:T(8,128)(2,1)} %all-gather.11.cloned.1.call-done.x_ref.refs_1_, bf16[2,1024,1024]{2,1,0:T(8,128)(2,1)} %get-tuple-element.83.refs_2_, ...), custom_call_target="tpu_custom_call" | custom-call | tf_op jit(solution)/shard_map/pallas_call | solution.py:869
  727.2 86.2 %shard_map.311 = (f32[2,512,1024]{2,1,0:T(8,128)}, f32[256,2048]{1,0:T(8,128)}, f32[256,2048]{1,0:T(8,128)}, f32[256,2048]{1,0:T(8,128)}, f32[256,2048]{1,0:T(8,128)}, /*index=5*/f32[24,256]{1,0:T(8,128)}) custom-call(bf16[1024,2048]{1,0:T(8,128)(2,1)} %all-gather.7.cloned.1.call-done.x_ref.refs_0_, ...), custom_call_target="tpu_custom_call" | custom-call | tf_op jit(solution)/shard_map/pallas_call | solution.py:869
  (294 shorter events, 159.8 us)
Async XLA Ops:
  7.2 174.6 %all-gather.5.cloned.1.call-start = ((), (), s32[]{:S(2)}) async-start(), calls=%async_computation.5 | async-start | bytes 4718592 | tf_op jit(solution)/shard_map/all_gather | solution.py:929
  8.4 15.0 %collective-permute-start = (bf16[256,512]{1,0:T(8,128)(2,1)S(1)}, bf16[256,512]{1,0:T(8,128)(2,1)S(1)}, u32[]{:S(2)}, u32[]{:S(2)}) collective-permute-start(bf16[256,512]{1,0:T(8,128)(2,1)S(1)} %constant_dynamic-slice_fusion), channel_id=1, source_target_pairs={{0,0},{1,1},{8,2},{9,3},{16,4},{17,5},{24,6},{25,7},{2,8},{3,9},{1... | collective-permute-start | bytes 786440 | tf_op jit(solution)/shard_map/ppermute | solution.py:985
  112.1 111.7 %all-gather.9.cloned.1.call-start = ((), (), s32[]{:S(2)}) async-start(), calls=%async_computation.7 | async-start | bytes 4718592 | tf_op jit(solution)/shard_map/all_gather | solution.py:929
  127.5 128.4 %all-gather.7.cloned.1.call-start = ((), (), s32[]{:S(2)}) async-start(), calls=%async_computation.6 | async-start | bytes 4718592 | tf_op jit(solution)/shard_map/all_gather | solution.py:929
  131.3 10.3 %copy-start.26 = (bf16[1024,2048]{1,0:T(8,128)(2,1)}, bf16[1024,2048]{1,0:T(8,128)(2,1)S(1)}, u32[]{:S(2)}) copy-start(bf16[1024,2048]{1,0:T(8,128)(2,1)S(1)} %fusion.1.x_ref) | copy-start | bytes 12582916
  161.4 9.7 %copy-start.17 = (bf16[4,512,512]{1,2,0:T(8,128)(2,1)S(1)}, bf16[4,512,512]{1,2,0:T(8,128)(2,1)}, u32[]{:S(2)}) copy-start(bf16[4,512,512]{1,2,0:T(8,128)(2,1)} %copy.55) | copy-start | bytes 6291460
  172.8 26.9 %collective-permute-start.3 = (bf16[128,2048]{1,0:T(8,128)(2,1)}, bf16[128,2048]{1,0:T(8,128)(2,1)S(1)}, u32[]{:S(2)}, u32[]{:S(2)}) collective-permute-start(bf16[128,2048]{1,0:T(8,128)(2,1)} %convolution_convert_fusion.3), channel_id=1, source_target_pairs={{0,8},{8,0},{16,24},{24,16},{1,9},{9,1},{17,25},{25,17},{2,10},{10... | collective-permute-start | bytes 1572872 | tf_op jit(solution)/shard_map/ppermute | solution.py:942
  175.0 24.7 %collective-permute-start.2 = (bf16[128,2048]{1,0:T(8,128)(2,1)}, bf16[128,2048]{1,0:T(8,128)(2,1)}, u32[]{:S(2)}, u32[]{:S(2)}) collective-permute-start(bf16[128,2048]{1,0:T(8,128)(2,1)} %convolution_convert_fusion.4), channel_id=1, source_target_pairs={{0,16},{8,24},{16,0},{24,8},{1,17},{9,25},{17,1},{25,9},{2,18},{10... | collective-permute-start | bytes 1572872 | tf_op jit(solution)/shard_map/ppermute | solution.py:942
  178.0 21.7 %collective-permute-start.1 = (bf16[128,2048]{1,0:T(8,128)(2,1)}, bf16[128,2048]{1,0:T(8,128)(2,1)}, u32[]{:S(2)}, u32[]{:S(2)}) collective-permute-start(bf16[128,2048]{1,0:T(8,128)(2,1)} %convolution_convert_fusion.5), channel_id=1, source_target_pairs={{0,24},{8,16},{16,8},{24,0},{1,25},{9,17},{17,9},{25,1},{2,26},{10... | collective-permute-start | bytes 1572872 | tf_op jit(solution)/shard_map/ppermute | solution.py:942
  203.9 101.3 %all-gather.11.cloned.1.call-start = ((), (), s32[]{:S(2)}) async-start(), calls=%async_computation.8 | async-start | bytes 4718592 | tf_op jit(solution)/shard_map/all_gather | solution.py:929
  203.9 9.7 %copy-start.18 = (bf16[4,512,512]{1,2,0:T(8,128)(2,1)S(1)}, bf16[4,512,512]{1,2,0:T(8,128)(2,1)}, u32[]{:S(2)}) copy-start(bf16[4,512,512]{1,2,0:T(8,128)(2,1)} %copy.55) | copy-start | bytes 6291460
  215.2 26.1 %collective-permute-start.6 = (bf16[128,2048]{1,0:T(8,128)(2,1)}, bf16[128,2048]{1,0:T(8,128)(2,1)S(1)}, u32[]{:S(2)}, u32[]{:S(2)}) collective-permute-start(bf16[128,2048]{1,0:T(8,128)(2,1)} %convolution_convert_fusion), channel_id=1, source_target_pairs={{0,8},{8,0},{16,24},{24,16},{1,9},{9,1},{17,25},{25,17},{2,10},{10... | collective-permute-start | bytes 1572872 | tf_op jit(solution)/shard_map/ppermute | solution.py:942
  217.5 23.9 %collective-permute-start.5 = (bf16[128,2048]{1,0:T(8,128)(2,1)}, bf16[128,2048]{1,0:T(8,128)(2,1)}, u32[]{:S(2)}, u32[]{:S(2)}) collective-permute-start(bf16[128,2048]{1,0:T(8,128)(2,1)} %convolution_convert_fusion.1), channel_id=1, source_target_pairs={{0,16},{8,24},{16,0},{24,8},{1,17},{9,25},{17,1},{25,9},{2,18},{10... | collective-permute-start | bytes 1572872 | tf_op jit(solution)/shard_map/ppermute | solution.py:942
  220.4 21.0 %collective-permute-start.4 = (bf16[128,2048]{1,0:T(8,128)(2,1)}, bf16[128,2048]{1,0:T(8,128)(2,1)}, u32[]{:S(2)}, u32[]{:S(2)}) collective-permute-start(bf16[128,2048]{1,0:T(8,128)(2,1)} %convolution_convert_fusion.2), channel_id=1, source_target_pairs={{0,24},{8,16},{16,8},{24,0},{1,25},{9,17},{17,9},{25,1},{2,26},{10... | collective-permute-start | bytes 1572872 | tf_op jit(solution)/shard_map/ppermute | solution.py:942
  245.5 204.0 %reduce-scatter.10.cloned.1.call-start = ((), (), s32[]{:S(2)}) async-start(), calls=%async_computation.11 | async-start | bytes 4718592 | tf_op jit(solution)/shard_map/reduce_scatter | solution.py:933
  305.2 151.3 %reduce-scatter.12.cloned.1.call-start = ((), (), s32[]{:S(2)}) async-start(), calls=%async_computation.12 | async-start | bytes 4718592 | tf_op jit(solution)/shard_map/reduce_scatter | solution.py:933
  354.8 237.9 %reduce-scatter.6.cloned.1.call-start = ((), (), s32[]{:S(2)}) async-start(), calls=%async_computation.9 | async-start | bytes 4718592 | tf_op jit(solution)/shard_map/reduce_scatter | solution.py:933
  445.5 149.5 %reduce-scatter.8.cloned.1.call-start = ((), (), s32[]{:S(2)}) async-start(), calls=%async_computation.10 | async-start | bytes 4718592 | tf_op jit(solution)/shard_map/reduce_scatter | solution.py:933
  448.9 271.1 %reduce-scatter.14.cloned.1.call-start = ((), (), s32[]{:S(2)}) async-start(), calls=%async_computation.13 | async-start | bytes 9437184 | tf_op jit(solution)/shard_map/reduce_scatter | solution.py:933
  453.1 42.6 %collective-permute-start.7 = (bf16[128,2048]{1,0:T(8,128)(2,1)}, bf16[128,2048]{1,0:T(8,128)(2,1)}, u32[]{:S(2)}, u32[]{:S(2)}) collective-permute-start(bf16[128,2048]{1,0:T(8,128)(2,1)} %get-tuple-element.85.refs_6_), channel_id=1, source_target_pairs={{0,8},{8,0},{16,24},{24,16},{1,9},{9,1},{17,25},{25,17},{2,10},{10... | collective-permute-start | bytes 1572872 | tf_op jit(solution)/shard_map/ppermute | solution.py:942
  453.6 46.3 %collective-permute-start.8 = (bf16[128,2048]{1,0:T(8,128)(2,1)}, bf16[128,2048]{1,0:T(8,128)(2,1)}, u32[]{:S(2)}, u32[]{:S(2)}) collective-permute-start(bf16[128,2048]{1,0:T(8,128)(2,1)} %get-tuple-element.85.refs_6_), channel_id=1, source_target_pairs={{0,16},{8,24},{16,0},{24,8},{1,17},{9,25},{17,1},{25,9},{2,18},{10... | collective-permute-start | bytes 1572872 | tf_op jit(solution)/shard_map/ppermute | solution.py:942
  455.4 48.0 %collective-permute-start.9 = (bf16[128,2048]{1,0:T(8,128)(2,1)}, bf16[128,2048]{1,0:T(8,128)(2,1)S(1)}, u32[]{:S(2)}, u32[]{:S(2)}) collective-permute-start(bf16[128,2048]{1,0:T(8,128)(2,1)} %get-tuple-element.85.refs_6_), channel_id=1, source_target_pairs={{0,24},{8,16},{16,8},{24,0},{1,25},{9,17},{17,9},{25,1},{2,26},{10... | collective-permute-start | bytes 1572872 | tf_op jit(solution)/shard_map/ppermute | solution.py:942
  460.0 39.0 %collective-permute-start.10 = (bf16[128,2048]{1,0:T(8,128)(2,1)}, bf16[128,2048]{1,0:T(8,128)(2,1)S(1)}, u32[]{:S(2)}, u32[]{:S(2)}) collective-permute-start(bf16[128,2048]{1,0:T(8,128)(2,1)} %get-tuple-element.88.refs_7_), channel_id=1, source_target_pairs={{0,8},{8,0},{16,24},{24,16},{1,9},{9,1},{17,25},{25,17},{2,10},{10... | collective-permute-start | bytes 1572872 | tf_op jit(solution)/shard_map/ppermute | solution.py:942
  460.6 42.7 %collective-permute-start.11 = (bf16[128,2048]{1,0:T(8,128)(2,1)}, bf16[128,2048]{1,0:T(8,128)(2,1)S(1)}, u32[]{:S(2)}, u32[]{:S(2)}) collective-permute-start(bf16[128,2048]{1,0:T(8,128)(2,1)} %get-tuple-element.88.refs_7_), channel_id=1, source_target_pairs={{0,16},{8,24},{16,0},{24,8},{1,17},{9,25},{17,1},{25,9},{2,18},{10... | collective-permute-start | bytes 1572872 | tf_op jit(solution)/shard_map/ppermute | solution.py:942
  481.7 17.3 %copy-start.3 = (bf16[2,512,1024]{2,1,0:T(8,128)(2,1)S(1)}, bf16[2,512,1024]{2,1,0:T(8,128)(2,1)}, u32[]{:S(2)}) copy-start(bf16[2,512,1024]{2,1,0:T(8,128)(2,1)} %copy-done.2) | copy-start | bytes 6291460
  495.7 26.6 %collective-permute-start.12 = (bf16[128,2048]{1,0:T(8,128)(2,1)S(1)}, bf16[128,2048]{1,0:T(8,128)(2,1)S(1)}, u32[]{:S(2)}, u32[]{:S(2)}) collective-permute-start(bf16[128,2048]{1,0:T(8,128)(2,1)S(1)} %copy-done.7), channel_id=1, source_target_pairs={{0,24},{8,16},{16,8},{24,0},{1,25},{9,17},{17,9},{25,1},{2,26},{10... | collective-permute-start | bytes 1572872 | tf_op jit(solution)/shard_map/ppermute | solution.py:942
  499.0 54.4 %collective-permute-start.13 = (bf16[2,512,1024]{2,1,0:T(8,128)(2,1)S(1)}, bf16[2,512,1024]{2,1,0:T(8,128)(2,1)}, u32[]{:S(2)}, u32[]{:S(2)}) collective-permute-start(bf16[2,512,1024]{2,1,0:T(8,128)(2,1)S(1)} %copy-done.3), channel_id=1, source_target_pairs={{0,8},{8,0},{16,24},{24,16},{1,9},{9,1},{17,25},{25,17},{2,10},{10... | collective-permute-start | bytes 6291464 | tf_op jit(solution)/shard_map/ppermute | solution.py:942
  499.9 53.4 %collective-permute-start.14 = (bf16[2,512,1024]{2,1,0:T(8,128)(2,1)S(1)}, bf16[2,512,1024]{2,1,0:T(8,128)(2,1)}, u32[]{:S(2)}, u32[]{:S(2)}) collective-permute-start(bf16[2,512,1024]{2,1,0:T(8,128)(2,1)S(1)} %get-tuple-element.90.refs_1_), channel_id=1, source_target_pairs={{0,16},{8,24},{16,0},{24,8},{1,17},{9,25},{17,1},{25,9},{2,18},{10... | collective-permute-start | bytes 6291464 | tf_op jit(solution)/shard_map/ppermute | solution.py:942
  586.8 46.8 %collective-permute-start.15 = (bf16[2,512,1024]{2,1,0:T(8,128)(2,1)}, bf16[2,512,1024]{2,1,0:T(8,128)(2,1)S(1)}, u32[]{:S(2)}, u32[]{:S(2)}) collective-permute-start(bf16[2,512,1024]{2,1,0:T(8,128)(2,1)} %get-tuple-element.99), channel_id=1, source_target_pairs={{0,8},{8,0},{16,24},{24,16},{1,9},{9,1},{17,25},{25,17},{2,10},{10... | collective-permute-start | bytes 6291464 | tf_op jit(solution)/shard_map/ppermute | solution.py:942
  588.2 46.5 %collective-permute-start.16 = (bf16[2,512,1024]{2,1,0:T(8,128)(2,1)}, bf16[2,512,1024]{2,1,0:T(8,128)(2,1)}, u32[]{:S(2)}, u32[]{:S(2)}) collective-permute-start(bf16[2,512,1024]{2,1,0:T(8,128)(2,1)} %get-tuple-element.100), channel_id=1, source_target_pairs={{0,16},{8,24},{16,0},{24,8},{1,17},{9,25},{17,1},{25,9},{2,18},{10... | collective-permute-start | bytes 6291464 | tf_op jit(solution)/shard_map/ppermute | solution.py:942
  633.6 12.5 %copy-start.4 = (bf16[2,512,1024]{2,1,0:T(8,128)(2,1)}, bf16[2,512,1024]{2,1,0:T(8,128)(2,1)S(1)}, u32[]{:S(2)}) copy-start(bf16[2,512,1024]{2,1,0:T(8,128)(2,1)S(1)} %collective-permute-done.15.refs_0_.refs_6_) | copy-start | bytes 6291460
  721.0 4.0 collective-permute-start.17
  (50 other events, 168.3 us)
Sparse Core Ops, SparseCore 0:
  112.2 48.6 all-gather.4
  162.5 45.8 all-gather.8
  210.0 45.8 all-gather.6
  257.9 46.2 all-gather.10
  306.3 48.7 reduce-scatter.9
  357.3 48.1 reduce-scatter.11
  445.6 47.8 reduce-scatter.5
  495.8 48.1 reduce-scatter.7
  581.4 87.1 reduce-scatter.13

commit v5 on v4

--- a/solution.py
+++ b/solution.py
@@ -518,10 +518,12 @@
 
 
 class Halving:
-    def __init__(self, n, me, source, blocks, got, send, recv, out, first=None):
+    def __init__(
+        self, n, me, source, blocks, got, send, recv, out, first=None, acc=None, kept=None
+    ):
         self.n, self.me, self.source, self.blocks, self.got = n, me, source, blocks, got
         self.send, self.recv, self.out = send, recv, out
-        self.first = first
+        self.first, self.acc, self.kept = first, out if acc is None else acc, kept
         bits = list(range(n.bit_length() - 1))
         self.own = out.shape[0]
         self.orders = [bits if j % 2 == 0 else bits[::-1] for j in range(self.own)]
@@ -532,7 +534,8 @@
         return flip(self.me, self.masks[j][k])
 
     def slot(self, s, k):
-        return self.n - (self.n >> s) + k - (self.n >> (s + 1))
+        made = 0 if self.first is None else self.n >> 1
+        return self.n - (self.n >> s) + k - (self.n >> (s + 1)) - made
 
     def copy(self, j, s, k):
         given = self.source is not None and s == 0
@@ -566,7 +569,7 @@
 
     def rest(self, value=None):
         for j in range(self.own):
-            self.out[j] = self.source[j, self.me].astype(F32) if value is None else value(j, self.me)
+            self.acc[j] = self.source[j, self.me].astype(F32) if value is None else value(j, self.me)
 
     def arrived(self, j, k, steps):
         total = None
@@ -583,13 +586,15 @@
     def pass_on(self):
         for s in range(1, self.steps):
             for j, k in self.going(s):
-                total = self.blocks[j, k - 1].astype(F32) + self.arrived(j, k, s)
+                mine = self.blocks[j, k - 1] if self.kept is None else self.kept[j, k]
+                total = mine.astype(F32) + self.arrived(j, k, s)
                 self.blocks[j, k - 1] = total.astype(BF16)
                 self.copy(j, s, k).start()
 
     def finish(self):
         for j in range(self.own):
-            self.out[j] += self.arrived(j, 0, self.steps)
+            mine = self.acc[j] if self.kept is None else self.kept[j, 0].astype(F32)
+            self.out[j] = (mine + self.arrived(j, 0, self.steps)).astype(self.out.dtype)
         for s in range(0 if self.first is None else 1, self.steps):
             for j, k in self.going(s):
                 self.copy(j, s, k).wait_send()
@@ -630,7 +635,7 @@
     out, ys, scratch = refs[0], refs[1 : 1 + halves], refs[1 + halves :]
     me = lax.axis_index("ctx")
     meet(ctx_peers(n, me))
-    sums = Halving(n, me, None, *scratch, out)
+    sums = Halving(n, me, None, *scratch[:4], out, acc=scratch[4])
     value = product(hid, grad, hid[0].shape[2] // n)
     sums.begin(value)
     sums.rest(value)
@@ -647,27 +652,32 @@
 
 
 def gate_kernel(n, halves, *refs):
-    mids, pres = refs[:halves], refs[halves : 2 * halves]
-    partial, out, dxn = refs[2 * halves], refs[-10], refs[-9]
-    first = refs[2 * halves + 1 : 2 * halves + 1 + out.shape[0]]
+    mids, gate_pres, up_pres = [refs[k * halves : (k + 1) * halves] for k in range(3)]
+    own = gate_pres[0].shape[0]
+    partial, first = refs[3 * halves], refs[3 * halves + 1 : 3 * halves + 1 + own]
+    out, dxn, kept = refs[-12:-9]
     me = lax.axis_index("ctx")
     meet(ctx_peers(n, me))
-    rows = Halving(n, me, partial, *refs[-8:-4], dxn)
+    rows = Halving(n, me, partial, *refs[-9:-5], dxn)
     rows.begin()
-    sums = Halving(n, me, None, *refs[-4:], out, first)
-    value = product(mids, pres, mids[0].shape[1] // n)
+    block = mids[0].shape[1] // n
+    sums = Halving(n, me, None, *refs[-5:-1], out, first, refs[-1])
+    value = product(mids, gate_pres, block)
     sums.begin(value)
     sums.pass_on()
     rows.pass_on()
     sums.rest(value)
     rows.rest()
+    value = product(mids, up_pres, block)
+    for k in range(n // 2):
+        for j in range(own):
+            kept[j, k] = value(j, sums.target(j, k)).astype(BF16)
     rows.finish()
     sums.finish()
 
 
-def up_kernel(n, halves, *refs):
-    mids, pres = refs[:halves], refs[halves : 2 * halves]
-    piece, x = refs[2 * halves], refs[2 * halves + 1]
+def up_kernel(n, *refs):
+    piece, x, kept = refs[:3]
     out, *whole = refs[-16:-11]
     small_out, slots, send, recv = refs[-11:-7]
     me = lax.axis_index("ctx")
@@ -696,13 +706,11 @@
             )
         return copies
 
-    first = refs[2 * halves + 2 : 2 * halves + 2 + out.shape[0]]
-    sums = Halving(n, me, None, *refs[-4:], out, first)
+    first = refs[3 : 3 + kept.shape[0]]
+    sums = Halving(n, me, None, *refs[-4:], out, first, kept=kept)
     for i in range(2):
         for copy in doubling(i, 0):
             copy.start()
-    value = product(mids, pres, mids[0].shape[1] // n)
-    sums.begin(value)
     sums.pass_on()
     smalls.pass_on()
     slots[me] = piece[...]
@@ -712,7 +720,6 @@
                 copy.wait_recv()
             for copy in doubling(i, s):
                 copy.start()
-    sums.rest(value)
     smalls.finish(small_out)
     sums.finish()
     for i in range(2):
@@ -724,7 +731,7 @@
     cols = piece.shape[1] // len(whole)
     for c in range(n):
         for k, ref in enumerate(whole):
-            ref[:, c * cols : (c + 1) * cols] = slots[c, :, k * cols : (k + 1) * cols].astype(F32)
+            ref[:, c * cols : (c + 1) * cols] = slots[c, :, k * cols : (k + 1) * cols]
 
 
 class Doubling:
@@ -881,47 +888,49 @@
 def down_sums(hid, grad, w_down):
     n, halves = lax.axis_size("ctx"), len(hid)
     own, ff, width = w_down.shape
-    outs = [jax.ShapeDtypeStruct((own, ff // n, width), F32)]
+    outs = [jax.ShapeDtypeStruct((own, ff // n, width), BF16)]
     outs += [jax.ShapeDtypeStruct((h.shape[1], width), BF16) for h in hid]
     return exchange(
         functools.partial(down_kernel, n, halves), 3, [*hid, *grad, w_down], (), outs,
-        Halving.scratch(own, n, ff // n, width),
-    )
-
-
-def gate_sums(mids, pres, partial, first, earlier):
+        Halving.scratch(own, n, ff // n, width) + [pltpu.VMEM((own, ff // n, width), F32)],
+    )
+
+
+def gate_sums(mids, gate_pres, up_pres, partial, first, earlier):
     n, halves = lax.axis_size("ctx"), len(mids)
-    own, _, ff = pres[0].shape
+    own, _, ff = gate_pres[0].shape
     rows = mids[0].shape[1] // n
     shape = partial.shape
     outs = [
-        jax.ShapeDtypeStruct((own, rows, ff), F32),
+        jax.ShapeDtypeStruct((own, rows, ff), BF16),
         jax.ShapeDtypeStruct((shape[0],) + shape[2:], F32),
+        jax.ShapeDtypeStruct((own, n // 2, rows, ff), BF16),
     ]
     return exchange(
-        functools.partial(gate_kernel, n, halves), 4, [*mids, *pres, partial, *first], earlier, outs,
-        Halving.scratch(shape[0], n, *shape[2:]) + Halving.scratch(own, n, rows, ff),
-    )
-
-
-def up_sums(mids, pres, piece, smalls, first, earlier):
-    n, halves = lax.axis_size("ctx"), len(mids)
-    own, _, ff = pres[0].shape
-    rows = mids[0].shape[1] // n
+        functools.partial(gate_kernel, n, halves), 4,
+        [*mids, *gate_pres, *up_pres, partial, *first], earlier, outs,
+        Halving.scratch(shape[0], n, *shape[2:])
+        + Halving.scratch(own, n // 2, rows, ff)
+        + [pltpu.VMEM((own, rows, ff), F32)],
+    )
+
+
+def up_sums(kept, first, piece, smalls):
+    n = lax.axis_size("ctx")
+    own, _, rows, ff = kept.shape
     shard, width = piece.shape
-    outs = [jax.ShapeDtypeStruct((own, rows, ff), F32)]
-    outs += [jax.ShapeDtypeStruct((shard, n * width // 4), F32) for _ in range(4)]
+    outs = [jax.ShapeDtypeStruct((own, rows, ff), BF16)]
+    outs += [jax.ShapeDtypeStruct((shard, n * width // 4), BF16) for _ in range(4)]
     outs += [jax.ShapeDtypeStruct(smalls.shape[1:], F32)]
     return exchange(
-        functools.partial(up_kernel, n, halves), 5, [*mids, *pres, piece, smalls, *first], earlier,
-        outs,
+        functools.partial(up_kernel, n), 5, [piece, smalls, kept, *first], (), outs,
         [
             pltpu.VMEM((n,) + piece.shape, BF16),
             pltpu.SemaphoreType.DMA((2, n - 1)),
             pltpu.SemaphoreType.DMA((2, n - 1)),
         ]
         + SmallSum.scratch(n, smalls.shape)
-        + Halving.scratch(own, n, rows, ff),
+        + Halving.scratch(own, n // 2, rows, ff),
     )
 
 
@@ -991,14 +1000,10 @@
         span_order, c_at * rows + jnp.arange(rows, dtype=jnp.int32), rows // 2
     )
     valid = (my_positions < seq_length).astype(F32)[:, None]
-    member = jnp.sum(
-        (routes[0][:, None, :] == jnp.arange(experts, dtype=jnp.int32)[None, :, None]).astype(BF16),
-        axis=2,
-    )
     small = jnp.concatenate(
         [
             w_router.reshape(-1), gain_attn, gain_query, gain_key, gain_mlp,
-            member.reshape(-1),
+            routes[0].astype(BF16).reshape(-1),
         ]
     )
     used = small.shape[0]
@@ -1019,8 +1024,8 @@
         gains.append(small_all[:, at : at + shard].reshape(width).astype(F32))
         at += shard
     attn_gain, query_gain_all, key_gain_all, mlp_gain = gains
-    member_all = small_all[:, at:].reshape(n_exp, rows, experts)
-    member_all = jnp.pad(member_all, ((0, 0), (0, 0), (0, LANES - experts)))
+    routes_all = small_all[:, at:].reshape(n_exp, rows, routes.shape[2])
+    lane = jnp.arange(LANES, dtype=jnp.int32)[None, :]
     query_gain = take(query_gain_all, c_at * cols, cols)
     key_gain = take(key_gain_all, c_at * cols, cols)
 
@@ -1066,12 +1071,14 @@
         scale_parts.append(scale)
         mids.append(gather(mid, "exp"))
 
-    lane = jnp.arange(LANES, dtype=jnp.int32)[None, :]
     pick = (lane == e_at * own + jnp.arange(max(own, 8), dtype=jnp.int32)[:, None]).astype(F32)
     hid_parts, da_parts, db_parts, coef_parts = [], [], [], []
     dxs = []
     for h in range(halves):
-        member_h = member_all[:, h * part : (h + 1) * part].reshape(n_exp * part, LANES)
+        named = routes_all[:, h * part : (h + 1) * part].reshape(n_exp * part, -1)
+        member_h = sum(
+            (named[:, k : k + 1] == lane.astype(BF16)).astype(BF16) for k in range(named.shape[1])
+        )
         hid, da, db, dx, coef = expert_pass(
             mids[h], d_hid_parts[h], member_h, router_w, pick, w_gate, w_up, experts
         )
@@ -1137,11 +1144,9 @@
     g_query_gain = jnp.sum(dq_n * qp * q_scale, axis=0)
     g_key_gain = jnp.sum(dk_n * kp * k_scale, axis=0)
     d_qkv = jnp.concatenate([dqp.astype(BF16), dkp.astype(BF16), dv.astype(BF16)], axis=1)
-    g_mine = attention_grads(xn, d_qkv, attended_parts, dl_parts, cols, ())
-    partial = input_partial(d_qkv, weights, part, first_up)
-    g_gate, dxn = gate_sums(
-        mids, da_parts, partial, first_gate, (g_mine,)
-    )
+    partial = input_partial(d_qkv, weights, part, ())
+    g_mine = attention_grads(xn, d_qkv, attended_parts, dl_parts, cols, (partial, *first_up))
+    g_gate, dxn, kept_up = gate_sums(mids, da_parts, db_parts, partial, first_gate, (g_mine,))
     dxn = jnp.concatenate([dxn[0], dxn[1]], axis=1)
     block_input = tokens[0].astype(F32)
     in_scale = rms_scale(block_input)
@@ -1159,13 +1164,13 @@
     spare = -(experts + 4) % 8
     smalls = jnp.concatenate([g_router] + gain_grads + [jnp.zeros((spare, width), F32)], axis=0)
     smalls = smalls.reshape(-1, n_exp, shard).transpose(1, 0, 2)
-    g_up, *g_full, smalls = up_sums(mids, db_parts, g_mine, smalls, first_up, (g_gate,))
+    g_up, *g_full, smalls = up_sums(kept_up, first_up, g_mine, smalls)
     return (
         mixed[None], d_tokens[None],
-        *g_full,
+        *[g.astype(F32) for g in g_full],
         smalls[:experts].T,
         smalls[experts], smalls[experts + 2], smalls[experts + 3], smalls[experts + 1],
-        g_gate, g_up, g_down,
+        g_gate.astype(F32), g_up.astype(F32), g_down.astype(F32),
     )
 
 

time: 852 us -> 832 us (0.977)
  local copies, waits for them, and re-layouts: 77.5 us -> 60.3 us
  other arithmetic: 52.2 us -> 68.6 us
  waiting for transfers between devices: 50.3 us -> 37.2 us
    unnamed x127 -> x134, local copies, waits for them, and re-layouts: 36.8 us -> 18.4 us
    convert_element_type x0 -> x9, other arithmetic: none -> 17.9 us  [the longest x4 6.24 us: local(): g.astype(F32)]
  transfers between devices with their start and end apart: 27 -> 27, of which waited for: 4 -> 3; matrix products, arithmetic and copies ran while one was open for 18% -> 19% of each run, Pallas kernels for 46% -> 48%
where the time goes in v5:
time: 832 us; the launch traced here: 824 us
  Pallas kernels  558 us (67%)
  other arithmetic  68.6 us (8%)
  matrix products  62.8 us (8%)
  local copies, waits for them, and re-layouts  60.3 us (7%)
  waiting for transfers between devices  37.2 us (4%)
  starting transfers between devices  21.2 us (3%)
  between operations  15.8 us (2%)
    pallas_call x3, Pallas kernels, exchange(): pl.pallas_call(kernel, in_specs=[VMEM] * len(operands) + [ANY] * len(earl...  243 us
    pallas_call x2, Pallas kernels, expert_pass(): pl.pallas_call(functools.partial(expert_kernel, experts, own, 512), grid=...  98.4 us
    pallas_call x1, Pallas kernels, gather_start(): pl.pallas_call(functools.partial(start_kernel, n_ctx, n_exp), in_specs=[A...  82.5 us
    ppermute x16, waiting for transfers between devices, swap(): return lax.ppermute(block, 'ctx', [(i, i ^ bits) for i in range(n)])  37 us
    dot_general x6, matrix products, mm_t(): lax.dot_general(left, right, (((1,), (1,)), ((), ())), preferred_element_...  35 us
    pallas_call x2, Pallas kernels, attend_back(): pl.pallas_call(attend_back_kernel, grid=(heads,), in_specs=attention_spec...  28.1 us
    pallas_call x2, Pallas kernels, given_grads(): pl.pallas_call(functools.partial(give_kernel, n, len(rights)), grid_spec=...  27.9 us
    dot_general x9, matrix products, mm(): return jnp.dot(left, right, preferred_element_type=F32)  23.5 us
  transfers between devices with their start and end apart: 27, of which 3 were waited for; matrix products, arithmetic and copies ran while one was open for 19% of the time, Pallas kernels for 48%

profile of v5, /device:TPU:0, one launch (start us, length us, event | category | flops | bytes accessed | tf_op | source)
XLA Modules:
  0.0 823.7 jit_solution(9133508989265422840)
XLA Ops:
  15.7 4.8 select_reduce_fusion.1
  24.5 82.5 %shard_map.290 = (bf16[8,256,2048]{2,1,0:T(8,128)(2,1)}, bf16[2,4,128,2048]{3,2,1,0:T(8,128)(2,1)}, bf16[8,64,128]{2,1,0:T(8,128)(2,1)}) custom-call(bf16[256,2048]{1,0:T(8,128)(2,1)} %pad_maximum_fusion.4.w_ref, bf16[2,128,2048]{2,1,0:T(8,128)(2,1)} %bitcast.197, bf16[64,128]{1,0:T(8,128)(2,1)} %pad_bitcast_fusion.small_ref), custom_call_target="tpu_custom_call" | custom-call | tf_op jit(solution)/shard_map/pallas_call | solution.py:825
  112.5 5.3 select_reduce_fusion
  130.7 10.3 %fusion.2.q_ref.k_ref.v_ref = f32[1024,1536]{1,0:T(8,128)S(1)} fusion(bf16[1024,2048]{1,0:T(8,128)(2,1)S(1)} %fusion.1.x_ref, bf16[2048,2048]{1,0:T(8,128)(2,1)} %bitcast.195), kind=kOutput, calls=%fused_computation.4 | convolution fusion | flops 6442450944 | bytes 16777216 | tf_op jit(solution)/shard_map/dot_general | solution.py:24
  144.7 10.7 %shard_map.291 = f32[8,1024]{1,0:T(8,128)} custom-call(f32[8,1024]{1,0:T(8,128)} %select_maximum_fusion.1.x_ref), custom_call_target="tpu_custom_call" | custom-call | tf_op jit(solution)/shard_map/pallas_call | solution.py:434
  156.9 4.2 copy.40
  161.1 9.7 %shard_map.292.refs_0_ = bf16[512,512]{1,0:T(8,128)(2,1)S(1)} custom-call(f32[1024,1536]{1,0:T(8,128)} %copy-done.16, f32[1024,1536]{1,0:T(8,128)} %copy-done.16, f32[1024,1536]{1,0:T(8,128)} %copy-done.16, f32[1024,1]{1,0:T(8,128)S(1)} %copy.38.qs_ref, f32[1024,1]{1,0:T(8,128)S(1)} %copy.39.ks_ref, f32[1,512]{1,0:T(1,128)S(1)} %bitcast.173, ...), custom_call_target="tpu_custom_call" | custom-call | flops 1073741824 | bytes 8388608 | tf_op jit(solution)/shard_map/pallas_call | solution.py:125
  181.5 8.2 convert_bitcast_fusion.3
  189.8 7.5 convert_bitcast_fusion.4
  203.8 9.7 %shard_map.296.refs_1_ = bf16[512,512]{1,0:T(8,128)(2,1)S(1)} custom-call(f32[1024,1536]{1,0:T(8,128)} %copy-done.16, f32[1024,1536]{1,0:T(8,128)} %copy-done.16, f32[1024,1536]{1,0:T(8,128)} %copy-done.16, f32[1024,1]{1,0:T(8,128)S(1)} %copy.38.qs_ref, f32[1024,1]{1,0:T(8,128)S(1)} %copy.39.ks_ref, f32[1,512]{1,0:T(1,128)S(1)} %bitcast.174, ...), custom_call_target="tpu_custom_call" | custom-call | flops 1073741824 | bytes 8388608 | tf_op jit(solution)/shard_map/pallas_call | solution.py:125
  223.6 8.2 convert_bitcast_fusion.1
  231.8 7.0 convert_bitcast_fusion.2
  255.9 49.1 %shard_map.295 = (bf16[2,1024,1024]{2,1,0:T(8,128)(2,1)}, bf16[2,1024,1024]{2,1,0:T(8,128)(2,1)}, bf16[2,1024,1024]{2,1,0:T(8,128)(2,1)}, bf16[1024,2048]{1,0:T(8,128)(2,1)}, bf16[1024,128]{1,0:T(8,128)(2,1)}) custom-call(bf16[1024,2048]{1,0:T(8,128)(2,1)} %all-gather.7.cloned.1.call-done.x_ref.refs_0_, ...), custom_call_target="tpu_custom_call" | custom-call | flops 34359738368 | bytes 41943040 | tf_op jit(solution)/shard_map/pallas_call | solution.py:230
  305.0 49.3 %shard_map.298 = (bf16[2,1024,1024]{2,1,0:T(8,128)(2,1)}, bf16[2,1024,1024]{2,1,0:T(8,128)(2,1)}, bf16[2,1024,1024]{2,1,0:T(8,128)(2,1)}, bf16[1024,2048]{1,0:T(8,128)(2,1)}, bf16[1024,128]{1,0:T(8,128)(2,1)}) custom-call(bf16[1024,2048]{1,0:T(8,128)(2,1)} %all-gather.11.cloned.1.call-done.x_ref.refs_1_, ...), custom_call_target="tpu_custom_call" | custom-call | flops 34359738368 | bytes 41943040 | tf_op jit(solution)/shard_map/pallas_call | solution.py:230
  354.8 89.2 %shard_map.299 = (bf16[2,256,2048]{2,1,0:T(8,128)(2,1)}, bf16[1024,2048]{1,0:T(8,128)(2,1)}, bf16[1024,2048]{1,0:T(8,128)(2,1)}) custom-call(bf16[2,1024,1024]{2,1,0:T(8,128)(2,1)} %get-tuple-element.70.refs_0_, bf16[2,1024,1024]{2,1,0:T(8,128)(2,1)} %get-tuple-element.72.refs_1_, bf16[1024,2048]{1,0:T(8,128)(2,1)} %all-gather.5.cloned.1.call-done.refs_2_, ...), custom_call_target="tpu_custom_call" | custom-call | tf_op jit(solution)/shard_map/pallas_call | solution.py:876
  447.8 3.5 shard_map.300
  454.8 3.5 shard_map.301
  463.4 13.9 %shard_map.302 = (bf16[2,512,1024]{2,1,0:T(8,128)(2,1)S(1)}, bf16[2,512,1024]{2,1,0:T(8,128)(2,1)S(1)}) custom-call(s32[2]{0:T(128)S(1)} %get-tuple-element.186.table, bf16[1024,2048]{1,0:T(8,128)(2,1)} %all-gather.7.cloned.1.call-done.x_ref.refs_0_, bf16[1024,2048]{1,0:T(8,128)(2,1)} %all-gather.11.cloned.1.call-done.x_ref.refs_1_, ...), custom_call_target="tpu_custom_call" | custom-call | tf_op jit(solution)/shard_map/pallas_call | solution.py:331
  479.9 14.0 %shard_map.303 = (bf16[2,512,1024]{2,1,0:T(8,128)(2,1)S(1)}, bf16[2,512,1024]{2,1,0:T(8,128)(2,1)S(1)}) custom-call(s32[2]{0:T(128)S(1)} %get-tuple-element.185.table, bf16[1024,2048]{1,0:T(8,128)(2,1)} %all-gather.7.cloned.1.call-done.x_ref.refs_0_, bf16[1024,2048]{1,0:T(8,128)(2,1)} %all-gather.11.cloned.1.call-done.x_ref.refs_1_, ...), custom_call_target="tpu_custom_call" | custom-call | tf_op jit(solution)/shard_map/pallas_call | solution.py:331
  506.8 13.7 %shard_map.304 = (f32[512,512]{1,0:T(8,128)S(1)}, f32[1024,512]{1,0:T(8,128)}, f32[1024,512]{1,0:T(8,128)}) custom-call(f32[1024,1536]{1,0:T(8,128)} %copy-done.16, f32[1024,1536]{1,0:T(8,128)} %copy-done.16, f32[1024,1536]{1,0:T(8,128)} %copy-done.16, f32[1024,1]{1,0:T(8,128)S(1)} %copy.38.qs_ref, f32[1024,1]{1,0:T(8,128)S(1)} %copy.39.ks_ref, ...), custom_call_target="tpu_custom_call" | custom-call | flops 2684354560 | bytes 16777216 | tf_op jit(solution)/shard_map/pallas_call | solution.py:143
  523.1 14.4 %shard_map.305 = (f32[512,512]{1,0:T(8,128)S(1)}, f32[1024,512]{1,0:T(8,128)}, f32[1024,512]{1,0:T(8,128)}) custom-call(f32[1024,1536]{1,0:T(8,128)} %copy-done.16, f32[1024,1536]{1,0:T(8,128)} %copy-done.16, f32[1024,1536]{1,0:T(8,128)} %copy-done.16, f32[1024,1]{1,0:T(8,128)S(1)} %copy.38.qs_ref, f32[1024,1]{1,0:T(8,128)S(1)} %copy.39.ks_ref, ...), custom_call_target="tpu_custom_call" | custom-call | flops 2684354560 | bytes 16777216 | tf_op jit(solution)/shard_map/pallas_call | solution.py:143
  542.9 8.7 %collective-permute-done.14.refs_1_.refs_8_ = bf16[2,512,1024]{2,1,0:T(8,128)(2,1)} collective-permute-done((bf16[2,512,1024]{2,1,0:T(8,128)(2,1)S(1)}, bf16[2,512,1024]{2,1,0:T(8,128)(2,1)}, u32[]{:S(2)}, u32[]{:S(2)}) %collective-permute-start.14) | collective-permute-done | bytes 2097184 | tf_op jit(solution)/shard_map/ppermute | solution.py:951
  551.6 6.8 shard_map.306.refs_2_
  563.2 3.4 subtract_convert_fusion.1
  566.9 11.3 %shard_map.307.refs_4_.refs_6_ = bf16[2,4,256,1024]{3,2,1,0:T(8,128)(2,1)} custom-call(bf16[1024,1536]{1,0:T(8,128)(2,1)S(1)} %pad_maximum_fusion.2.d_ref, bf16[2048,2048]{1,0:T(8,128)(2,1)} %bitcast.196), custom_call_target="tpu_custom_call" | custom-call | tf_op jit(solution)/shard_map/pallas_call | solution.py:305
  578.2 27.3 %collective-permute-done.15.refs_5_.refs_3_ = bf16[2,512,1024]{2,1,0:T(8,128)(2,1)S(1)} collective-permute-done((bf16[2,512,1024]{2,1,0:T(8,128)(2,1)}, bf16[2,512,1024]{2,1,0:T(8,128)(2,1)S(1)}, u32[]{:S(2)}, u32[]{:S(2)}) %collective-permute-start.15) | collective-permute-done | bytes 2097184 | tf_op jit(solution)/shard_map/ppermute | solution.py:951
  608.1 13.6 %shard_map.309.refs_9_ = bf16[2048,2048]{1,0:T(8,128)(2,1)} custom-call(bf16[1024,2048]{1,0:T(8,128)(2,1)} %copy-done.26, bf16[1024,1536]{1,0:T(8,128)(2,1)} %copy-done.4, bf16[512,512]{1,0:T(8,128)(2,1)S(1)} %copy-done.13, bf16[512,512]{1,0:T(8,128)(2,1)S(1)} %copy-done.15, bf16[512,2048]{1,0:T(8,128)(2,1)} %bitcast.47.refs_2_, ...), custom_call_target="tpu_custom_call" | custom-call | flops 8589934592 | bytes 20971520 | tf_op jit(solution)/shard_map/pallas_call | solution.py:275
  623.2 3.6 fusion.139
  636.0 72.6 %shard_map.310 = (bf16[2,512,1024]{2,1,0:T(8,128)(2,1)}, f32[2,256,1024]{2,1,0:T(8,128)}, bf16[2,2,512,1024]{3,2,1,0:T(8,128)(2,1)}) custom-call(bf16[1024,2048]{1,0:T(8,128)(2,1)} %all-gather.7.cloned.1.call-done.x_ref.refs_0_, bf16[1024,2048]{1,0:T(8,128)(2,1)} %all-gather.11.cloned.1.call-done.x_ref.refs_1_, ...), custom_call_target="tpu_custom_call" | custom-call | tf_op jit(solution)/shard_map/pallas_call | solution.py:876
  708.7 4.2 convert_element_type.338
  722.6 81.1 %shard_map.311 = (bf16[2,512,1024]{2,1,0:T(8,128)(2,1)}, bf16[256,2048]{1,0:T(8,128)(2,1)}, bf16[256,2048]{1,0:T(8,128)(2,1)}, bf16[256,2048]{1,0:T(8,128)(2,1)}...) custom-call(bf16[256,2048]{1,0:T(8,128)(2,1)} %pad_maximum_fusion.5.refs_0_, f32[8,24,256]{2,1,0:T(8,128)} %bitcast.204, ...), custom_call_target="tpu_custom_call" | custom-call | tf_op jit(solution)/shard_map/pallas_call | solution.py:876
  806.5 4.2 convert_element_type.339
  (314 shorter events, 152.4 us)
Async XLA Ops:
  7.2 174.3 %all-gather.5.cloned.1.call-start = ((), (), s32[]{:S(2)}) async-start(), calls=%async_computation.5 | async-start | bytes 4718592 | tf_op jit(solution)/shard_map/all_gather | solution.py:938
  8.4 15.0 %collective-permute-start = (bf16[256,512]{1,0:T(8,128)(2,1)S(1)}, bf16[256,512]{1,0:T(8,128)(2,1)S(1)}, u32[]{:S(2)}, u32[]{:S(2)}) collective-permute-start(bf16[256,512]{1,0:T(8,128)(2,1)S(1)} %constant_dynamic-slice_fusion), channel_id=1, source_target_pairs={{0,0},{1,1},{8,2},{9,3},{16,4},{17,5},{24,6},{25,7},{2,8},{3,9},{1... | collective-permute-start | bytes 786440 | tf_op jit(solution)/shard_map/ppermute | solution.py:994
  111.8 111.9 %all-gather.9.cloned.1.call-start = ((), (), s32[]{:S(2)}) async-start(), calls=%async_computation.7 | async-start | bytes 4718592 | tf_op jit(solution)/shard_map/all_gather | solution.py:938
  127.2 128.6 %all-gather.7.cloned.1.call-start = ((), (), s32[]{:S(2)}) async-start(), calls=%async_computation.6 | async-start | bytes 4718592 | tf_op jit(solution)/shard_map/all_gather | solution.py:938
  172.4 27.1 %collective-permute-start.3 = (bf16[128,2048]{1,0:T(8,128)(2,1)}, bf16[128,2048]{1,0:T(8,128)(2,1)S(1)}, u32[]{:S(2)}, u32[]{:S(2)}) collective-permute-start(bf16[128,2048]{1,0:T(8,128)(2,1)} %convolution_convert_fusion.3), channel_id=1, source_target_pairs={{0,8},{8,0},{16,24},{24,16},{1,9},{9,1},{17,25},{25,17},{2,10},{10... | collective-permute-start | bytes 1572872 | tf_op jit(solution)/shard_map/ppermute | solution.py:951
  174.6 25.0 %collective-permute-start.2 = (bf16[128,2048]{1,0:T(8,128)(2,1)}, bf16[128,2048]{1,0:T(8,128)(2,1)}, u32[]{:S(2)}, u32[]{:S(2)}) collective-permute-start(bf16[128,2048]{1,0:T(8,128)(2,1)} %convolution_convert_fusion.4), channel_id=1, source_target_pairs={{0,16},{8,24},{16,0},{24,8},{1,17},{9,25},{17,1},{25,9},{2,18},{10... | collective-permute-start | bytes 1572872 | tf_op jit(solution)/shard_map/ppermute | solution.py:951
  177.6 22.0 %collective-permute-start.1 = (bf16[128,2048]{1,0:T(8,128)(2,1)}, bf16[128,2048]{1,0:T(8,128)(2,1)}, u32[]{:S(2)}, u32[]{:S(2)}) collective-permute-start(bf16[128,2048]{1,0:T(8,128)(2,1)} %convolution_convert_fusion.5), channel_id=1, source_target_pairs={{0,24},{8,16},{16,8},{24,0},{1,25},{9,17},{17,9},{25,1},{2,26},{10... | collective-permute-start | bytes 1572872 | tf_op jit(solution)/shard_map/ppermute | solution.py:951
  203.7 101.2 %all-gather.11.cloned.1.call-start = ((), (), s32[]{:S(2)}) async-start(), calls=%async_computation.8 | async-start | bytes 4718592 | tf_op jit(solution)/shard_map/all_gather | solution.py:938
  215.2 26.1 %collective-permute-start.6 = (bf16[128,2048]{1,0:T(8,128)(2,1)}, bf16[128,2048]{1,0:T(8,128)(2,1)S(1)}, u32[]{:S(2)}, u32[]{:S(2)}) collective-permute-start(bf16[128,2048]{1,0:T(8,128)(2,1)} %convolution_convert_fusion), channel_id=1, source_target_pairs={{0,8},{8,0},{16,24},{24,16},{1,9},{9,1},{17,25},{25,17},{2,10},{10... | collective-permute-start | bytes 1572872 | tf_op jit(solution)/shard_map/ppermute | solution.py:951
  217.3 24.0 %collective-permute-start.5 = (bf16[128,2048]{1,0:T(8,128)(2,1)}, bf16[128,2048]{1,0:T(8,128)(2,1)}, u32[]{:S(2)}, u32[]{:S(2)}) collective-permute-start(bf16[128,2048]{1,0:T(8,128)(2,1)} %convolution_convert_fusion.1), channel_id=1, source_target_pairs={{0,16},{8,24},{16,0},{24,8},{1,17},{9,25},{17,1},{25,9},{2,18},{10... | collective-permute-start | bytes 1572872 | tf_op jit(solution)/shard_map/ppermute | solution.py:951
  220.3 21.0 %collective-permute-start.4 = (bf16[128,2048]{1,0:T(8,128)(2,1)}, bf16[128,2048]{1,0:T(8,128)(2,1)}, u32[]{:S(2)}, u32[]{:S(2)}) collective-permute-start(bf16[128,2048]{1,0:T(8,128)(2,1)} %convolution_convert_fusion.2), channel_id=1, source_target_pairs={{0,24},{8,16},{16,8},{24,0},{1,25},{9,17},{17,9},{25,1},{2,26},{10... | collective-permute-start | bytes 1572872 | tf_op jit(solution)/shard_map/ppermute | solution.py:951
  245.4 202.4 %reduce-scatter.10.cloned.1.call-start = ((), (), s32[]{:S(2)}) async-start(), calls=%async_computation.11 | async-start | bytes 4718592 | tf_op jit(solution)/shard_map/reduce_scatter | solution.py:942
  305.0 149.9 %reduce-scatter.12.cloned.1.call-start = ((), (), s32[]{:S(2)}) async-start(), calls=%async_computation.12 | async-start | bytes 4718592 | tf_op jit(solution)/shard_map/reduce_scatter | solution.py:942
  354.4 277.3 %reduce-scatter.6.cloned.1.call-start = ((), (), s32[]{:S(2)}) async-start(), calls=%async_computation.9 | async-start | bytes 4718592 | tf_op jit(solution)/shard_map/reduce_scatter | solution.py:942
  444.1 189.6 %reduce-scatter.8.cloned.1.call-start = ((), (), s32[]{:S(2)}) async-start(), calls=%async_computation.10 | async-start | bytes 4718592 | tf_op jit(solution)/shard_map/reduce_scatter | solution.py:942
  447.5 268.1 %reduce-scatter.14.cloned.1.call-start = ((), (), s32[]{:S(2)}) async-start(), calls=%async_computation.13 | async-start | bytes 9437184 | tf_op jit(solution)/shard_map/reduce_scatter | solution.py:942
  451.3 42.6 %collective-permute-start.7 = (bf16[128,2048]{1,0:T(8,128)(2,1)}, bf16[128,2048]{1,0:T(8,128)(2,1)}, u32[]{:S(2)}, u32[]{:S(2)}) collective-permute-start(bf16[128,2048]{1,0:T(8,128)(2,1)} %get-tuple-element.88.refs_6_), channel_id=1, source_target_pairs={{0,8},{8,0},{16,24},{24,16},{1,9},{9,1},{17,25},{25,17},{2,10},{10... | collective-permute-start | bytes 1572872 | tf_op jit(solution)/shard_map/ppermute | solution.py:951
  451.6 46.4 %collective-permute-start.8 = (bf16[128,2048]{1,0:T(8,128)(2,1)}, bf16[128,2048]{1,0:T(8,128)(2,1)}, u32[]{:S(2)}, u32[]{:S(2)}) collective-permute-start(bf16[128,2048]{1,0:T(8,128)(2,1)} %get-tuple-element.88.refs_6_), channel_id=1, source_target_pairs={{0,16},{8,24},{16,0},{24,8},{1,17},{9,25},{17,1},{25,9},{2,18},{10... | collective-permute-start | bytes 1572872 | tf_op jit(solution)/shard_map/ppermute | solution.py:951
  453.5 48.0 %collective-permute-start.9 = (bf16[128,2048]{1,0:T(8,128)(2,1)}, bf16[128,2048]{1,0:T(8,128)(2,1)S(1)}, u32[]{:S(2)}, u32[]{:S(2)}) collective-permute-start(bf16[128,2048]{1,0:T(8,128)(2,1)} %get-tuple-element.88.refs_6_), channel_id=1, source_target_pairs={{0,24},{8,16},{16,8},{24,0},{1,25},{9,17},{17,9},{25,1},{2,26},{10... | collective-permute-start | bytes 1572872 | tf_op jit(solution)/shard_map/ppermute | solution.py:951
  458.3 38.9 %collective-permute-start.10 = (bf16[128,2048]{1,0:T(8,128)(2,1)}, bf16[128,2048]{1,0:T(8,128)(2,1)S(1)}, u32[]{:S(2)}, u32[]{:S(2)}) collective-permute-start(bf16[128,2048]{1,0:T(8,128)(2,1)} %get-tuple-element.89.refs_7_), channel_id=1, source_target_pairs={{0,8},{8,0},{16,24},{24,16},{1,9},{9,1},{17,25},{25,17},{2,10},{10... | collective-permute-start | bytes 1572872 | tf_op jit(solution)/shard_map/ppermute | solution.py:951
  458.6 42.9 %collective-permute-start.11 = (bf16[128,2048]{1,0:T(8,128)(2,1)}, bf16[128,2048]{1,0:T(8,128)(2,1)S(1)}, u32[]{:S(2)}, u32[]{:S(2)}) collective-permute-start(bf16[128,2048]{1,0:T(8,128)(2,1)} %get-tuple-element.89.refs_7_), channel_id=1, source_target_pairs={{0,16},{8,24},{16,0},{24,8},{1,17},{9,25},{17,1},{25,9},{2,18},{10... | collective-permute-start | bytes 1572872 | tf_op jit(solution)/shard_map/ppermute | solution.py:951
  479.9 17.3 %copy-start.3 = (bf16[2,512,1024]{2,1,0:T(8,128)(2,1)S(1)}, bf16[2,512,1024]{2,1,0:T(8,128)(2,1)}, u32[]{:S(2)}) copy-start(bf16[2,512,1024]{2,1,0:T(8,128)(2,1)} %copy-done.2) | copy-start | bytes 6291460
  494.0 27.7 %collective-permute-start.12 = (bf16[128,2048]{1,0:T(8,128)(2,1)S(1)}, bf16[128,2048]{1,0:T(8,128)(2,1)S(1)}, u32[]{:S(2)}, u32[]{:S(2)}) collective-permute-start(bf16[128,2048]{1,0:T(8,128)(2,1)S(1)} %copy-done.7), channel_id=1, source_target_pairs={{0,24},{8,16},{16,8},{24,0},{1,25},{9,17},{17,9},{25,1},{2,26},{10... | collective-permute-start | bytes 1572872 | tf_op jit(solution)/shard_map/ppermute | solution.py:951
  497.2 54.4 %collective-permute-start.13 = (bf16[2,512,1024]{2,1,0:T(8,128)(2,1)S(1)}, bf16[2,512,1024]{2,1,0:T(8,128)(2,1)}, u32[]{:S(2)}, u32[]{:S(2)}) collective-permute-start(bf16[2,512,1024]{2,1,0:T(8,128)(2,1)S(1)} %copy-done.3), channel_id=1, source_target_pairs={{0,8},{8,0},{16,24},{24,16},{1,9},{9,1},{17,25},{25,17},{2,10},{10... | collective-permute-start | bytes 6291464 | tf_op jit(solution)/shard_map/ppermute | solution.py:951
  498.0 53.6 %collective-permute-start.14 = (bf16[2,512,1024]{2,1,0:T(8,128)(2,1)S(1)}, bf16[2,512,1024]{2,1,0:T(8,128)(2,1)}, u32[]{:S(2)}, u32[]{:S(2)}) collective-permute-start(bf16[2,512,1024]{2,1,0:T(8,128)(2,1)S(1)} %get-tuple-element.91.refs_1_), channel_id=1, source_target_pairs={{0,16},{8,24},{16,0},{24,8},{1,17},{9,25},{17,1},{25,9},{2,18},{10... | collective-permute-start | bytes 6291464 | tf_op jit(solution)/shard_map/ppermute | solution.py:951
  523.1 15.5 %copy-start.50 = (f32[1,1024]{1,0:T(1,128)S(1)}, f32[1,1024]{1,0:T(1,128)}, u32[]{:S(2)}) copy-start(f32[1,1024]{1,0:T(1,128)} %copy-done.49) | copy-start | bytes 12292
  558.5 47.0 %collective-permute-start.15 = (bf16[2,512,1024]{2,1,0:T(8,128)(2,1)}, bf16[2,512,1024]{2,1,0:T(8,128)(2,1)S(1)}, u32[]{:S(2)}, u32[]{:S(2)}) collective-permute-start(bf16[2,512,1024]{2,1,0:T(8,128)(2,1)} %get-tuple-element.100), channel_id=1, source_target_pairs={{0,8},{8,0},{16,24},{24,16},{1,9},{9,1},{17,25},{25,17},{2,10},{10... | collective-permute-start | bytes 6291464 | tf_op jit(solution)/shard_map/ppermute | solution.py:951
  560.0 46.4 %collective-permute-start.16 = (bf16[2,512,1024]{2,1,0:T(8,128)(2,1)}, bf16[2,512,1024]{2,1,0:T(8,128)(2,1)S(1)}, u32[]{:S(2)}, u32[]{:S(2)}) collective-permute-start(bf16[2,512,1024]{2,1,0:T(8,128)(2,1)} %get-tuple-element.101), channel_id=1, source_target_pairs={{0,16},{8,24},{16,0},{24,8},{1,17},{9,25},{17,1},{25,9},{2,18},{10... | collective-permute-start | bytes 6291464 | tf_op jit(solution)/shard_map/ppermute | solution.py:951
  566.9 41.2 %copy-start.9 = (bf16[4,128,2048]{2,1,0:T(8,128)(2,1)S(1)}, bf16[4,128,2048]{2,1,0:T(8,128)(2,1)}, u32[]{:S(2)}) copy-start(bf16[4,128,2048]{2,1,0:T(8,128)(2,1)} %copy-done.8) | copy-start | bytes 6291460
  566.9 41.2 %copy-start.13 = (bf16[512,512]{1,0:T(8,128)(2,1)S(1)}, bf16[512,512]{1,0:T(8,128)(2,1)}, u32[]{:S(2)}) copy-start(bf16[512,512]{1,0:T(8,128)(2,1)} %copy-done.12) | copy-start | bytes 1572868
  566.9 41.2 %copy-start.15 = (bf16[512,512]{1,0:T(8,128)(2,1)S(1)}, bf16[512,512]{1,0:T(8,128)(2,1)}, u32[]{:S(2)}) copy-start(bf16[512,512]{1,0:T(8,128)(2,1)} %copy-done.14) | copy-start | bytes 1572868
  716.6 3.8 collective-permute-start.17
  (57 other events, 238.3 us)
Sparse Core Ops, SparseCore 0:
  111.9 48.7 all-gather.4
  162.2 45.7 all-gather.8
  209.7 45.8 all-gather.6
  257.6 46.3 all-gather.10
  306.1 48.6 reduce-scatter.9
  356.9 48.1 reduce-scatter.11
  444.3 47.7 reduce-scatter.5
  494.4 48.1 reduce-scatter.7
  621.9 86.9 reduce-scatter.13

commit v6 on v5

--- a/solution.py
+++ b/solution.py
@@ -252,40 +252,35 @@
     )(x, d_hid, member, router_w, pick, w_gate, w_up)
 
 
-def weight_kernel(n, x_ref, d_ref, *refs):
-    out_ref = refs[-1]
-    width = d_ref.shape[1]
-    out_ref[:, :width] = t_mm(x_ref[...], d_ref[...]).astype(BF16)
+def weight_kernel(n, *refs):
     total = t_mm(refs[0][...], refs[n][...])
     for h in range(1, n):
         total = total + t_mm(refs[h][...], refs[n + h][...])
-    out_ref[:, width:] = total.astype(BF16)
-
-
-def attention_grads(xn, d_qkv, attended, dl, cols, earlier):
-    seq, width = xn.shape
-    n = len(attended)
+    refs[-1][...] = total.astype(BF16)
+
+
+def weight_grad(lefts, rights, block, tall, earlier):
+    n = len(lefts)
 
     def by_column(a):
-        return pl.BlockSpec((a.shape[0], cols), lambda i: (0, i))
+        return pl.BlockSpec((a.shape[0], block), lambda i: (0, i))
 
     def fixed(a):
         return pl.BlockSpec(a.shape, lambda i: (0, 0))
 
+    columns = rights[0].shape[1] if tall else block
+    rows = block if tall else lefts[0].shape[1]
+    count = (lefts if tall else rights)[0].shape[1] // block
     return pl.pallas_call(
         functools.partial(weight_kernel, n),
-        grid=(width // cols,),
-        in_specs=[by_column(xn), fixed(d_qkv)]
-        + [fixed(a) for a in attended]
-        + [by_column(a) for a in dl]
+        grid=(count,),
+        in_specs=[(by_column if tall else fixed)(a) for a in lefts]
+        + [(fixed if tall else by_column)(a) for a in rights]
         + [pl.BlockSpec(memory_space=pl.ANY)] * len(earlier),
-        out_specs=pl.BlockSpec((cols, 4 * cols), lambda i: (i, 0)),
-        out_shape=jax.ShapeDtypeStruct((width, 4 * cols), BF16),
+        out_specs=pl.BlockSpec((rows, columns), lambda i: (i, 0)),
+        out_shape=jax.ShapeDtypeStruct((count * rows, columns), BF16),
         compiler_params=pltpu.CompilerParams(vmem_limit_bytes=48 * MIB),
-        cost_estimate=pl.CostEstimate(
-            flops=8 * seq * width * cols, bytes_accessed=20 * MIB, transcendentals=0
-        ),
-    )(xn, d_qkv, *attended, *dl, *earlier)
+    )(*lefts, *rights, *earlier)
 
 
 def partial_kernel(n, part, d_ref, w_ref, *refs):
@@ -1124,9 +1119,11 @@
     dq_parts = []
     dk_n = jnp.zeros((seq, cols), F32)
     dv = jnp.zeros((seq, cols), F32)
+    g_out = weight_grad(attended_parts, dl_parts, cols, False, (*gives, y_mine[0]))
     for h in range(halves):
-        dq, dk_n, dv = attend_back(base, half_seq, h, d_att_parts[h], dk_n, dv, gives)
+        dq, dk_n, dv = attend_back(base, half_seq, h, d_att_parts[h], dk_n, dv, (g_out,))
         dq_parts.append(dq)
+    g_out = lax.ppermute(scatter_sum(g_out, "exp"), ("ctx", "exp"), [(b, a) for a, b in moves])
     dq_n = jnp.concatenate(dq_parts, axis=0)
     inner = jnp.stack(
         [
@@ -1145,7 +1142,7 @@
     g_key_gain = jnp.sum(dk_n * kp * k_scale, axis=0)
     d_qkv = jnp.concatenate([dqp.astype(BF16), dkp.astype(BF16), dv.astype(BF16)], axis=1)
     partial = input_partial(d_qkv, weights, part, ())
-    g_mine = attention_grads(xn, d_qkv, attended_parts, dl_parts, cols, (partial, *first_up))
+    g_mine = weight_grad([xn], [d_qkv], cols, True, (partial, g_out, y_mine[1], *first_up))
     g_gate, dxn, kept_up = gate_sums(mids, da_parts, db_parts, partial, first_gate, (g_mine,))
     dxn = jnp.concatenate([dxn[0], dxn[1]], axis=1)
     block_input = tokens[0].astype(F32)
@@ -1154,8 +1151,7 @@
     d_tokens = (jnp.concatenate(d_res_parts, axis=0) + d_in_norm).astype(BF16)
 
     g_mine = scatter_sum(g_mine, "exp")
-    g_out = lax.ppermute(g_mine[:, 3 * cols :], ("ctx", "exp"), [(b, a) for a, b in moves])
-    g_mine = jnp.concatenate([g_mine[:, : 3 * cols], g_out], axis=1)
+    g_mine = jnp.concatenate([g_mine, g_out], axis=1)
     gain_grads = [g_attn_gain[None], g_mid_gain]
     for piece in (g_query_gain, g_key_gain):
         gain_grads.append(

time: 832 us -> 829 us (level)
  Pallas kernels: 558 us -> 544 us
    ppermute x16, waiting for transfers between devices: 37 us -> 11 us  [swap(): return lax.ppermute(block, 'ctx', [(i, i ^ bits) for i in range(n)])]
    reduce_scatter x5 -> x6, waiting for transfers between devices: 0.04 us -> 20.7 us  [scatter_sum(): lax.psum_scatter(block, axis, scatter_dimension=dimension, tiled=True)]
    pallas_call x3, Pallas kernels: 243 us -> 226 us  [exchange(): pl.pallas_call(kernel, in_specs=[VMEM] * len(operands) + [ANY] * len(earl...]
    unnamed x134 -> x136, local copies, waits for them, and re-layouts: 18.4 us -> 22.2 us
  transfers between devices with their start and end apart: 27 -> 28, of which waited for: 3 -> 4; matrix products, arithmetic and copies ran while one was open for 19% -> 20% of each run, Pallas kernels for 48% -> 46%
where the time goes in v6:
time: 829 us; the launch traced here: 820 us
  Pallas kernels  544 us (66%)
  other arithmetic  74.8 us (9%)
  matrix products  66.2 us (8%)
  local copies, waits for them, and re-layouts  63.5 us (8%)
  waiting for transfers between devices  32.6 us (4%)
  starting transfers between devices  22.9 us (3%)
  between operations  16.1 us (2%)
    pallas_call x3, Pallas kernels, exchange(): pl.pallas_call(kernel, in_specs=[VMEM] * len(operands) + [ANY] * len(earl...  226 us
    pallas_call x2, Pallas kernels, expert_pass(): pl.pallas_call(functools.partial(expert_kernel, experts, own, 512), grid=...  98.7 us
    pallas_call x1, Pallas kernels, gather_start(): pl.pallas_call(functools.partial(start_kernel, n_ctx, n_exp), in_specs=[A...  82.5 us
    dot_general x6, matrix products, mm_t(): lax.dot_general(left, right, (((1,), (1,)), ((), ())), preferred_element_...  37.2 us
    pallas_call x2, Pallas kernels, given_grads(): pl.pallas_call(functools.partial(give_kernel, n, len(rights)), grid_spec=...  27.8 us
    pallas_call x2, Pallas kernels, attend_back(): pl.pallas_call(attend_back_kernel, grid=(heads,), in_specs=attention_spec...  27.4 us
    dot_general x9, matrix products, mm(): return jnp.dot(left, right, preferred_element_type=F32)  25.2 us
    unnamed x136, local copies, waits for them, and re-layouts  22.2 us
  transfers between devices with their start and end apart: 28, of which 4 were waited for; matrix products, arithmetic and copies ran while one was open for 20% of the time, Pallas kernels for 46%

profile of v6, /device:TPU:0, one launch (start us, length us, event | category | flops | bytes accessed | tf_op | source)
XLA Modules:
  0.0 820.0 jit_solution(575668202358909124)
XLA Ops:
  15.7 4.8 select_reduce_fusion.1
  24.5 82.5 %shard_map.290 = (bf16[8,256,2048]{2,1,0:T(8,128)(2,1)}, bf16[2,4,128,2048]{3,2,1,0:T(8,128)(2,1)}, bf16[8,64,128]{2,1,0:T(8,128)(2,1)}) custom-call(bf16[256,2048]{1,0:T(8,128)(2,1)} %pad_maximum_fusion.4.w_ref, bf16[2,128,2048]{2,1,0:T(8,128)(2,1)} %bitcast.195, bf16[64,128]{1,0:T(8,128)(2,1)} %pad_bitcast_fusion.small_ref), custom_call_target="tpu_custom_call" | custom-call | tf_op jit(solution)/shard_map/pallas_call | solution.py:820
  112.5 5.3 select_reduce_fusion
  130.7 12.0 %fusion.2.q_ref.k_ref.v_ref = f32[1024,1536]{1,0:T(8,128)} fusion(bf16[1024,2048]{1,0:T(8,128)(2,1)S(1)} %fusion.1.refs_0_, bf16[2048,2048]{1,0:T(8,128)(2,1)} %bitcast.193), kind=kOutput, calls=%fused_computation.4 | convolution fusion | flops 6442450944 | bytes 16777216 | tf_op jit(solution)/shard_map/dot_general | solution.py:24
  146.1 10.7 %shard_map.291 = f32[8,1024]{1,0:T(8,128)} custom-call(f32[8,1024]{1,0:T(8,128)} %select_maximum_fusion.1.x_ref), custom_call_target="tpu_custom_call" | custom-call | tf_op jit(solution)/shard_map/pallas_call | solution.py:429
  158.3 4.1 copy.40
  162.4 9.6 %shard_map.292.refs_0_ = bf16[512,512]{1,0:T(8,128)(2,1)S(1)} custom-call(f32[1024,1536]{1,0:T(8,128)} %fusion.2.q_ref.k_ref.v_ref, f32[1024,1536]{1,0:T(8,128)} %fusion.2.q_ref.k_ref.v_ref, f32[1024,1536]{1,0:T(8,128)} %fusion.2.q_ref.k_ref.v_ref, f32[1024,1]{1,0:T(8,128)S(1)} %copy.38.qs_ref, f32[1024,1]{1,0:T(8,128)S(1)} %copy.39.ks_ref, ...), custom_call_target="tpu_custom_call" | custom-call | flops 1073741824 | bytes 8388608 | tf_op jit(solution)/shard_map/pallas_call | solution.py:125
  182.7 8.2 %convert_bitcast_fusion.3 = bf16[1,1024,1024]{2,1,0:T(8,128)(2,1)S(1)} fusion(bf16[1024,2048]{1,0:T(8,128)(2,1)} %all-gather.5.cloned.1.call-done.refs_2_, bf16[2,1024,2048]{2,1,0:T(8,128)(2,1)} %refs_4_.1), kind=kOutput, calls=%fused_computation.51 | convolution fusion | flops 4296015872 | bytes 10485760 | tf_op jit(solution)/shard_map/dot_general | solution.py:28
  191.0 7.4 convert_bitcast_fusion.4
  205.0 9.7 %shard_map.296.refs_1_ = bf16[512,512]{1,0:T(8,128)(2,1)S(1)} custom-call(f32[1024,1536]{1,0:T(8,128)} %fusion.2.q_ref.k_ref.v_ref, f32[1024,1536]{1,0:T(8,128)} %fusion.2.q_ref.k_ref.v_ref, f32[1024,1536]{1,0:T(8,128)} %fusion.2.q_ref.k_ref.v_ref, f32[1024,1]{1,0:T(8,128)S(1)} %copy.38.qs_ref, f32[1024,1]{1,0:T(8,128)S(1)} %copy.39.ks_ref, ...), custom_call_target="tpu_custom_call" | custom-call | flops 1073741824 | bytes 8388608 | tf_op jit(solution)/shard_map/pallas_call | solution.py:125
  224.8 8.2 %convert_bitcast_fusion.1 = bf16[1,1024,1024]{2,1,0:T(8,128)(2,1)S(1)} fusion(bf16[1024,2048]{1,0:T(8,128)(2,1)} %all-gather.9.cloned.1.call-done.refs_3_, bf16[2,1024,2048]{2,1,0:T(8,128)(2,1)} %refs_4_.1), kind=kOutput, calls=%fused_computation.49 | convolution fusion | flops 4296015872 | bytes 10485760 | tf_op jit(solution)/shard_map/dot_general | solution.py:28
  233.0 7.0 convert_bitcast_fusion.2
  257.0 49.1 %shard_map.295 = (bf16[2,1024,1024]{2,1,0:T(8,128)(2,1)}, bf16[2,1024,1024]{2,1,0:T(8,128)(2,1)}, bf16[2,1024,1024]{2,1,0:T(8,128)(2,1)}, bf16[1024,2048]{1,0:T(8,128)(2,1)}, bf16[1024,128]{1,0:T(8,128)(2,1)}) custom-call(bf16[1024,2048]{1,0:T(8,128)(2,1)} %all-gather.7.cloned.1.call-done.x_ref.refs_0_, ...), custom_call_target="tpu_custom_call" | custom-call | flops 34359738368 | bytes 41943040 | tf_op jit(solution)/shard_map/pallas_call | solution.py:230
  306.2 49.6 %shard_map.298 = (bf16[2,1024,1024]{2,1,0:T(8,128)(2,1)}, bf16[2,1024,1024]{2,1,0:T(8,128)(2,1)}, bf16[2,1024,1024]{2,1,0:T(8,128)(2,1)}, bf16[1024,2048]{1,0:T(8,128)(2,1)}, bf16[1024,128]{1,0:T(8,128)(2,1)}) custom-call(bf16[1024,2048]{1,0:T(8,128)(2,1)} %all-gather.11.cloned.1.call-done.x_ref.refs_1_, ...), custom_call_target="tpu_custom_call" | custom-call | flops 34359738368 | bytes 41943040 | tf_op jit(solution)/shard_map/pallas_call | solution.py:230
  356.3 87.5 %shard_map.299 = (bf16[2,256,2048]{2,1,0:T(8,128)(2,1)}, bf16[1024,2048]{1,0:T(8,128)(2,1)}, bf16[1024,2048]{1,0:T(8,128)(2,1)}) custom-call(bf16[2,1024,1024]{2,1,0:T(8,128)(2,1)} %get-tuple-element.70.refs_0_, bf16[2,1024,1024]{2,1,0:T(8,128)(2,1)} %get-tuple-element.72.refs_1_, bf16[1024,2048]{1,0:T(8,128)(2,1)} %all-gather.5.cloned.1.call-done.refs_2_, ...), custom_call_target="tpu_custom_call" | custom-call | tf_op jit(solution)/shard_map/pallas_call | solution.py:871
  462.7 13.9 %shard_map.302 = (bf16[2,512,1024]{2,1,0:T(8,128)(2,1)S(1)}, bf16[2,512,1024]{2,1,0:T(8,128)(2,1)S(1)}) custom-call(s32[2]{0:T(128)S(1)} %get-tuple-element.186.table, bf16[1024,2048]{1,0:T(8,128)(2,1)} %all-gather.7.cloned.1.call-done.x_ref.refs_0_, bf16[1024,2048]{1,0:T(8,128)(2,1)} %all-gather.11.cloned.1.call-done.x_ref.refs_1_, ...), custom_call_target="tpu_custom_call" | custom-call | tf_op jit(solution)/shard_map/pallas_call | solution.py:326
  479.3 13.9 %shard_map.303 = (bf16[2,512,1024]{2,1,0:T(8,128)(2,1)S(1)}, bf16[2,512,1024]{2,1,0:T(8,128)(2,1)S(1)}) custom-call(s32[2]{0:T(128)S(1)} %get-tuple-element.185.table, bf16[1024,2048]{1,0:T(8,128)(2,1)} %all-gather.7.cloned.1.call-done.x_ref.refs_0_, bf16[1024,2048]{1,0:T(8,128)(2,1)} %all-gather.11.cloned.1.call-done.x_ref.refs_1_, ...), custom_call_target="tpu_custom_call" | custom-call | tf_op jit(solution)/shard_map/pallas_call | solution.py:326
  500.9 3.8 collective-permute-done.12
  509.3 5.4 shard_map.304.refs_0_
  518.1 3.7 convolution_convert_fusion.7.da_ref
  523.4 13.7 %shard_map.305 = (f32[512,512]{1,0:T(8,128)S(1)}, f32[1024,512]{1,0:T(8,128)}, f32[1024,512]{1,0:T(8,128)}) custom-call(f32[1024,1536]{1,0:T(8,128)} %fusion.2.q_ref.k_ref.v_ref, f32[1024,1536]{1,0:T(8,128)} %fusion.2.q_ref.k_ref.v_ref, f32[1024,1536]{1,0:T(8,128)} %fusion.2.q_ref.k_ref.v_ref, f32[1024,1]{1,0:T(8,128)S(1)} %copy.38.qs_ref, ...), custom_call_target="tpu_custom_call" | custom-call | flops 2684354560 | bytes 16777216 | tf_op jit(solution)/shard_map/pallas_call | solution.py:143
  541.5 13.7 %shard_map.306 = (f32[512,512]{1,0:T(8,128)S(1)}, f32[1024,512]{1,0:T(8,128)}, f32[1024,512]{1,0:T(8,128)}) custom-call(f32[1024,1536]{1,0:T(8,128)} %fusion.2.q_ref.k_ref.v_ref, f32[1024,1536]{1,0:T(8,128)} %fusion.2.q_ref.k_ref.v_ref, f32[1024,1536]{1,0:T(8,128)} %fusion.2.q_ref.k_ref.v_ref, f32[1024,1]{1,0:T(8,128)S(1)} %copy.38.qs_ref, ...), custom_call_target="tpu_custom_call" | custom-call | flops 2684354560 | bytes 16777216 | tf_op jit(solution)/shard_map/pallas_call | solution.py:143
  561.4 7.4 shard_map.307.refs_2_
  575.1 3.8 subtract_convert_fusion.1
  582.5 11.3 %shard_map.308.refs_2_.refs_6_ = bf16[2,4,256,1024]{3,2,1,0:T(8,128)(2,1)} custom-call(bf16[1024,1536]{1,0:T(8,128)(2,1)S(1)} %pad_maximum_fusion.2.d_ref.refs_1_, bf16[2048,2048]{1,0:T(8,128)(2,1)} %bitcast.194), custom_call_target="tpu_custom_call" | custom-call | tf_op jit(solution)/shard_map/pallas_call | solution.py:300
  593.8 20.7 %reduce-scatter.9.cloned.1.call-done.refs_4_ = bf16[128,2048]{1,0:T(8,128)(2,1)} async-done(((bf16[1024,2048]{1,0:T(8,128)(2,1)}), bf16[128,2048]{1,0:T(8,128)(2,1)}) %reduce-scatter.9.cloned.1.call-update) | async-done | bytes 524304 | tf_op jit(solution)/shard_map/reduce_scatter | solution.py:937
  614.5 7.0 collective-permute-done.16.refs_5_.refs_3_
  622.5 10.9 %shard_map.310.refs_9_ = bf16[2048,1536]{1,0:T(8,128)(2,1)} custom-call(bf16[1024,2048]{1,0:T(8,128)(2,1)} %copy-done.26, bf16[1024,1536]{1,0:T(8,128)(2,1)} %copy-done.2, bf16[2,4,256,1024]{3,2,1,0:T(8,128)(2,1)} %shard_map.308.refs_2_.refs_6_, bf16[256,512]{1,0:T(8,128)(2,1)S(1)} %collective-permute-done.15.refs_3_, bf16[128,2048]{1,0:T(8,128)(2,1)S(1)} %copy-done.16, ...), custom_call_target="tpu_custom_call" | custom-call | tf_op jit(solution)/shard_map/pallas_call | solution.py:274
  646.2 69.8 %shard_map.311 = (bf16[2,512,1024]{2,1,0:T(8,128)(2,1)}, f32[2,256,1024]{2,1,0:T(8,128)}, bf16[2,2,512,1024]{3,2,1,0:T(8,128)(2,1)}) custom-call(bf16[1024,2048]{1,0:T(8,128)(2,1)} %all-gather.7.cloned.1.call-done.x_ref.refs_0_, bf16[1024,2048]{1,0:T(8,128)(2,1)} %all-gather.11.cloned.1.call-done.x_ref.refs_1_, ...), custom_call_target="tpu_custom_call" | custom-call | tf_op jit(solution)/shard_map/pallas_call | solution.py:871
  716.1 4.2 convert_element_type.338
  730.9 68.9 %shard_map.312 = (bf16[2,512,1024]{2,1,0:T(8,128)(2,1)}, bf16[256,2048]{1,0:T(8,128)(2,1)}, bf16[256,2048]{1,0:T(8,128)(2,1)}, bf16[256,2048]{1,0:T(8,128)(2,1)}...) custom-call(bf16[256,2048]{1,0:T(8,128)(2,1)} %pad_maximum_fusion.5.refs_0_, f32[8,24,256]{2,1,0:T(8,128)} %bitcast.202, ...), custom_call_target="tpu_custom_call" | custom-call | tf_op jit(solution)/shard_map/pallas_call | solution.py:871
  802.5 4.2 convert_element_type.339
  (316 shorter events, 171.9 us)
Async XLA Ops:
  7.2 175.5 %all-gather.5.cloned.1.call-start = ((), (), s32[]{:S(2)}) async-start(), calls=%async_computation.6 | async-start | bytes 4718592 | tf_op jit(solution)/shard_map/all_gather | solution.py:933
  8.4 15.0 %collective-permute-start = (bf16[256,512]{1,0:T(8,128)(2,1)S(1)}, bf16[256,512]{1,0:T(8,128)(2,1)S(1)}, u32[]{:S(2)}, u32[]{:S(2)}) collective-permute-start(bf16[256,512]{1,0:T(8,128)(2,1)S(1)} %constant_dynamic-slice_fusion), channel_id=1, source_target_pairs={{0,0},{1,1},{8,2},{9,3},{16,4},{17,5},{24,6},{25,7},{2,8},{3,9},{1... | collective-permute-start | bytes 786440 | tf_op jit(solution)/shard_map/ppermute | solution.py:989
  111.8 113.0 %all-gather.9.cloned.1.call-start = ((), (), s32[]{:S(2)}) async-start(), calls=%async_computation.8 | async-start | bytes 4718592 | tf_op jit(solution)/shard_map/all_gather | solution.py:933
  127.2 129.8 %all-gather.7.cloned.1.call-start = ((), (), s32[]{:S(2)}) async-start(), calls=%async_computation.7 | async-start | bytes 4718592 | tf_op jit(solution)/shard_map/all_gather | solution.py:933
  173.7 27.0 %collective-permute-start.3 = (bf16[128,2048]{1,0:T(8,128)(2,1)}, bf16[128,2048]{1,0:T(8,128)(2,1)S(1)}, u32[]{:S(2)}, u32[]{:S(2)}) collective-permute-start(bf16[128,2048]{1,0:T(8,128)(2,1)} %convolution_convert_fusion.3), channel_id=1, source_target_pairs={{0,8},{8,0},{16,24},{24,16},{1,9},{9,1},{17,25},{25,17},{2,10},{10... | collective-permute-start | bytes 1572872 | tf_op jit(solution)/shard_map/ppermute | solution.py:946
  175.9 24.8 %collective-permute-start.2 = (bf16[128,2048]{1,0:T(8,128)(2,1)}, bf16[128,2048]{1,0:T(8,128)(2,1)}, u32[]{:S(2)}, u32[]{:S(2)}) collective-permute-start(bf16[128,2048]{1,0:T(8,128)(2,1)} %convolution_convert_fusion.4), channel_id=1, source_target_pairs={{0,16},{8,24},{16,0},{24,8},{1,17},{9,25},{17,1},{25,9},{2,18},{10... | collective-permute-start | bytes 1572872 | tf_op jit(solution)/shard_map/ppermute | solution.py:946
  178.9 21.8 %collective-permute-start.1 = (bf16[128,2048]{1,0:T(8,128)(2,1)}, bf16[128,2048]{1,0:T(8,128)(2,1)}, u32[]{:S(2)}, u32[]{:S(2)}) collective-permute-start(bf16[128,2048]{1,0:T(8,128)(2,1)} %convolution_convert_fusion.5), channel_id=1, source_target_pairs={{0,24},{8,16},{16,8},{24,0},{1,25},{9,17},{17,9},{25,1},{2,26},{10... | collective-permute-start | bytes 1572872 | tf_op jit(solution)/shard_map/ppermute | solution.py:946
  205.0 101.2 %all-gather.11.cloned.1.call-start = ((), (), s32[]{:S(2)}) async-start(), calls=%async_computation.9 | async-start | bytes 4718592 | tf_op jit(solution)/shard_map/all_gather | solution.py:933
  216.3 26.0 %collective-permute-start.6 = (bf16[128,2048]{1,0:T(8,128)(2,1)}, bf16[128,2048]{1,0:T(8,128)(2,1)S(1)}, u32[]{:S(2)}, u32[]{:S(2)}) collective-permute-start(bf16[128,2048]{1,0:T(8,128)(2,1)} %convolution_convert_fusion), channel_id=1, source_target_pairs={{0,8},{8,0},{16,24},{24,16},{1,9},{9,1},{17,25},{25,17},{2,10},{10... | collective-permute-start | bytes 1572872 | tf_op jit(solution)/shard_map/ppermute | solution.py:946
  218.6 23.9 %collective-permute-start.5 = (bf16[128,2048]{1,0:T(8,128)(2,1)}, bf16[128,2048]{1,0:T(8,128)(2,1)}, u32[]{:S(2)}, u32[]{:S(2)}) collective-permute-start(bf16[128,2048]{1,0:T(8,128)(2,1)} %convolution_convert_fusion.1), channel_id=1, source_target_pairs={{0,16},{8,24},{16,0},{24,8},{1,17},{9,25},{17,1},{25,9},{2,18},{10... | collective-permute-start | bytes 1572872 | tf_op jit(solution)/shard_map/ppermute | solution.py:946
  221.6 20.9 %collective-permute-start.4 = (bf16[128,2048]{1,0:T(8,128)(2,1)}, bf16[128,2048]{1,0:T(8,128)(2,1)}, u32[]{:S(2)}, u32[]{:S(2)}) collective-permute-start(bf16[128,2048]{1,0:T(8,128)(2,1)} %convolution_convert_fusion.2), channel_id=1, source_target_pairs={{0,24},{8,16},{16,8},{24,0},{1,25},{9,17},{17,9},{25,1},{2,26},{10... | collective-permute-start | bytes 1572872 | tf_op jit(solution)/shard_map/ppermute | solution.py:946
  246.6 200.7 %reduce-scatter.11.cloned.1.call-start = ((), (), s32[]{:S(2)}) async-start(), calls=%async_computation.12 | async-start | bytes 4718592 | tf_op jit(solution)/shard_map/reduce_scatter | solution.py:937
  306.1 148.1 %reduce-scatter.13.cloned.1.call-start = ((), (), s32[]{:S(2)}) async-start(), calls=%async_computation.13 | async-start | bytes 4718592 | tf_op jit(solution)/shard_map/reduce_scatter | solution.py:937
  355.9 149.8 %reduce-scatter.7.cloned.1.call-start = ((), (), s32[]{:S(2)}) async-start(), calls=%async_computation.10 | async-start | bytes 4718592 | tf_op jit(solution)/shard_map/reduce_scatter | solution.py:937
  443.9 135.0 %reduce-scatter.15.cloned.1.call-start = ((), (), s32[]{:S(2)}) async-start(), calls=%async_computation.14 | async-start | bytes 2359296 | tf_op jit(solution)/shard_map/reduce_scatter | solution.py:937
  450.8 42.4 %collective-permute-start.7 = (bf16[128,2048]{1,0:T(8,128)(2,1)}, bf16[128,2048]{1,0:T(8,128)(2,1)}, u32[]{:S(2)}, u32[]{:S(2)}) collective-permute-start(bf16[128,2048]{1,0:T(8,128)(2,1)} %get-tuple-element.88.refs_6_), channel_id=1, source_target_pairs={{0,8},{8,0},{16,24},{24,16},{1,9},{9,1},{17,25},{25,17},{2,10},{10... | collective-permute-start | bytes 1572872 | tf_op jit(solution)/shard_map/ppermute | solution.py:946
  451.9 44.6 %collective-permute-start.8 = (bf16[128,2048]{1,0:T(8,128)(2,1)}, bf16[128,2048]{1,0:T(8,128)(2,1)}, u32[]{:S(2)}, u32[]{:S(2)}) collective-permute-start(bf16[128,2048]{1,0:T(8,128)(2,1)} %get-tuple-element.88.refs_6_), channel_id=1, source_target_pairs={{0,16},{8,24},{16,0},{24,8},{1,17},{9,25},{17,1},{25,9},{2,18},{10... | collective-permute-start | bytes 1572872 | tf_op jit(solution)/shard_map/ppermute | solution.py:946
  453.0 45.6 %collective-permute-start.9 = (bf16[128,2048]{1,0:T(8,128)(2,1)}, bf16[128,2048]{1,0:T(8,128)(2,1)}, u32[]{:S(2)}, u32[]{:S(2)}) collective-permute-start(bf16[128,2048]{1,0:T(8,128)(2,1)} %get-tuple-element.88.refs_6_), channel_id=1, source_target_pairs={{0,24},{8,16},{16,8},{24,0},{1,25},{9,17},{17,9},{25,1},{2,26},{10... | collective-permute-start | bytes 1572872 | tf_op jit(solution)/shard_map/ppermute | solution.py:946
  457.8 37.9 %collective-permute-start.10 = (bf16[128,2048]{1,0:T(8,128)(2,1)}, bf16[128,2048]{1,0:T(8,128)(2,1)S(1)}, u32[]{:S(2)}, u32[]{:S(2)}) collective-permute-start(bf16[128,2048]{1,0:T(8,128)(2,1)} %get-tuple-element.89.refs_7_), channel_id=1, source_target_pairs={{0,8},{8,0},{16,24},{24,16},{1,9},{9,1},{17,25},{25,17},{2,10},{10... | collective-permute-start | bytes 1572872 | tf_op jit(solution)/shard_map/ppermute | solution.py:946
  458.9 38.8 %collective-permute-start.11 = (bf16[128,2048]{1,0:T(8,128)(2,1)}, bf16[128,2048]{1,0:T(8,128)(2,1)S(1)}, u32[]{:S(2)}, u32[]{:S(2)}) collective-permute-start(bf16[128,2048]{1,0:T(8,128)(2,1)} %get-tuple-element.89.refs_7_), channel_id=1, source_target_pairs={{0,16},{8,24},{16,0},{24,8},{1,17},{9,25},{17,1},{25,9},{2,18},{10... | collective-permute-start | bytes 1572872 | tf_op jit(solution)/shard_map/ppermute | solution.py:946
  493.2 11.6 %collective-permute-start.12 = (bf16[128,2048]{1,0:T(8,128)(2,1)S(1)}, bf16[128,2048]{1,0:T(8,128)(2,1)S(1)}, u32[]{:S(2)}, u32[]{:S(2)}) collective-permute-start(bf16[128,2048]{1,0:T(8,128)(2,1)S(1)} %copy-done.11), channel_id=1, source_target_pairs={{0,24},{8,16},{16,8},{24,0},{1,25},{9,17},{17,9},{25,1},{2,26},{10... | collective-permute-start | bytes 1572872 | tf_op jit(solution)/shard_map/ppermute | solution.py:946
  514.7 99.7 %reduce-scatter.9.cloned.1.call-start = ((), (), s32[]{:S(2)}) async-start(), calls=%async_computation.11 | async-start | bytes 4718592 | tf_op jit(solution)/shard_map/reduce_scatter | solution.py:937
  515.5 213.2 %reduce-scatter.17.cloned.1.call-start = ((), (), s32[]{:S(2)}) async-start(), calls=%async_computation.15 | async-start | bytes 7077888 | tf_op jit(solution)/shard_map/reduce_scatter | solution.py:937
  515.9 45.5 %collective-permute-start.14 = (bf16[2,512,1024]{2,1,0:T(8,128)(2,1)}, bf16[2,512,1024]{2,1,0:T(8,128)(2,1)}, u32[]{:S(2)}, u32[]{:S(2)}) collective-permute-start(bf16[2,512,1024]{2,1,0:T(8,128)(2,1)} %copy-done.18), channel_id=1, source_target_pairs={{0,16},{8,24},{16,0},{24,8},{1,17},{9,25},{17,1},{25,9},{2,18},{10... | collective-permute-start | bytes 6291464 | tf_op jit(solution)/shard_map/ppermute | solution.py:946
  517.0 44.4 %collective-permute-start.13 = (bf16[2,512,1024]{2,1,0:T(8,128)(2,1)}, bf16[2,512,1024]{2,1,0:T(8,128)(2,1)}, u32[]{:S(2)}, u32[]{:S(2)}) collective-permute-start(bf16[2,512,1024]{2,1,0:T(8,128)(2,1)} %copy-done.5), channel_id=1, source_target_pairs={{0,8},{8,0},{16,24},{24,16},{1,9},{9,1},{17,25},{25,17},{2,10},{10... | collective-permute-start | bytes 6291464 | tf_op jit(solution)/shard_map/ppermute | solution.py:946
  541.5 13.8 %copy-start.50 = (f32[1,1024]{1,0:T(1,128)S(1)}, f32[1,1024]{1,0:T(1,128)}, u32[]{:S(2)}) copy-start(f32[1,1024]{1,0:T(1,128)} %copy-done.49) | copy-start | bytes 12292
  568.9 52.6 %collective-permute-start.16 = (bf16[2,512,1024]{2,1,0:T(8,128)(2,1)}, bf16[2,512,1024]{2,1,0:T(8,128)(2,1)}, u32[]{:S(2)}, u32[]{:S(2)}) collective-permute-start(bf16[2,512,1024]{2,1,0:T(8,128)(2,1)} %get-tuple-element.100), channel_id=1, source_target_pairs={{0,8},{8,0},{16,24},{24,16},{1,9},{9,1},{17,25},{25,17},{2,10},{10... | collective-permute-start | bytes 6291464 | tf_op jit(solution)/shard_map/ppermute | solution.py:946
  570.1 51.4 %collective-permute-start.17 = (bf16[2,512,1024]{2,1,0:T(8,128)(2,1)}, bf16[2,512,1024]{2,1,0:T(8,128)(2,1)}, u32[]{:S(2)}, u32[]{:S(2)}) collective-permute-start(bf16[2,512,1024]{2,1,0:T(8,128)(2,1)} %get-tuple-element.101), channel_id=1, source_target_pairs={{0,16},{8,24},{16,0},{24,8},{1,17},{9,25},{17,1},{25,9},{2,18},{10... | collective-permute-start | bytes 6291464 | tf_op jit(solution)/shard_map/ppermute | solution.py:946
  578.9 42.6 %collective-permute-start.15 = (bf16[256,512]{1,0:T(8,128)(2,1)}, bf16[256,512]{1,0:T(8,128)(2,1)S(1)}, u32[]{:S(2)}, u32[]{:S(2)}) collective-permute-start(bf16[256,512]{1,0:T(8,128)(2,1)} %reduce-scatter.15.cloned.1.call-done), channel_id=1, source_target_pairs={{0,0},{1,1},{2,8},{3,9},{4,16},{5,17},{6,24},{7,25},{8,2},{9,3},{1... | collective-permute-start | bytes 786440 | tf_op jit(solution)/shard_map/ppermute | solution.py:1126
  635.6 85.0 %copy-start.53 = (f32[256]{0:T(256)}, f32[256]{0:T(256)S(1)}, u32[]{:S(2)}) copy-start(f32[256]{0:T(256)S(1)} %get-tuple-element.174) | copy-start | bytes 3076
  646.2 69.9 %copy-start.52 = (f32[1,2048]{1,0:T(1,128)}, f32[1,2048]{1,0:T(1,128)S(1)}, u32[]{:S(2)}) copy-start(f32[1,2048]{1,0:T(1,128)S(1)} %constant_dynamic-update-slice_fusion.4) | copy-start | bytes 24580
  646.2 69.8 %copy-start.51 = (f32[1,2048]{1,0:T(1,128)}, f32[1,2048]{1,0:T(1,128)S(1)}, u32[]{:S(2)}) copy-start(f32[1,2048]{1,0:T(1,128)S(1)} %constant_dynamic-update-slice_fusion.3) | copy-start | bytes 24580
  (58 other events, 223.7 us)
Sparse Core Ops, SparseCore 0:
  111.9 48.7 all-gather.4
  162.3 45.7 all-gather.8
  209.7 46.1 all-gather.6
  257.9 45.4 all-gather.10
  306.3 48.0 reduce-scatter.10
  356.5 48.1 reduce-scatter.12
  444.0 47.4 reduce-scatter.6
  514.9 34.0 reduce-scatter.14
  551.3 63.1 reduce-scatter.8
  633.6 70.0 reduce-scatter.16

commit v7 on v6

--- a/solution.py
+++ b/solution.py
@@ -625,15 +625,20 @@
 
 
 def down_kernel(n, halves, *refs):
-    hid, grad, w_down = refs[:halves], refs[halves : 2 * halves], refs[2 * halves]
+    hid, grad, w_hbm = refs[:halves], refs[halves : 2 * halves], refs[2 * halves]
     refs = refs[2 * halves + 1 :]
-    out, ys, scratch = refs[0], refs[1 : 1 + halves], refs[1 + halves :]
+    out, y_hbm, scratch = refs[0], refs[1 : 1 + halves], refs[1 + halves :]
+    w_down, ys, local_sems = scratch[5], scratch[6 : 6 + halves], scratch[6 + halves]
+    load = pltpu.make_async_copy(w_hbm, w_down, local_sems.at[halves])
+    stores = [pltpu.make_async_copy(ys[h], y_hbm[h], local_sems.at[h]) for h in range(halves)]
+    load.start()
     me = lax.axis_index("ctx")
     meet(ctx_peers(n, me))
     sums = Halving(n, me, None, *scratch[:4], out, acc=scratch[4])
     value = product(hid, grad, hid[0].shape[2] // n)
     sums.begin(value)
     sums.rest(value)
+    load.wait()
     width = w_down.shape[2]
     for h in range(halves):
         for start in range(0, width, 512):
@@ -642,8 +647,12 @@
             for j in range(1, w_down.shape[0]):
                 total = total + mm(hid[h][j], w_down[j, :, cut])
             ys[h][:, cut] = total.astype(BF16)
-    sums.pass_on()
+        stores[h].start()
+        if h == 0:
+            sums.pass_on()
     sums.finish()
+    for store in stores:
+        store.wait()
 
 
 def gate_kernel(n, halves, *refs):
@@ -866,13 +875,13 @@
 ANY = pl.BlockSpec(memory_space=pl.ANY)
 
 
-def exchange(kernel, number, operands, earlier, outs, scratch):
+def exchange(kernel, number, operands, earlier, outs, scratch, far=()):
     n = lax.axis_size("ctx")
     return pl.pallas_call(
         kernel,
         in_specs=[VMEM] * len(operands) + [ANY] * len(earlier),
-        out_specs=[VMEM] * len(outs),
-        out_shape=outs,
+        out_specs=[VMEM] * len(outs) + [ANY] * len(far),
+        out_shape=[*outs, *far],
         scratch_shapes=scratch,
         compiler_params=pltpu.CompilerParams(
             collective_id=number, has_side_effects=True, vmem_limit_bytes=60 * MIB
@@ -884,10 +893,14 @@
     n, halves = lax.axis_size("ctx"), len(hid)
     own, ff, width = w_down.shape
     outs = [jax.ShapeDtypeStruct((own, ff // n, width), BF16)]
-    outs += [jax.ShapeDtypeStruct((h.shape[1], width), BF16) for h in hid]
+    ys = [jax.ShapeDtypeStruct((h.shape[1], width), BF16) for h in hid]
     return exchange(
-        functools.partial(down_kernel, n, halves), 3, [*hid, *grad, w_down], (), outs,
-        Halving.scratch(own, n, ff // n, width) + [pltpu.VMEM((own, ff // n, width), F32)],
+        functools.partial(down_kernel, n, halves), 3, [*hid, *grad], (w_down,), outs,
+        Halving.scratch(own, n, ff // n, width)
+        + [pltpu.VMEM((own, ff // n, width), F32), pltpu.VMEM(w_down.shape, BF16)]
+        + [pltpu.VMEM(y.shape, BF16) for y in ys]
+        + [pltpu.SemaphoreType.DMA((halves + 1,))],
+        ys,
     )
 
 

time: 829 us -> 824 us (level)
  transfers between devices with their start and end apart: 28 -> 28, of which waited for: 4 -> 4; matrix products, arithmetic and copies ran while one was open for 20% -> 20% of each run, Pallas kernels for 46% -> 45%
where the time goes in v7:
time: 824 us; the launch traced here: 815 us
  Pallas kernels  540 us (66%)
  other arithmetic  74.8 us (9%)
  matrix products  66.2 us (8%)
  local copies, waits for them, and re-layouts  63.7 us (8%)
  waiting for transfers between devices  32.6 us (4%)
  starting transfers between devices  22.3 us (3%)
  between operations  16.1 us (2%)
    pallas_call x3, Pallas kernels, exchange(): pl.pallas_call(kernel, in_specs=[VMEM] * len(operands) + [ANY] * len(earl...  222 us
    pallas_call x2, Pallas kernels, expert_pass(): pl.pallas_call(functools.partial(expert_kernel, experts, own, 512), grid=...  98.7 us
    pallas_call x1, Pallas kernels, gather_start(): pl.pallas_call(functools.partial(start_kernel, n_ctx, n_exp), in_specs=[A...  82.5 us
    dot_general x6, matrix products, mm_t(): lax.dot_general(left, right, (((1,), (1,)), ((), ())), preferred_element_...  37.2 us
    pallas_call x2, Pallas kernels, given_grads(): pl.pallas_call(functools.partial(give_kernel, n, len(rights)), grid_spec=...  27.8 us
    pallas_call x2, Pallas kernels, attend_back(): pl.pallas_call(attend_back_kernel, grid=(heads,), in_specs=attention_spec...  27.4 us
    dot_general x9, matrix products, mm(): return jnp.dot(left, right, preferred_element_type=F32)  25.2 us
    unnamed x136, local copies, waits for them, and re-layouts  22.4 us
  transfers between devices with their start and end apart: 28, of which 4 were waited for; matrix products, arithmetic and copies ran while one was open for 20% of the time, Pallas kernels for 45%

profile of v7, /device:TPU:0, one launch (start us, length us, event | category | flops | bytes accessed | tf_op | source)
XLA Modules:
  0.0 815.3 jit_solution(7746351426733567873)
XLA Ops:
  15.7 4.8 select_reduce_fusion.1
  24.5 82.5 %shard_map.290 = (bf16[8,256,2048]{2,1,0:T(8,128)(2,1)}, bf16[2,4,128,2048]{3,2,1,0:T(8,128)(2,1)}, bf16[8,64,128]{2,1,0:T(8,128)(2,1)}) custom-call(bf16[256,2048]{1,0:T(8,128)(2,1)} %pad_maximum_fusion.4.w_ref, bf16[2,128,2048]{2,1,0:T(8,128)(2,1)} %bitcast.195, bf16[64,128]{1,0:T(8,128)(2,1)} %pad_bitcast_fusion.small_ref), custom_call_target="tpu_custom_call" | custom-call | tf_op jit(solution)/shard_map/pallas_call | solution.py:829
  112.5 5.3 select_reduce_fusion
  130.7 12.0 %fusion.2.q_ref.k_ref.v_ref = f32[1024,1536]{1,0:T(8,128)} fusion(bf16[1024,2048]{1,0:T(8,128)(2,1)S(1)} %fusion.1.refs_0_, bf16[2048,2048]{1,0:T(8,128)(2,1)} %bitcast.193), kind=kOutput, calls=%fused_computation.4 | convolution fusion | flops 6442450944 | bytes 16777216 | tf_op jit(solution)/shard_map/dot_general | solution.py:24
  146.1 10.7 %shard_map.291 = f32[8,1024]{1,0:T(8,128)} custom-call(f32[8,1024]{1,0:T(8,128)} %select_maximum_fusion.1.x_ref), custom_call_target="tpu_custom_call" | custom-call | tf_op jit(solution)/shard_map/pallas_call | solution.py:429
  158.3 4.1 copy.40
  162.4 9.6 %shard_map.292.refs_0_ = bf16[512,512]{1,0:T(8,128)(2,1)S(1)} custom-call(f32[1024,1536]{1,0:T(8,128)} %fusion.2.q_ref.k_ref.v_ref, f32[1024,1536]{1,0:T(8,128)} %fusion.2.q_ref.k_ref.v_ref, f32[1024,1536]{1,0:T(8,128)} %fusion.2.q_ref.k_ref.v_ref, f32[1024,1]{1,0:T(8,128)S(1)} %copy.38.qs_ref, f32[1024,1]{1,0:T(8,128)S(1)} %copy.39.ks_ref, ...), custom_call_target="tpu_custom_call" | custom-call | flops 1073741824 | bytes 8388608 | tf_op jit(solution)/shard_map/pallas_call | solution.py:125
  182.7 8.2 %convert_bitcast_fusion.3 = bf16[1,1024,1024]{2,1,0:T(8,128)(2,1)S(1)} fusion(bf16[1024,2048]{1,0:T(8,128)(2,1)} %all-gather.5.cloned.1.call-done.refs_2_, bf16[2,1024,2048]{2,1,0:T(8,128)(2,1)} %refs_4_.1), kind=kOutput, calls=%fused_computation.51 | convolution fusion | flops 4296015872 | bytes 10485760 | tf_op jit(solution)/shard_map/dot_general | solution.py:28
  191.0 7.4 convert_bitcast_fusion.4
  205.0 9.7 %shard_map.296.refs_1_ = bf16[512,512]{1,0:T(8,128)(2,1)S(1)} custom-call(f32[1024,1536]{1,0:T(8,128)} %fusion.2.q_ref.k_ref.v_ref, f32[1024,1536]{1,0:T(8,128)} %fusion.2.q_ref.k_ref.v_ref, f32[1024,1536]{1,0:T(8,128)} %fusion.2.q_ref.k_ref.v_ref, f32[1024,1]{1,0:T(8,128)S(1)} %copy.38.qs_ref, f32[1024,1]{1,0:T(8,128)S(1)} %copy.39.ks_ref, ...), custom_call_target="tpu_custom_call" | custom-call | flops 1073741824 | bytes 8388608 | tf_op jit(solution)/shard_map/pallas_call | solution.py:125
  224.8 8.2 %convert_bitcast_fusion.1 = bf16[1,1024,1024]{2,1,0:T(8,128)(2,1)S(1)} fusion(bf16[1024,2048]{1,0:T(8,128)(2,1)} %all-gather.9.cloned.1.call-done.refs_3_, bf16[2,1024,2048]{2,1,0:T(8,128)(2,1)} %refs_4_.1), kind=kOutput, calls=%fused_computation.49 | convolution fusion | flops 4296015872 | bytes 10485760 | tf_op jit(solution)/shard_map/dot_general | solution.py:28
  233.0 7.0 convert_bitcast_fusion.2
  257.0 49.1 %shard_map.295 = (bf16[2,1024,1024]{2,1,0:T(8,128)(2,1)}, bf16[2,1024,1024]{2,1,0:T(8,128)(2,1)}, bf16[2,1024,1024]{2,1,0:T(8,128)(2,1)}, bf16[1024,2048]{1,0:T(8,128)(2,1)}, bf16[1024,128]{1,0:T(8,128)(2,1)}) custom-call(bf16[1024,2048]{1,0:T(8,128)(2,1)} %all-gather.7.cloned.1.call-done.x_ref.refs_0_, ...), custom_call_target="tpu_custom_call" | custom-call | flops 34359738368 | bytes 41943040 | tf_op jit(solution)/shard_map/pallas_call | solution.py:230
  306.2 49.6 %shard_map.298 = (bf16[2,1024,1024]{2,1,0:T(8,128)(2,1)}, bf16[2,1024,1024]{2,1,0:T(8,128)(2,1)}, bf16[2,1024,1024]{2,1,0:T(8,128)(2,1)}, bf16[1024,2048]{1,0:T(8,128)(2,1)}, bf16[1024,128]{1,0:T(8,128)(2,1)}) custom-call(bf16[1024,2048]{1,0:T(8,128)(2,1)} %all-gather.11.cloned.1.call-done.x_ref.refs_1_, ...), custom_call_target="tpu_custom_call" | custom-call | flops 34359738368 | bytes 41943040 | tf_op jit(solution)/shard_map/pallas_call | solution.py:230
  356.3 82.1 %shard_map.299 = (bf16[2,256,2048]{2,1,0:T(8,128)(2,1)}, bf16[1024,2048]{1,0:T(8,128)(2,1)}, bf16[1024,2048]{1,0:T(8,128)(2,1)}) custom-call(bf16[2,1024,1024]{2,1,0:T(8,128)(2,1)} %get-tuple-element.70.refs_0_, bf16[2,1024,1024]{2,1,0:T(8,128)(2,1)} %get-tuple-element.72.refs_1_, bf16[1024,2048]{1,0:T(8,128)(2,1)} %all-gather.5.cloned.1.call-done.refs_2_, ...), custom_call_target="tpu_custom_call" | custom-call | tf_op jit(solution)/shard_map/pallas_call | solution.py:880
  457.1 13.9 %shard_map.302 = (bf16[2,512,1024]{2,1,0:T(8,128)(2,1)S(1)}, bf16[2,512,1024]{2,1,0:T(8,128)(2,1)S(1)}) custom-call(s32[2]{0:T(128)S(1)} %get-tuple-element.186.table, bf16[1024,2048]{1,0:T(8,128)(2,1)} %all-gather.7.cloned.1.call-done.x_ref.refs_0_, bf16[1024,2048]{1,0:T(8,128)(2,1)} %all-gather.11.cloned.1.call-done.x_ref.refs_1_, ...), custom_call_target="tpu_custom_call" | custom-call | tf_op jit(solution)/shard_map/pallas_call | solution.py:326
  473.7 13.9 %shard_map.303 = (bf16[2,512,1024]{2,1,0:T(8,128)(2,1)S(1)}, bf16[2,512,1024]{2,1,0:T(8,128)(2,1)S(1)}) custom-call(s32[2]{0:T(128)S(1)} %get-tuple-element.185.table, bf16[1024,2048]{1,0:T(8,128)(2,1)} %all-gather.7.cloned.1.call-done.x_ref.refs_0_, bf16[1024,2048]{1,0:T(8,128)(2,1)} %all-gather.11.cloned.1.call-done.x_ref.refs_1_, ...), custom_call_target="tpu_custom_call" | custom-call | tf_op jit(solution)/shard_map/pallas_call | solution.py:326
  495.6 3.6 collective-permute-done.12
  503.8 5.4 shard_map.304.refs_0_
  512.5 3.6 convolution_convert_fusion.7.da_ref
  517.7 13.7 %shard_map.305 = (f32[512,512]{1,0:T(8,128)S(1)}, f32[1024,512]{1,0:T(8,128)}, f32[1024,512]{1,0:T(8,128)}) custom-call(f32[1024,1536]{1,0:T(8,128)} %fusion.2.q_ref.k_ref.v_ref, f32[1024,1536]{1,0:T(8,128)} %fusion.2.q_ref.k_ref.v_ref, f32[1024,1536]{1,0:T(8,128)} %fusion.2.q_ref.k_ref.v_ref, f32[1024,1]{1,0:T(8,128)S(1)} %copy.38.qs_ref, ...), custom_call_target="tpu_custom_call" | custom-call | flops 2684354560 | bytes 16777216 | tf_op jit(solution)/shard_map/pallas_call | solution.py:143
  535.9 13.7 %shard_map.306 = (f32[512,512]{1,0:T(8,128)S(1)}, f32[1024,512]{1,0:T(8,128)}, f32[1024,512]{1,0:T(8,128)}) custom-call(f32[1024,1536]{1,0:T(8,128)} %fusion.2.q_ref.k_ref.v_ref, f32[1024,1536]{1,0:T(8,128)} %fusion.2.q_ref.k_ref.v_ref, f32[1024,1536]{1,0:T(8,128)} %fusion.2.q_ref.k_ref.v_ref, f32[1024,1]{1,0:T(8,128)S(1)} %copy.38.qs_ref, ...), custom_call_target="tpu_custom_call" | custom-call | flops 2684354560 | bytes 16777216 | tf_op jit(solution)/shard_map/pallas_call | solution.py:143
  555.8 7.6 shard_map.307.refs_2_
  569.3 3.8 subtract_convert_fusion.1
  576.7 11.3 %shard_map.308.refs_2_.refs_6_ = bf16[2,4,256,1024]{3,2,1,0:T(8,128)(2,1)} custom-call(bf16[1024,1536]{1,0:T(8,128)(2,1)S(1)} %pad_maximum_fusion.2.d_ref.refs_1_, bf16[2048,2048]{1,0:T(8,128)(2,1)} %bitcast.194), custom_call_target="tpu_custom_call" | custom-call | tf_op jit(solution)/shard_map/pallas_call | solution.py:300
  587.9 21.5 %reduce-scatter.9.cloned.1.call-done.refs_4_ = bf16[128,2048]{1,0:T(8,128)(2,1)} async-done(((bf16[1024,2048]{1,0:T(8,128)(2,1)}), bf16[128,2048]{1,0:T(8,128)(2,1)}) %reduce-scatter.9.cloned.1.call-update) | async-done | bytes 524304 | tf_op jit(solution)/shard_map/reduce_scatter | solution.py:950
  609.4 6.4 collective-permute-done.16.refs_5_.refs_3_
  616.9 10.9 %shard_map.310.refs_9_ = bf16[2048,1536]{1,0:T(8,128)(2,1)} custom-call(bf16[1024,2048]{1,0:T(8,128)(2,1)} %copy-done.26, bf16[1024,1536]{1,0:T(8,128)(2,1)} %copy-done.2, bf16[2,4,256,1024]{3,2,1,0:T(8,128)(2,1)} %shard_map.308.refs_2_.refs_6_, bf16[256,512]{1,0:T(8,128)(2,1)S(1)} %collective-permute-done.15.refs_3_, bf16[128,2048]{1,0:T(8,128)(2,1)S(1)} %copy-done.16, ...), custom_call_target="tpu_custom_call" | custom-call | tf_op jit(solution)/shard_map/pallas_call | solution.py:274
  640.6 69.9 %shard_map.311 = (bf16[2,512,1024]{2,1,0:T(8,128)(2,1)}, f32[2,256,1024]{2,1,0:T(8,128)}, bf16[2,2,512,1024]{3,2,1,0:T(8,128)(2,1)}) custom-call(bf16[1024,2048]{1,0:T(8,128)(2,1)} %all-gather.7.cloned.1.call-done.x_ref.refs_0_, bf16[1024,2048]{1,0:T(8,128)(2,1)} %all-gather.11.cloned.1.call-done.x_ref.refs_1_, ...), custom_call_target="tpu_custom_call" | custom-call | tf_op jit(solution)/shard_map/pallas_call | solution.py:880
  710.5 4.2 convert_element_type.338
  725.3 69.7 %shard_map.312 = (bf16[2,512,1024]{2,1,0:T(8,128)(2,1)}, bf16[256,2048]{1,0:T(8,128)(2,1)}, bf16[256,2048]{1,0:T(8,128)(2,1)}, bf16[256,2048]{1,0:T(8,128)(2,1)}...) custom-call(bf16[256,2048]{1,0:T(8,128)(2,1)} %pad_maximum_fusion.5.refs_0_, f32[8,24,256]{2,1,0:T(8,128)} %bitcast.202, ...), custom_call_target="tpu_custom_call" | custom-call | tf_op jit(solution)/shard_map/pallas_call | solution.py:880
  797.8 4.2 convert_element_type.339
  (316 shorter events, 171.5 us)
Async XLA Ops:
  7.2 175.5 %all-gather.5.cloned.1.call-start = ((), (), s32[]{:S(2)}) async-start(), calls=%async_computation.6 | async-start | bytes 4718592 | tf_op jit(solution)/shard_map/all_gather | solution.py:946
  8.4 15.0 %collective-permute-start = (bf16[256,512]{1,0:T(8,128)(2,1)S(1)}, bf16[256,512]{1,0:T(8,128)(2,1)S(1)}, u32[]{:S(2)}, u32[]{:S(2)}) collective-permute-start(bf16[256,512]{1,0:T(8,128)(2,1)S(1)} %constant_dynamic-slice_fusion), channel_id=1, source_target_pairs={{0,0},{1,1},{8,2},{9,3},{16,4},{17,5},{24,6},{25,7},{2,8},{3,9},{1... | collective-permute-start | bytes 786440 | tf_op jit(solution)/shard_map/ppermute | solution.py:1002
  111.8 113.0 %all-gather.9.cloned.1.call-start = ((), (), s32[]{:S(2)}) async-start(), calls=%async_computation.8 | async-start | bytes 4718592 | tf_op jit(solution)/shard_map/all_gather | solution.py:946
  127.2 129.8 %all-gather.7.cloned.1.call-start = ((), (), s32[]{:S(2)}) async-start(), calls=%async_computation.7 | async-start | bytes 4718592 | tf_op jit(solution)/shard_map/all_gather | solution.py:946
  173.7 27.0 %collective-permute-start.3 = (bf16[128,2048]{1,0:T(8,128)(2,1)}, bf16[128,2048]{1,0:T(8,128)(2,1)S(1)}, u32[]{:S(2)}, u32[]{:S(2)}) collective-permute-start(bf16[128,2048]{1,0:T(8,128)(2,1)} %convolution_convert_fusion.3), channel_id=1, source_target_pairs={{0,8},{8,0},{16,24},{24,16},{1,9},{9,1},{17,25},{25,17},{2,10},{10... | collective-permute-start | bytes 1572872 | tf_op jit(solution)/shard_map/ppermute | solution.py:959
  175.9 24.8 %collective-permute-start.2 = (bf16[128,2048]{1,0:T(8,128)(2,1)}, bf16[128,2048]{1,0:T(8,128)(2,1)}, u32[]{:S(2)}, u32[]{:S(2)}) collective-permute-start(bf16[128,2048]{1,0:T(8,128)(2,1)} %convolution_convert_fusion.4), channel_id=1, source_target_pairs={{0,16},{8,24},{16,0},{24,8},{1,17},{9,25},{17,1},{25,9},{2,18},{10... | collective-permute-start | bytes 1572872 | tf_op jit(solution)/shard_map/ppermute | solution.py:959
  178.9 21.8 %collective-permute-start.1 = (bf16[128,2048]{1,0:T(8,128)(2,1)}, bf16[128,2048]{1,0:T(8,128)(2,1)}, u32[]{:S(2)}, u32[]{:S(2)}) collective-permute-start(bf16[128,2048]{1,0:T(8,128)(2,1)} %convolution_convert_fusion.5), channel_id=1, source_target_pairs={{0,24},{8,16},{16,8},{24,0},{1,25},{9,17},{17,9},{25,1},{2,26},{10... | collective-permute-start | bytes 1572872 | tf_op jit(solution)/shard_map/ppermute | solution.py:959
  205.0 101.2 %all-gather.11.cloned.1.call-start = ((), (), s32[]{:S(2)}) async-start(), calls=%async_computation.9 | async-start | bytes 4718592 | tf_op jit(solution)/shard_map/all_gather | solution.py:946
  216.3 26.0 %collective-permute-start.6 = (bf16[128,2048]{1,0:T(8,128)(2,1)}, bf16[128,2048]{1,0:T(8,128)(2,1)S(1)}, u32[]{:S(2)}, u32[]{:S(2)}) collective-permute-start(bf16[128,2048]{1,0:T(8,128)(2,1)} %convolution_convert_fusion), channel_id=1, source_target_pairs={{0,8},{8,0},{16,24},{24,16},{1,9},{9,1},{17,25},{25,17},{2,10},{10... | collective-permute-start | bytes 1572872 | tf_op jit(solution)/shard_map/ppermute | solution.py:959
  218.6 23.9 %collective-permute-start.5 = (bf16[128,2048]{1,0:T(8,128)(2,1)}, bf16[128,2048]{1,0:T(8,128)(2,1)}, u32[]{:S(2)}, u32[]{:S(2)}) collective-permute-start(bf16[128,2048]{1,0:T(8,128)(2,1)} %convolution_convert_fusion.1), channel_id=1, source_target_pairs={{0,16},{8,24},{16,0},{24,8},{1,17},{9,25},{17,1},{25,9},{2,18},{10... | collective-permute-start | bytes 1572872 | tf_op jit(solution)/shard_map/ppermute | solution.py:959
  221.6 20.9 %collective-permute-start.4 = (bf16[128,2048]{1,0:T(8,128)(2,1)}, bf16[128,2048]{1,0:T(8,128)(2,1)}, u32[]{:S(2)}, u32[]{:S(2)}) collective-permute-start(bf16[128,2048]{1,0:T(8,128)(2,1)} %convolution_convert_fusion.2), channel_id=1, source_target_pairs={{0,24},{8,16},{16,8},{24,0},{1,25},{9,17},{17,9},{25,1},{2,26},{10... | collective-permute-start | bytes 1572872 | tf_op jit(solution)/shard_map/ppermute | solution.py:959
  246.6 195.3 %reduce-scatter.11.cloned.1.call-start = ((), (), s32[]{:S(2)}) async-start(), calls=%async_computation.12 | async-start | bytes 4718592 | tf_op jit(solution)/shard_map/reduce_scatter | solution.py:950
  306.1 142.8 %reduce-scatter.13.cloned.1.call-start = ((), (), s32[]{:S(2)}) async-start(), calls=%async_computation.13 | async-start | bytes 4718592 | tf_op jit(solution)/shard_map/reduce_scatter | solution.py:950
  355.9 144.2 %reduce-scatter.7.cloned.1.call-start = ((), (), s32[]{:S(2)}) async-start(), calls=%async_computation.10 | async-start | bytes 4718592 | tf_op jit(solution)/shard_map/reduce_scatter | solution.py:950
  438.5 134.5 %reduce-scatter.15.cloned.1.call-start = ((), (), s32[]{:S(2)}) async-start(), calls=%async_computation.14 | async-start | bytes 2359296 | tf_op jit(solution)/shard_map/reduce_scatter | solution.py:950
  445.5 42.2 %collective-permute-start.7 = (bf16[128,2048]{1,0:T(8,128)(2,1)}, bf16[128,2048]{1,0:T(8,128)(2,1)}, u32[]{:S(2)}, u32[]{:S(2)}) collective-permute-start(bf16[128,2048]{1,0:T(8,128)(2,1)} %get-tuple-element.88.refs_6_), channel_id=1, source_target_pairs={{0,8},{8,0},{16,24},{24,16},{1,9},{9,1},{17,25},{25,17},{2,10},{10... | collective-permute-start | bytes 1572872 | tf_op jit(solution)/shard_map/ppermute | solution.py:959
  446.5 44.7 %collective-permute-start.8 = (bf16[128,2048]{1,0:T(8,128)(2,1)}, bf16[128,2048]{1,0:T(8,128)(2,1)}, u32[]{:S(2)}, u32[]{:S(2)}) collective-permute-start(bf16[128,2048]{1,0:T(8,128)(2,1)} %get-tuple-element.88.refs_6_), channel_id=1, source_target_pairs={{0,16},{8,24},{16,0},{24,8},{1,17},{9,25},{17,1},{25,9},{2,18},{10... | collective-permute-start | bytes 1572872 | tf_op jit(solution)/shard_map/ppermute | solution.py:959
  447.4 45.8 %collective-permute-start.9 = (bf16[128,2048]{1,0:T(8,128)(2,1)}, bf16[128,2048]{1,0:T(8,128)(2,1)}, u32[]{:S(2)}, u32[]{:S(2)}) collective-permute-start(bf16[128,2048]{1,0:T(8,128)(2,1)} %get-tuple-element.88.refs_6_), channel_id=1, source_target_pairs={{0,24},{8,16},{16,8},{24,0},{1,25},{9,17},{17,9},{25,1},{2,26},{10... | collective-permute-start | bytes 1572872 | tf_op jit(solution)/shard_map/ppermute | solution.py:959
  452.4 37.9 %collective-permute-start.10 = (bf16[128,2048]{1,0:T(8,128)(2,1)}, bf16[128,2048]{1,0:T(8,128)(2,1)S(1)}, u32[]{:S(2)}, u32[]{:S(2)}) collective-permute-start(bf16[128,2048]{1,0:T(8,128)(2,1)} %get-tuple-element.89.refs_7_), channel_id=1, source_target_pairs={{0,8},{8,0},{16,24},{24,16},{1,9},{9,1},{17,25},{25,17},{2,10},{10... | collective-permute-start | bytes 1572872 | tf_op jit(solution)/shard_map/ppermute | solution.py:959
  453.5 38.9 %collective-permute-start.11 = (bf16[128,2048]{1,0:T(8,128)(2,1)}, bf16[128,2048]{1,0:T(8,128)(2,1)S(1)}, u32[]{:S(2)}, u32[]{:S(2)}) collective-permute-start(bf16[128,2048]{1,0:T(8,128)(2,1)} %get-tuple-element.89.refs_7_), channel_id=1, source_target_pairs={{0,16},{8,24},{16,0},{24,8},{1,17},{9,25},{17,1},{25,9},{2,18},{10... | collective-permute-start | bytes 1572872 | tf_op jit(solution)/shard_map/ppermute | solution.py:959
  487.7 11.6 %collective-permute-start.12 = (bf16[128,2048]{1,0:T(8,128)(2,1)S(1)}, bf16[128,2048]{1,0:T(8,128)(2,1)S(1)}, u32[]{:S(2)}, u32[]{:S(2)}) collective-permute-start(bf16[128,2048]{1,0:T(8,128)(2,1)S(1)} %copy-done.11), channel_id=1, source_target_pairs={{0,24},{8,16},{16,8},{24,0},{1,25},{9,17},{17,9},{25,1},{2,26},{10... | collective-permute-start | bytes 1572872 | tf_op jit(solution)/shard_map/ppermute | solution.py:959
  509.2 100.2 %reduce-scatter.9.cloned.1.call-start = ((), (), s32[]{:S(2)}) async-start(), calls=%async_computation.11 | async-start | bytes 4718592 | tf_op jit(solution)/shard_map/reduce_scatter | solution.py:950
  510.0 213.1 %reduce-scatter.17.cloned.1.call-start = ((), (), s32[]{:S(2)}) async-start(), calls=%async_computation.15 | async-start | bytes 7077888 | tf_op jit(solution)/shard_map/reduce_scatter | solution.py:950
  510.4 45.3 %collective-permute-start.14 = (bf16[2,512,1024]{2,1,0:T(8,128)(2,1)}, bf16[2,512,1024]{2,1,0:T(8,128)(2,1)}, u32[]{:S(2)}, u32[]{:S(2)}) collective-permute-start(bf16[2,512,1024]{2,1,0:T(8,128)(2,1)} %copy-done.18), channel_id=1, source_target_pairs={{0,16},{8,24},{16,0},{24,8},{1,17},{9,25},{17,1},{25,9},{2,18},{10... | collective-permute-start | bytes 6291464 | tf_op jit(solution)/shard_map/ppermute | solution.py:959
  511.5 44.2 %collective-permute-start.13 = (bf16[2,512,1024]{2,1,0:T(8,128)(2,1)}, bf16[2,512,1024]{2,1,0:T(8,128)(2,1)}, u32[]{:S(2)}, u32[]{:S(2)}) collective-permute-start(bf16[2,512,1024]{2,1,0:T(8,128)(2,1)} %copy-done.5), channel_id=1, source_target_pairs={{0,8},{8,0},{16,24},{24,16},{1,9},{9,1},{17,25},{25,17},{2,10},{10... | collective-permute-start | bytes 6291464 | tf_op jit(solution)/shard_map/ppermute | solution.py:959
  535.9 13.9 %copy-start.50 = (f32[1,1024]{1,0:T(1,128)S(1)}, f32[1,1024]{1,0:T(1,128)}, u32[]{:S(2)}) copy-start(f32[1,1024]{1,0:T(1,128)} %copy-done.49) | copy-start | bytes 12292
  563.4 52.5 %collective-permute-start.16 = (bf16[2,512,1024]{2,1,0:T(8,128)(2,1)}, bf16[2,512,1024]{2,1,0:T(8,128)(2,1)}, u32[]{:S(2)}, u32[]{:S(2)}) collective-permute-start(bf16[2,512,1024]{2,1,0:T(8,128)(2,1)} %get-tuple-element.100), channel_id=1, source_target_pairs={{0,8},{8,0},{16,24},{24,16},{1,9},{9,1},{17,25},{25,17},{2,10},{10... | collective-permute-start | bytes 6291464 | tf_op jit(solution)/shard_map/ppermute | solution.py:959
  564.3 51.6 %collective-permute-start.17 = (bf16[2,512,1024]{2,1,0:T(8,128)(2,1)}, bf16[2,512,1024]{2,1,0:T(8,128)(2,1)}, u32[]{:S(2)}, u32[]{:S(2)}) collective-permute-start(bf16[2,512,1024]{2,1,0:T(8,128)(2,1)} %get-tuple-element.101), channel_id=1, source_target_pairs={{0,16},{8,24},{16,0},{24,8},{1,17},{9,25},{17,1},{25,9},{2,18},{10... | collective-permute-start | bytes 6291464 | tf_op jit(solution)/shard_map/ppermute | solution.py:959
  573.0 42.8 %collective-permute-start.15 = (bf16[256,512]{1,0:T(8,128)(2,1)}, bf16[256,512]{1,0:T(8,128)(2,1)S(1)}, u32[]{:S(2)}, u32[]{:S(2)}) collective-permute-start(bf16[256,512]{1,0:T(8,128)(2,1)} %reduce-scatter.15.cloned.1.call-done), channel_id=1, source_target_pairs={{0,0},{1,1},{2,8},{3,9},{4,16},{5,17},{6,24},{7,25},{8,2},{9,3},{1... | collective-permute-start | bytes 786440 | tf_op jit(solution)/shard_map/ppermute | solution.py:1139
  629.9 85.1 %copy-start.53 = (f32[256]{0:T(256)}, f32[256]{0:T(256)S(1)}, u32[]{:S(2)}) copy-start(f32[256]{0:T(256)S(1)} %get-tuple-element.174) | copy-start | bytes 3076
  640.5 69.9 %copy-start.52 = (f32[1,2048]{1,0:T(1,128)}, f32[1,2048]{1,0:T(1,128)S(1)}, u32[]{:S(2)}) copy-start(f32[1,2048]{1,0:T(1,128)S(1)} %constant_dynamic-update-slice_fusion.4) | copy-start | bytes 24580
  640.6 69.9 %copy-start.51 = (f32[1,2048]{1,0:T(1,128)}, f32[1,2048]{1,0:T(1,128)S(1)}, u32[]{:S(2)}) copy-start(f32[1,2048]{1,0:T(1,128)S(1)} %constant_dynamic-update-slice_fusion.3) | copy-start | bytes 24580
  (58 other events, 223.1 us)
Sparse Core Ops, SparseCore 0:
  111.9 48.7 all-gather.4
  162.3 45.7 all-gather.8
  209.7 46.1 all-gather.6
  257.9 45.4 all-gather.10
  306.3 48.0 reduce-scatter.10
  356.5 48.1 reduce-scatter.12
  438.6 47.6 reduce-scatter.6
  509.3 34.3 reduce-scatter.14
  546.0 63.3 reduce-scatter.8
  628.0 70.4 reduce-scatter.16
